TPU v7x, 32 devices: a whole 2x2x4 slice. The times are simulated.
32 devices in a mesh: segment: 2 (over y), expert: 4 (over x, core), dp: 4 (over z).
Axes of the slice: x: 2, y: 2, z: 4, core: 2. Of those that a mesh axis runs over, the one named last changes fastest.
Arguments:
- tokens: bfloat16 [2, 2048, 3072], P(None, ('segment', 'expert', 'dp')), may hold values from -6 to 6
- routes: int32 [2, 2048, 2], P(None, ('segment', 'expert', 'dp')), may hold values from 0 to 3, all different within a row; in each aligned block of 64 rows (0 to 63, 64 to 127, ..., all dimensions but the last counted through in order) at most 34 rows name the same one
- combine: float32 [2, 2048, 2], P(None, ('segment', 'expert', 'dp')), may hold values from 0.2 to 1
- expert_home: int32 [4], replicated, may hold values from 0 to 3, each once
- up_weight: bfloat16 [2, 4, 8192, 3072], P('segment', 'expert', 'dp'), may hold values from -0.109375 to 0.109375
- down_weight: bfloat16 [2, 4, 8192, 3072], P('segment', 'expert', 'dp'), may hold values from -0.0625 to 0.0625
Outputs:
- received: bfloat16 [2, 2048, 3072], P(None, ('segment', 'expert', 'dp'))
Inputs may be any that keep to these rules, and one draw needn't show every extreme that they name: `routes`: each token names 2 different experts. In each micro-batch the 64 tokens of one device name one expert at most 34 times. `expert_home`: every home holds exactly one expert.
All inputs are finite; a program needn't handle non-finite values.
Results may differ from a plain program's by a relative error of at most 0.0065.
Values may be sent and summed in bfloat16 or wider, within the bound.
No kernel may reach another device: no remote copies, remote signals or barrier semaphores. Data moves between devices by JAX's collectives and lax.ppermute only.
A program may use at most 128 MiB of HBM per device.

v0:
```python
import jax
import jax.numpy as jnp
from jax import lax
from jax.sharding import PartitionSpec as P


def passed_along(block, axis, distance):
    devices = range(lax.axis_size(axis))
    route = [((i - distance) % len(devices), i) for i in devices]
    return lax.ppermute(block, axis, route)


def expert_partial(row_block, up_rows, down_rows):
    features = row_block.shape[-1]
    flattened = row_block.reshape(-1, features)
    pre_act = lax.dot_general(
        flattened, up_rows, (((1,), (1,)), ((), ())), preferred_element_type=jnp.float32
    )
    hidden = jax.nn.silu(pre_act).astype(jnp.bfloat16)
    partial_sum = jnp.dot(hidden, down_rows, preferred_element_type=jnp.float32)
    return partial_sum.reshape(row_block.shape[:-1] + (down_rows.shape[1],))


def on_device(tokens, routes, combine, expert_home, up_weight, down_weight):
    up_rows = up_weight[0, 0]
    down_rows = down_weight[0, 0]
    batches, tok_rows, features = tokens.shape
    top_count = routes.shape[2]
    experts = expert_home.shape[0]
    home_count = lax.axis_size("expert")
    replica_count = lax.axis_size("dp")
    capacity = min(tok_rows, tok_rows * top_count // experts + tok_rows // 32)
    pair_count = tok_rows * top_count
    expert_ids = jnp.arange(experts, dtype=jnp.int32)
    owner_of = jnp.arange(pair_count, dtype=jnp.int32) // top_count
    results = []
    for batch_index in range(batches):
        chosen = routes[batch_index].reshape(-1)
        onehot = (chosen[:, None] == expert_ids[None, :]).astype(jnp.int32)
        home_of = jnp.sum(onehot * expert_home[None, :], axis=1)
        before = jnp.cumsum(onehot, axis=0) - onehot
        position = jnp.sum(before * onehot, axis=1)
        slot_index = home_of * capacity + position
        picked = tokens[batch_index][owner_of]
        packed = (
            jnp.zeros((home_count * capacity, features), jnp.bfloat16).at[slot_index].set(picked)
        )
        spread = jnp.broadcast_to(
            packed.reshape(home_count, 1, capacity, features),
            (home_count, replica_count, capacity, features),
        )
        spread = spread.reshape(home_count * replica_count, capacity, features)
        partial_sum = expert_partial(
            lax.all_to_all(spread, ("expert", "dp"), split_axis=0, concat_axis=0, tiled=True),
            up_rows,
            down_rows,
        ).astype(jnp.bfloat16)
        returned = lax.all_to_all(
            partial_sum, ("expert", "dp"), split_axis=0, concat_axis=0, tiled=True
        )
        summed = jnp.sum(
            returned.reshape(home_count, replica_count, capacity, features).astype(jnp.float32),
            axis=1,
        )
        outputs = summed.astype(jnp.bfloat16).reshape(home_count * capacity, features)
        answers = outputs[slot_index].astype(jnp.float32).reshape(tok_rows, top_count, features)
        blended = jnp.sum(answers * combine[batch_index][:, :, None], axis=1).astype(jnp.bfloat16)
        results.append(blended)
    stacked = jnp.stack(results, axis=0)
    return passed_along(stacked, "segment", 1)


def solution(mesh):
    return jax.shard_map(
        on_device,
        mesh=mesh,
        in_specs=(
            P(None, ("segment", "expert", "dp"), None),
            P(None, ("segment", "expert", "dp"), None),
            P(None, ("segment", "expert", "dp"), None),
            P(),
            P("segment", "expert", "dp", None),
            P("segment", "expert", "dp", None),
        ),
        out_specs=P(None, ("segment", "expert", "dp"), None),
        check_vma=False,
    )
```

profile of v0, /device:TPU:0, one launch (start us, length us, event | category | flops | bytes accessed | tf_op | source)
XLA Modules:
  0.0 420.8 jit_solution(17574467086916412863)
XLA Ops:
  1.7 1.2 slice_bitcast_fusion.1
  3.8 4.2 %scatter_custom_fusion = bf16[136,3072]{1,0:T(8,128)(2,1)S(1)} fusion(s32[128]{0:T(128)S(1)} %get-tuple-element.15, bf16[64,3072]{1,0:T(8,128)(2,1)S(1)} %get-tuple-element.9, s32[1024]{0:T(1024)S(1)} %pad_clamp_fusion.2, bf16[]{:T(256)} %constant.33.clone.1), kind=kCustom, calls=%fused_computation.25 | custom fusion | bytes 835586 | tf_op jit(solution)/shard_map/scatter | solution.py:46
  8.3 2.4 broadcast_in_dim.9
  10.7 7.4 %all-to-all-start = ((bf16[16,34,3072]{2,1,0:T(8,128)(2,1)}), bf16[16,34,3072]{2,1,0:T(8,128)(2,1)}, u32[]{:S(2)}, u32[]{:S(2)}) async-start(bf16[16,34,3072]{2,1,0:T(8,128)(2,1)} %bitcast.54), calls=%async_computation | async-start | bytes 7864320 | tf_op jit(solution)/shard_map/all_to_all | solution.py:54
  18.1 4.2 %scatter_custom_fusion.1 = bf16[136,3072]{1,0:T(8,128)(2,1)S(1)} fusion(s32[128]{0:T(128)S(1)} %get-tuple-element.16, bf16[64,3072]{1,0:T(8,128)(2,1)S(1)} %get-tuple-element.10, s32[1024]{0:T(1024)S(1)} %pad_clamp_fusion.2, bf16[]{:T(256)} %constant.33.clone.1), kind=kCustom, calls=%fused_computation.23 | custom fusion | bytes 835586 | tf_op jit(solution)/shard_map/scatter | solution.py:46
  22.6 84.3 %all-to-all-done = bf16[16,34,3072]{2,1,0:T(8,128)(2,1)} async-done(((bf16[16,34,3072]{2,1,0:T(8,128)(2,1)}), bf16[16,34,3072]{2,1,0:T(8,128)(2,1)}, u32[]{:S(2)}, u32[]{:S(2)}) %all-to-all-start) | async-done | bytes 3342368 | tf_op jit(solution)/shard_map/all_to_all | solution.py:54
  106.9 2.4 broadcast_in_dim.11
  109.3 4.7 %all-to-all-start.2 = ((bf16[16,34,3072]{2,1,0:T(8,128)(2,1)}), bf16[16,34,3072]{2,1,0:T(8,128)(2,1)}, u32[]{:S(2)}, u32[]{:S(2)}) async-start(bf16[16,34,3072]{2,1,0:T(8,128)(2,1)} %bitcast.55), calls=%async_computation.2 | async-start | bytes 7864320 | tf_op jit(solution)/shard_map/all_to_all | solution.py:54
  114.0 3.3 reshape.157
  117.3 11.7 %multiply_convert_fusion.1 = bf16[544,2048]{1,0:T(8,128)(2,1)} fusion(bf16[544,3072]{1,0:T(8,128)(2,1)S(1)} %reshape.157, bf16[1,1,2048,3072]{3,2,1,0:T(8,128)(2,1)} %param.10), kind=kOutput, calls=%fused_computation.17 | convolution fusion | flops 6850674688 | bytes 18153472 | tf_op jit(solution)/shard_map/dot_general | solution.py:16
  129.0 2.6 dot_general.17
  131.6 12.7 %fusion.8 = bf16[16,34,3072]{2,1,0:T(8,128)(2,1)} fusion(bf16[16,34,2048]{2,1,0:T(8,128)(2,1)S(1)} %dot_general.17, bf16[1,1,2048,3072]{3,2,1,0:T(8,128)(2,1)} %param.11), kind=kOutput, calls=%fused_computation.14 | convolution fusion | flops 6846775296 | bytes 18153472 | tf_op jit(solution)/shard_map/dot_general | solution.py:20
  144.3 58.3 %all-to-all-done.2 = bf16[16,34,3072]{2,1,0:T(8,128)(2,1)} async-done(((bf16[16,34,3072]{2,1,0:T(8,128)(2,1)}), bf16[16,34,3072]{2,1,0:T(8,128)(2,1)}, u32[]{:S(2)}, u32[]{:S(2)}) %all-to-all-start.2) | async-done | bytes 3342368 | tf_op jit(solution)/shard_map/all_to_all | solution.py:54
  202.6 4.5 %all-to-all-start.1 = ((bf16[16,34,3072]{2,1,0:T(8,128)(2,1)}), bf16[16,34,3072]{2,1,0:T(8,128)(2,1)}, u32[]{:S(2)}, u32[]{:S(2)}) async-start(bf16[16,34,3072]{2,1,0:T(8,128)(2,1)} %fusion.8), calls=%async_computation.1 | async-start | bytes 7864320 | tf_op jit(solution)/shard_map/all_to_all | solution.py:58
  207.1 3.3 reshape.161
  210.4 11.6 %multiply_convert_fusion = bf16[544,2048]{1,0:T(8,128)(2,1)} fusion(bf16[544,3072]{1,0:T(8,128)(2,1)S(1)} %reshape.161, bf16[1,1,2048,3072]{3,2,1,0:T(8,128)(2,1)} %param.10), kind=kOutput, calls=%fused_computation.16 | convolution fusion | flops 6850674688 | bytes 18153472 | tf_op jit(solution)/shard_map/dot_general | solution.py:16
  222.0 2.6 dot_general.20
  224.7 12.6 %fusion.11 = bf16[16,34,3072]{2,1,0:T(8,128)(2,1)} fusion(bf16[16,34,2048]{2,1,0:T(8,128)(2,1)S(1)} %dot_general.20, bf16[1,1,2048,3072]{3,2,1,0:T(8,128)(2,1)} %param.11), kind=kOutput, calls=%fused_computation.15 | convolution fusion | flops 6846775296 | bytes 18153472 | tf_op jit(solution)/shard_map/dot_general | solution.py:20
  237.3 58.6 %all-to-all-done.1 = bf16[16,34,3072]{2,1,0:T(8,128)(2,1)} async-done(((bf16[16,34,3072]{2,1,0:T(8,128)(2,1)}), bf16[16,34,3072]{2,1,0:T(8,128)(2,1)}, u32[]{:S(2)}, u32[]{:S(2)}) %all-to-all-start.1) | async-done | bytes 3342368 | tf_op jit(solution)/shard_map/all_to_all | solution.py:58
  295.9 4.7 %all-to-all-start.3 = ((bf16[16,34,3072]{2,1,0:T(8,128)(2,1)}), bf16[16,34,3072]{2,1,0:T(8,128)(2,1)}, u32[]{:S(2)}, u32[]{:S(2)}) async-start(bf16[16,34,3072]{2,1,0:T(8,128)(2,1)} %fusion.11), calls=%async_computation.3 | async-start | bytes 7864320 | tf_op jit(solution)/shard_map/all_to_all | solution.py:58
  300.9 2.9 bitcast_reduce_fusion.1
  304.0 1.0 gather_fusion
  305.1 1.0 reshape.164
  306.0 83.1 %all-to-all-done.3 = bf16[16,34,3072]{2,1,0:T(8,128)(2,1)} async-done(((bf16[16,34,3072]{2,1,0:T(8,128)(2,1)}), bf16[16,34,3072]{2,1,0:T(8,128)(2,1)}, u32[]{:S(2)}, u32[]{:S(2)}) %all-to-all-start.3) | async-done | bytes 3342368 | tf_op jit(solution)/shard_map/all_to_all | solution.py:58
  389.2 2.9 bitcast_reduce_fusion
  392.3 1.9 gather_fusion.1
  394.2 2.2 reshape.165
  396.4 2.1 multiply_reduce_fusion.1
  398.6 2.1 multiply_reduce_fusion
  400.8 1.6 collective-permute-start
  402.4 17.6 %collective-permute-done = bf16[2,64,3072]{2,1,0:T(8,128)(2,1)S(1)} collective-permute-done((bf16[2,64,3072]{2,1,0:T(8,128)(2,1)S(1)}, bf16[2,64,3072]{2,1,0:T(8,128)(2,1)S(1)}, u32[]{:S(2)}, u32[]{:S(2)}) %collective-permute-start) | collective-permute-done | bytes 786464 | tf_op jit(solution)/shard_map/ppermute | solution.py:10
  419.9 0.9 copy.16
  (25 shorter events, 3.8 us)
Async XLA Ops:
  10.7 96.2 %all-to-all-start = ((bf16[16,34,3072]{2,1,0:T(8,128)(2,1)}), bf16[16,34,3072]{2,1,0:T(8,128)(2,1)}, u32[]{:S(2)}, u32[]{:S(2)}) async-start(bf16[16,34,3072]{2,1,0:T(8,128)(2,1)} %bitcast.54), calls=%async_computation | async-start | bytes 7864320 | tf_op jit(solution)/shard_map/all_to_all | solution.py:54
  109.3 93.3 %all-to-all-start.2 = ((bf16[16,34,3072]{2,1,0:T(8,128)(2,1)}), bf16[16,34,3072]{2,1,0:T(8,128)(2,1)}, u32[]{:S(2)}, u32[]{:S(2)}) async-start(bf16[16,34,3072]{2,1,0:T(8,128)(2,1)} %bitcast.55), calls=%async_computation.2 | async-start | bytes 7864320 | tf_op jit(solution)/shard_map/all_to_all | solution.py:54
  202.6 93.3 %all-to-all-start.1 = ((bf16[16,34,3072]{2,1,0:T(8,128)(2,1)}), bf16[16,34,3072]{2,1,0:T(8,128)(2,1)}, u32[]{:S(2)}, u32[]{:S(2)}) async-start(bf16[16,34,3072]{2,1,0:T(8,128)(2,1)} %fusion.8), calls=%async_computation.1 | async-start | bytes 7864320 | tf_op jit(solution)/shard_map/all_to_all | solution.py:58
  237.3 63.3 %copy-start = (f32[2,64,2]{1,2,0:T(2,128)S(1)}, f32[2,64,2]{1,2,0:T(2,128)}, u32[]{:S(2)}) copy-start(f32[2,64,2]{1,2,0:T(2,128)} %param.8) | copy-start | bytes 3076
  295.9 93.3 %all-to-all-start.3 = ((bf16[16,34,3072]{2,1,0:T(8,128)(2,1)}), bf16[16,34,3072]{2,1,0:T(8,128)(2,1)}, u32[]{:S(2)}, u32[]{:S(2)}) async-start(bf16[16,34,3072]{2,1,0:T(8,128)(2,1)} %fusion.11), calls=%async_computation.3 | async-start | bytes 7864320 | tf_op jit(solution)/shard_map/all_to_all | solution.py:58
  400.8 19.1 %collective-permute-start = (bf16[2,64,3072]{2,1,0:T(8,128)(2,1)S(1)}, bf16[2,64,3072]{2,1,0:T(8,128)(2,1)S(1)}, u32[]{:S(2)}, u32[]{:S(2)}) collective-permute-start(bf16[2,64,3072]{2,1,0:T(8,128)(2,1)S(1)} %pad_maximum_fusion), channel_id=1, source_target_pairs={{16,0},{0,16},{17,1},{1,17},{18,2},{2,18},{19,3},{3,19},{20,4},{4,... | collective-permute-start | bytes 2359304 | tf_op jit(solution)/shard_map/ppermute | solution.py:10
where the time goes:
time: 422 us; the launch traced here: 421 us
  waiting for transfers between devices  302 us (72%)
  matrix products  48.6 us (12%)
  local copies, waits for them, and re-layouts  35.5 us (8%)
  starting transfers between devices  23 us (5%)
  other arithmetic  11.6 us (3%)
    all_to_all x2, waiting for transfers between devices, on_device(): lax.all_to_all(spread, ('expert', 'dp'), split_axis=0, concat_axis=0, til...  143 us
    all_to_all x2, waiting for transfers between devices, on_device(): lax.all_to_all(partial_sum, ('expert', 'dp'), split_axis=0, concat_axis=0...  142 us
    dot_general x2, matrix products, expert_partial(): partial_sum = jnp.dot(hidden, down_rows, preferred_element_type=jnp.float32)  25.3 us
    dot_general x2, matrix products, expert_partial(): lax.dot_general(flattened, up_rows, (((1,), (1,)), ((), ())), preferred_e...  23.3 us
    ppermute x1, waiting for transfers between devices, passed_along(): return lax.ppermute(block, axis, route)  17.6 us
    all_to_all x2, starting transfers between devices, on_device(): lax.all_to_all(spread, ('expert', 'dp'), split_axis=0, concat_axis=0, til...  12.1 us
    all_to_all x2, starting transfers between devices, on_device(): lax.all_to_all(partial_sum, ('expert', 'dp'), split_axis=0, concat_axis=0...  9.26 us
    scatter x2, local copies, waits for them, and re-layouts, on_device(): jnp.zeros((home_count * capacity, features), jnp.bfloat16).at[slot_index]  8.49 us
  transfers between devices with their start and end apart: 5, of which 5 were waited for; matrix products, arithmetic and copies ran while one was open for 17% of the time, Pallas kernels for 0%

commit v1 on v0

v1 whole, which is shorter than its diff:
```python
import jax
import jax.numpy as jnp
from jax import lax
from jax.sharding import PartitionSpec as P


def passed_along(block, axis, distance):
    devices = range(lax.axis_size(axis))
    route = [((i - distance) % len(devices), i) for i in devices]
    return lax.ppermute(block, axis, route)


def swapped(block, axis, bits):
    return lax.ppermute(block, axis, [(i, i ^ bits) for i in range(lax.axis_size(axis))])


def placed_pairs(routes, expert_home):
    first, second = routes[:, 0], routes[:, 1]
    count = routes.shape[0]
    earlier = jnp.arange(count)[:, None] < jnp.arange(count)[None, :]
    rank_first = jnp.sum(jnp.where(earlier & (first[:, None] == first[None, :]), 1, 0), axis=0)
    rank_second = jnp.sum(
        jnp.where(first[:, None] == second[None, :], 1, 0)
        + jnp.where(earlier & (second[:, None] == second[None, :]), 1, 0),
        axis=0,
    )
    chosen = routes.T
    ids = jnp.arange(expert_home.shape[0], dtype=jnp.int32)
    home = jnp.sum(jnp.where(chosen[:, :, None] == ids, expert_home, 0), axis=-1)
    return home, jnp.stack([rank_first, rank_second])


def expert_share(rows, up_rows, down_rows):
    pre_act = lax.dot_general(
        rows, up_rows, (((1,), (1,)), ((), ())), preferred_element_type=jnp.float32
    )
    hidden = jax.nn.silu(pre_act).astype(jnp.bfloat16)
    return jnp.dot(hidden, down_rows, preferred_element_type=jnp.float32).astype(jnp.bfloat16)


def on_device(tokens, routes, combine, expert_home, up_weight, down_weight):
    up_rows = up_weight[0, 0]
    down_rows = down_weight[0, 0]
    batches, tok_rows, features = tokens.shape
    top_count = routes.shape[2]
    experts = expert_home.shape[0]
    sides = lax.axis_size("expert") // 2
    capacity = min(tok_rows, tok_rows * top_count // experts + tok_rows // 32)
    here = lax.axis_index("expert")
    side, core = here // 2, here % 2
    bf16, f32 = jnp.bfloat16, jnp.float32

    facts = []
    for m in range(batches):
        home, rank = placed_pairs(routes[m], expert_home)
        facts += [(home * tok_rows + rank).astype(f32), combine[m].T]
    facts = jnp.concatenate(facts)
    facts_far = jnp.stack([facts, swapped(facts, "dp", 2)])
    facts_own = jnp.stack([facts_far, swapped(facts_far, "dp", 1)])
    facts_all = jnp.stack([facts_own] + [swapped(facts_own, "expert", 2 * j) for j in range(1, sides)])
    facts_all = facts_all.reshape(sides, 2, 2, batches, 2, top_count, tok_rows)

    group_rows = sides * 2 * capacity
    group_tokens = sides * 2 * tok_rows

    def slots_of(m, near):
        code = facts_all[:, near, :, m, 0].astype(jnp.int32)
        weight = facts_all[:, near, :, m, 1]
        home, rank = code // tok_rows, code % tok_rows
        block = (jnp.arange(sides)[:, None] * 2 + jnp.arange(2)[None, :])[:, :, None, None]
        slot = jnp.where(home % 2 == core, 0, group_rows) + block * capacity + rank
        slot = jnp.where(home // 2 == side, slot, -1)
        slot = slot.transpose(2, 0, 1, 3).reshape(top_count, group_tokens)
        return slot, weight.transpose(2, 0, 1, 3).reshape(top_count, group_tokens)

    def spread(m):
        own = tokens[m]
        column = jnp.stack([own, swapped(own, "dp", 2)])
        columns = [column, swapped(column, "dp", 1)]
        groups = []
        for column in columns:
            groups.append(
                jnp.concatenate([column] + [swapped(column, "expert", 2 * j) for j in range(1, sides)])
                .reshape(group_tokens, features)
            )
        return groups

    def served(m, near, group):
        slot, weight = slots_of(m, near)
        ids = jnp.arange(2 * group_rows)
        pick = sum((ids[:, None] == slot[k][None, :]).astype(bf16) for k in range(top_count))
        packed = jnp.dot(pick, group, preferred_element_type=f32).astype(bf16)
        mine, other = packed[:group_rows], packed[group_rows:]
        rows = jnp.concatenate([mine, swapped(other, "expert", 1)])
        answers = expert_share(rows, up_rows, down_rows)
        answers = jnp.concatenate(
            [answers[:group_rows], swapped(answers[group_rows:], "expert", 1)]
        )
        mix = sum(
            jnp.where(slot[k][:, None] == ids[None, :], weight[k][:, None], 0.0)
            for k in range(top_count)
        )
        high = mix.astype(bf16)
        low = (mix - high.astype(f32)).astype(bf16)
        out = jnp.dot(high, answers, preferred_element_type=f32)
        out = out + jnp.dot(low, answers, preferred_element_type=f32)
        out = out.reshape(sides, 2 * tok_rows, features)
        total = out[0]
        for j in range(1, sides):
            total = total + swapped(out[j].astype(bf16), "expert", 2 * j).astype(f32)
        return total

    groups = [spread(m) for m in range(batches)]
    results = []
    for m in range(batches):
        far = served(m, 1, groups[m][1])
        total = served(m, 0, groups[m][0]) + swapped(far.astype(bf16), "dp", 1).astype(f32)
        back = swapped(total[tok_rows:].astype(bf16), "dp", 2)
        blended = (total[:tok_rows] + back.astype(f32)).astype(bf16)
        results.append(passed_along(blended, "segment", 1))
    return jnp.stack(results, axis=0)


def solution(mesh):
    return jax.shard_map(
        on_device,
        mesh=mesh,
        in_specs=(
            P(None, ("segment", "expert", "dp"), None),
            P(None, ("segment", "expert", "dp"), None),
            P(None, ("segment", "expert", "dp"), None),
            P(),
            P("segment", "expert", "dp", None),
            P("segment", "expert", "dp", None),
        ),
        out_specs=P(None, ("segment", "expert", "dp"), None),
        check_vma=False,
    )
```

time: 422 us -> 293 us (0.69)
  waiting for transfers between devices: 302 us -> 156 us
  matrix products: 48.6 us -> 68.5 us
  other arithmetic: 11.6 us -> 3.94 us
    all_to_all x4 -> x0, waiting for transfers between devices: 284 us -> none  [the longest x2 143 us: on_device(): lax.all_to_all(spread, ('expert', 'dp'), split_axis=0, concat_axis=0, til...]
    ppermute x0 -> x27, waiting for transfers between devices: none -> 146 us  [swapped(): lax.ppermute(block, axis, [(i, i ^ bits) for i in range(lax.axis_size(axi...]
    ppermute x0 -> x27, starting transfers between devices: none -> 23 us  [swapped(): lax.ppermute(block, axis, [(i, i ^ bits) for i in range(lax.axis_size(axi...]
    all_to_all x4 -> x0, starting transfers between devices: 21.4 us -> none  [the longest x2 12.1 us: on_device(): lax.all_to_all(spread, ('expert', 'dp'), split_axis=0, concat_axis=0, til...]
    dot_general x4 -> x16, matrix products: 48.6 us -> 68.5 us  [the longest x4 52.7 us: expert_share(): jnp.dot(hidden, down_rows, preferred_element_type=jnp.float32)]
    slice x3 -> x19, local copies, waits for them, and re-layouts: 0.89 us -> 16.7 us  [the longest x4 5.95 us: served(): answers[:group_rows]]
    reduce_sum x5 -> x3, other arithmetic: 11 us -> 0.95 us  [the longest x1 0.74 us: placed_pairs(): jnp.sum(jnp.where(chosen[:, :, None] == ids, expert_home, 0), axis=-1)]
    scatter x2 -> x0, local copies, waits for them, and re-layouts: 8.49 us -> none  [on_device(): jnp.zeros((home_count * capacity, features), jnp.bfloat16).at[slot_index]]
  transfers between devices with their start and end apart: 5 -> 29, of which waited for: 5 -> 14; matrix products, arithmetic and copies ran while one was open for 17% -> 36% of each run, Pallas kernels for 0% -> 0%
where the time goes in v1:
time: 293 us; the launch traced here: 292 us
  waiting for transfers between devices  156 us (53%)
  matrix products  68.5 us (23%)
  local copies, waits for them, and re-layouts  37.1 us (13%)
  starting transfers between devices  26.2 us (9%)
  other arithmetic  3.94 us (1%)
    ppermute x27, waiting for transfers between devices, swapped(): lax.ppermute(block, axis, [(i, i ^ bits) for i in range(lax.axis_size(axi...  146 us
    dot_general x4, matrix products, expert_share(): jnp.dot(hidden, down_rows, preferred_element_type=jnp.float32)  52.7 us
    ppermute x27, starting transfers between devices, swapped(): lax.ppermute(block, axis, [(i, i ^ bits) for i in range(lax.axis_size(axi...  23 us
    ppermute x2, waiting for transfers between devices, passed_along(): return lax.ppermute(block, axis, route)  9.52 us
    broadcast_in_dim x8, local copies, waits for them, and re-layouts, served(): jnp.where(slot[k][:, None] == ids[None, :], weight[k][:, None], 0.0)  9.13 us
    eq x8, local copies, waits for them, and re-layouts, served(): slot[k][:, None] == ids[None, :]  8.29 us
    dot_general x4, matrix products, served(): out = jnp.dot(high, answers, preferred_element_type=f32)  6.82 us
    dot_general x4, matrix products, served(): out = out + jnp.dot(low, answers, preferred_element_type=f32)  6.63 us
  transfers between devices with their start and end apart: 29, of which 14 were waited for; matrix products, arithmetic and copies ran while one was open for 36% of the time, Pallas kernels for 0%

profile of v1, /device:TPU:0, one launch (start us, length us, event | category | flops | bytes accessed | tf_op | source)
XLA Modules:
  0.0 292.2 jit_solution(14406732235555388787)
XLA Ops:
  2.4 4.1 %collective-permute-start = (f32[8,64]{1,0:T(8,128)S(1)}, f32[8,64]{1,0:T(8,128)S(1)}, u32[]{:S(2)}, u32[]{:S(2)}) collective-permute-start(f32[8,64]{1,0:T(8,128)S(1)} %get-tuple-element.58), channel_id=1, source_target_pairs={{0,2},{1,3},{2,0},{3,1},{4,6},{5,7},{6,4},{7,5},{8,10},{9,11},{10,... | collective-permute-start | bytes 6152 | tf_op jit(solution)/shard_map/ppermute | solution.py:14
  7.9 2.9 collective-permute-start.16
  10.8 1.6 collective-permute-start.1
  12.5 12.5 %collective-permute-done.1 = f32[2,8,64]{2,1,0:T(8,128)S(1)} collective-permute-done((f32[2,8,64]{2,1,0:T(8,128)S(1)}, f32[2,8,64]{2,1,0:T(8,128)S(1)}, u32[]{:S(2)}, u32[]{:S(2)}) %collective-permute-start.1) | collective-permute-done | bytes 4128 | tf_op jit(solution)/shard_map/ppermute | solution.py:14
  24.9 1.5 collective-permute-start.2
  26.5 2.1 collective-permute-done.2
  29.4 7.9 %collective-permute-done.3 = bf16[64,3072]{1,0:T(8,128)(2,1)S(1)} collective-permute-done((bf16[64,3072]{1,0:T(8,128)(2,1)S(1)}, bf16[64,3072]{1,0:T(8,128)(2,1)S(1)}, u32[]{:S(2)}, u32[]{:S(2)}) %collective-permute-start.3) | collective-permute-done | bytes 393248 | tf_op jit(solution)/shard_map/ppermute | solution.py:14
  37.4 1.6 collective-permute-start.4
  60.6 2.1 collective-permute-start.21
  65.0 15.9 %collective-permute-done.8 = bf16[2,64,3072]{2,1,0:T(8,128)(2,1)S(1)} collective-permute-done((bf16[2,64,3072]{2,1,0:T(8,128)(2,1)S(1)}, bf16[2,64,3072]{2,1,0:T(8,128)(2,1)S(1)}, u32[]{:S(2)}, u32[]{:S(2)}) %collective-permute-start.8) | collective-permute-done | bytes 786464 | tf_op jit(solution)/shard_map/ppermute | solution.py:14
  83.6 10.7 %collective-permute-done.21 = bf16[2,64,3072]{2,1,0:T(8,128)(2,1)S(1)} collective-permute-done((bf16[2,64,3072]{2,1,0:T(8,128)(2,1)S(1)}, bf16[2,64,3072]{2,1,0:T(8,128)(2,1)S(1)}, u32[]{:S(2)}, u32[]{:S(2)}) %collective-permute-start.21) | collective-permute-done | bytes 786464 | tf_op jit(solution)/shard_map/ppermute | solution.py:14
  94.8 3.5 %collective-permute-done.9 = bf16[2,64,3072]{2,1,0:T(8,128)(2,1)S(1)} collective-permute-done((bf16[2,64,3072]{2,1,0:T(8,128)(2,1)S(1)}, bf16[2,64,3072]{2,1,0:T(8,128)(2,1)S(1)}, u32[]{:S(2)}, u32[]{:S(2)}) %collective-permute-start.9) | collective-permute-done | bytes 786464 | tf_op jit(solution)/shard_map/ppermute | solution.py:14
  100.4 12.4 %collective-permute-done.22 = bf16[2,64,3072]{2,1,0:T(8,128)(2,1)S(1)} collective-permute-done((bf16[2,64,3072]{2,1,0:T(8,128)(2,1)S(1)}, bf16[2,64,3072]{2,1,0:T(8,128)(2,1)S(1)}, u32[]{:S(2)}, u32[]{:S(2)}) %collective-permute-start.22) | collective-permute-done | bytes 786464 | tf_op jit(solution)/shard_map/ppermute | solution.py:14
  115.8 12.4 %fusion.16 = bf16[272,3072]{1,0:T(8,128)(2,1)S(1)} fusion(bf16[1,1,2048,3072]{3,2,1,0:T(8,128)(2,1)} %param.11, bf16[1,1,2048,3072]{3,2,1,0:T(8,128)(2,1)} %param.10, bf16[136,3072]{1,0:T(8,128)(2,1)} %copy-done.14, bf16[136,3072]{1,0:T(8,128)(2,1)S(1)} %copy-done), kind=kOutput, calls=%fused_computation.24 | convolution fusion | flops 6852067328 | bytes 28508160 | tf_op jit(solution)/shard_map/dot_general | solution.py:38
  129.7 12.4 %fusion.22 = bf16[272,3072]{1,0:T(8,128)(2,1)S(1)} fusion(bf16[1,1,2048,3072]{3,2,1,0:T(8,128)(2,1)} %param.11, bf16[1,1,2048,3072]{3,2,1,0:T(8,128)(2,1)} %param.10, bf16[136,3072]{1,0:T(8,128)(2,1)} %collective-permute-done.18, bf16[136,3072]{1,0:T(8,128)(2,1)S(1)} %copy-done.1), kind=kOutput, calls=%fused_computation.26 | convolution fusion | flops 6852067328 | bytes 28508160 | tf_op jit(solution)/shard_map/dot_general | solution.py:38
  143.5 13.8 %fusion.19 = bf16[272,3072]{1,0:T(8,128)(2,1)} fusion(bf16[1,1,2048,3072]{3,2,1,0:T(8,128)(2,1)} %param.11, bf16[1,1,2048,3072]{3,2,1,0:T(8,128)(2,1)} %param.10, bf16[136,3072]{1,0:T(8,128)(2,1)} %collective-permute-done.10, bf16[136,3072]{1,0:T(8,128)(2,1)} %get-tuple-element.29), kind=kOutput, calls=%fused_computation.25 | convolution fusion | flops 6852067328 | bytes 28508160 | tf_op jit(solution)/shard_map/dot_general | solution.py:38
  157.3 2.4 fusion.185
  159.9 14.1 %fusion.25 = bf16[272,3072]{1,0:T(8,128)(2,1)} fusion(bf16[1,1,2048,3072]{3,2,1,0:T(8,128)(2,1)} %param.11, bf16[1,1,2048,3072]{3,2,1,0:T(8,128)(2,1)} %param.10, bf16[136,3072]{1,0:T(8,128)(2,1)} %collective-permute-done.23, bf16[136,3072]{1,0:T(8,128)(2,1)} %get-tuple-element.37), kind=kOutput, calls=%fused_computation.27 | convolution fusion | flops 6852067328 | bytes 28508160 | tf_op jit(solution)/shard_map/dot_general | solution.py:38
  175.8 2.2 fusion.71
  178.0 2.3 convolution_add_fusion.3
  181.1 2.2 fusion.70
  183.3 2.3 convolution_add_fusion.2
  185.7 1.6 collective-permute-start.12
  191.3 26.4 %collective-permute-done.12 = bf16[128,3072]{1,0:T(8,128)(2,1)S(1)} collective-permute-done((bf16[128,3072]{1,0:T(8,128)(2,1)S(1)}, bf16[128,3072]{1,0:T(8,128)(2,1)S(1)}, u32[]{:S(2)}, u32[]{:S(2)}) %collective-permute-start.12) | collective-permute-done | bytes 786464 | tf_op jit(solution)/shard_map/ppermute | solution.py:14
  220.2 14.4 %collective-permute-done.25 = bf16[128,3072]{1,0:T(8,128)(2,1)S(1)} collective-permute-done((bf16[128,3072]{1,0:T(8,128)(2,1)S(1)}, bf16[128,3072]{1,0:T(8,128)(2,1)S(1)}, u32[]{:S(2)}, u32[]{:S(2)}) %collective-permute-start.25) | collective-permute-done | bytes 786464 | tf_op jit(solution)/shard_map/ppermute | solution.py:14
  236.6 1.5 collective-permute-start.14
  238.1 12.7 %collective-permute-done.20 = bf16[128,3072]{1,0:T(8,128)(2,1)S(1)} collective-permute-done((bf16[128,3072]{1,0:T(8,128)(2,1)S(1)}, bf16[128,3072]{1,0:T(8,128)(2,1)S(1)}, u32[]{:S(2)}, u32[]{:S(2)}) %collective-permute-start.20) | collective-permute-done | bytes 786464 | tf_op jit(solution)/shard_map/ppermute | solution.py:14
  250.8 10.7 %collective-permute-done.26 = bf16[128,3072]{1,0:T(8,128)(2,1)S(1)} collective-permute-done((bf16[128,3072]{1,0:T(8,128)(2,1)S(1)}, bf16[128,3072]{1,0:T(8,128)(2,1)S(1)}, u32[]{:S(2)}, u32[]{:S(2)}) %collective-permute-start.26) | collective-permute-done | bytes 786464 | tf_op jit(solution)/shard_map/ppermute | solution.py:14
  262.4 1.6 collective-permute-start.15
  264.0 16.1 %collective-permute-done.27 = bf16[64,3072]{1,0:T(8,128)(2,1)S(1)} collective-permute-done((bf16[64,3072]{1,0:T(8,128)(2,1)S(1)}, bf16[64,3072]{1,0:T(8,128)(2,1)S(1)}, u32[]{:S(2)}, u32[]{:S(2)}) %collective-permute-start.27) | collective-permute-done | bytes 393248 | tf_op jit(solution)/shard_map/ppermute | solution.py:14
  280.1 1.6 collective-permute-start.28
  281.7 9.5 %collective-permute-done.28 = bf16[64,3072]{1,0:T(8,128)(2,1)S(1)} collective-permute-done((bf16[64,3072]{1,0:T(8,128)(2,1)S(1)}, bf16[64,3072]{1,0:T(8,128)(2,1)S(1)}, u32[]{:S(2)}, u32[]{:S(2)}) %collective-permute-start.28) | collective-permute-done | bytes 393248 | tf_op jit(solution)/shard_map/ppermute | solution.py:10
  (137 shorter events, 52.6 us)
Async XLA Ops:
  2.4 8.4 %collective-permute-start = (f32[8,64]{1,0:T(8,128)S(1)}, f32[8,64]{1,0:T(8,128)S(1)}, u32[]{:S(2)}, u32[]{:S(2)}) collective-permute-start(f32[8,64]{1,0:T(8,128)S(1)} %get-tuple-element.58), channel_id=1, source_target_pairs={{0,2},{1,3},{2,0},{3,1},{4,6},{5,7},{6,4},{7,5},{8,10},{9,11},{10,... | collective-permute-start | bytes 6152 | tf_op jit(solution)/shard_map/ppermute | solution.py:14
  7.8 29.6 %collective-permute-start.3 = (bf16[64,3072]{1,0:T(8,128)(2,1)S(1)}, bf16[64,3072]{1,0:T(8,128)(2,1)S(1)}, u32[]{:S(2)}, u32[]{:S(2)}) collective-permute-start(bf16[64,3072]{1,0:T(8,128)(2,1)S(1)} %get-tuple-element.44), channel_id=1, source_target_pairs={{0,2},{1,3},{2,0},{3,1},{4,6},{5,7},{6,4},{7,5},{8,10},{9,11},{10,... | collective-permute-start | bytes 1179656 | tf_op jit(solution)/shard_map/ppermute | solution.py:14
  7.9 52.6 %collective-permute-start.16 = (bf16[64,3072]{1,0:T(8,128)(2,1)S(1)}, bf16[64,3072]{1,0:T(8,128)(2,1)S(1)}, u32[]{:S(2)}, u32[]{:S(2)}) collective-permute-start(bf16[64,3072]{1,0:T(8,128)(2,1)S(1)} %get-tuple-element.45), channel_id=1, source_target_pairs={{0,2},{1,3},{2,0},{3,1},{4,6},{5,7},{6,4},{7,5},{8,10},{9,11},{10,... | collective-permute-start | bytes 1179656 | tf_op jit(solution)/shard_map/ppermute | solution.py:14
  10.8 14.1 %collective-permute-start.1 = (f32[2,8,64]{2,1,0:T(8,128)S(1)}, f32[2,8,64]{2,1,0:T(8,128)S(1)}, u32[]{:S(2)}, u32[]{:S(2)}) collective-permute-start(f32[2,8,64]{2,1,0:T(8,128)S(1)} %get-tuple-element.56), channel_id=1, source_target_pairs={{0,1},{1,0},{2,3},{3,2},{4,5},{5,4},{6,7},{7,6},{8,9},{9,8},{10,11... | collective-permute-start | bytes 12296 | tf_op jit(solution)/shard_map/ppermute | solution.py:14
  24.9 3.7 %collective-permute-start.2 = (f32[2,2,8,64]{3,2,1,0:T(8,128)S(1)}, f32[2,2,8,64]{3,2,1,0:T(8,128)S(1)}, u32[]{:S(2)}, u32[]{:S(2)}) collective-permute-start(f32[2,2,8,64]{3,2,1,0:T(8,128)S(1)} %pad_maximum_fusion.20), channel_id=1, source_target_pairs={{0,8},{4,12},{8,0},{12,4},{1,9},{5,13},{9,1},{13,5},{2,10},{6,14},... | collective-permute-start | bytes 24584 | tf_op jit(solution)/shard_map/ppermute | solution.py:14
  37.4 25.8 %collective-permute-start.4 = (bf16[2,64,3072]{2,1,0:T(8,128)(2,1)S(1)}, bf16[2,64,3072]{2,1,0:T(8,128)(2,1)S(1)}, u32[]{:S(2)}, u32[]{:S(2)}) collective-permute-start(bf16[2,64,3072]{2,1,0:T(8,128)(2,1)S(1)} %pad_maximum_fusion.16), channel_id=1, source_target_pairs={{0,8},{4,12},{8,0},{12,4},{1,9},{5,13},{9,1},{13,5},{2,10},{6,14},... | collective-permute-start | bytes 2359304 | tf_op jit(solution)/shard_map/ppermute | solution.py:14
  60.5 20.5 %collective-permute-start.8 = (bf16[2,64,3072]{2,1,0:T(8,128)(2,1)S(1)}, bf16[2,64,3072]{2,1,0:T(8,128)(2,1)S(1)}, u32[]{:S(2)}, u32[]{:S(2)}) collective-permute-start(bf16[2,64,3072]{2,1,0:T(8,128)(2,1)S(1)} %pad_maximum_fusion.16), channel_id=1, source_target_pairs={{0,1},{1,0},{2,3},{3,2},{4,5},{5,4},{6,7},{7,6},{8,9},{9,8},{10,11... | collective-permute-start | bytes 2359304 | tf_op jit(solution)/shard_map/ppermute | solution.py:14
  60.6 33.7 %collective-permute-start.21 = (bf16[2,64,3072]{2,1,0:T(8,128)(2,1)S(1)}, bf16[2,64,3072]{2,1,0:T(8,128)(2,1)S(1)}, u32[]{:S(2)}, u32[]{:S(2)}) collective-permute-start(bf16[2,64,3072]{2,1,0:T(8,128)(2,1)S(1)} %pad_maximum_fusion.17), channel_id=1, source_target_pairs={{0,1},{1,0},{2,3},{3,2},{4,5},{5,4},{6,7},{7,6},{8,9},{9,8},{10,11... | collective-permute-start | bytes 2359304 | tf_op jit(solution)/shard_map/ppermute | solution.py:14
  62.7 18.8 %collective-permute-start.17 = (bf16[2,64,3072]{2,1,0:T(8,128)(2,1)S(1)}, bf16[2,64,3072]{2,1,0:T(8,128)(2,1)S(1)}, u32[]{:S(2)}, u32[]{:S(2)}) collective-permute-start(bf16[2,64,3072]{2,1,0:T(8,128)(2,1)S(1)} %pad_maximum_fusion.17), channel_id=1, source_target_pairs={{0,8},{4,12},{8,0},{12,4},{1,9},{5,13},{9,1},{13,5},{2,10},{6,14},... | collective-permute-start | bytes 2359304 | tf_op jit(solution)/shard_map/ppermute | solution.py:14
  65.0 49.8 %collective-permute-start.5 = (bf16[136,3072]{1,0:T(8,128)(2,1)S(1)}, bf16[136,3072]{1,0:T(8,128)(2,1)S(1)}, u32[]{:S(2)}, u32[]{:S(2)}) collective-permute-start(bf16[136,3072]{1,0:T(8,128)(2,1)S(1)} %get-tuple-element.34), channel_id=1, source_target_pairs={{0,4},{4,0},{8,12},{12,8},{1,5},{5,1},{9,13},{13,9},{2,6},{6,2},{1... | collective-permute-start | bytes 2506760 | tf_op jit(solution)/shard_map/ppermute | solution.py:14
  81.0 17.3 %collective-permute-start.9 = (bf16[2,64,3072]{2,1,0:T(8,128)(2,1)S(1)}, bf16[2,64,3072]{2,1,0:T(8,128)(2,1)S(1)}, u32[]{:S(2)}, u32[]{:S(2)}) collective-permute-start(bf16[2,64,3072]{2,1,0:T(8,128)(2,1)S(1)} %collective-permute-done.8), channel_id=1, source_target_pairs={{0,8},{4,12},{8,0},{12,4},{1,9},{5,13},{9,1},{13,5},{2,10},{6,14},... | collective-permute-start | bytes 2359304 | tf_op jit(solution)/shard_map/ppermute | solution.py:14
  83.6 46.1 %collective-permute-start.18 = (bf16[136,3072]{1,0:T(8,128)(2,1)}, bf16[136,3072]{1,0:T(8,128)(2,1)}, u32[]{:S(2)}, u32[]{:S(2)}) collective-permute-start(bf16[136,3072]{1,0:T(8,128)(2,1)} %get-tuple-element.42), channel_id=1, source_target_pairs={{0,4},{4,0},{8,12},{12,8},{1,5},{5,1},{9,13},{13,9},{2,6},{6,2},{1... | collective-permute-start | bytes 2506760 | tf_op jit(solution)/shard_map/ppermute | solution.py:14
  94.3 18.5 %collective-permute-start.22 = (bf16[2,64,3072]{2,1,0:T(8,128)(2,1)S(1)}, bf16[2,64,3072]{2,1,0:T(8,128)(2,1)S(1)}, u32[]{:S(2)}, u32[]{:S(2)}) collective-permute-start(bf16[2,64,3072]{2,1,0:T(8,128)(2,1)S(1)} %collective-permute-done.21), channel_id=1, source_target_pairs={{0,8},{4,12},{8,0},{12,4},{1,9},{5,13},{9,1},{13,5},{2,10},{6,14},... | collective-permute-start | bytes 2359304 | tf_op jit(solution)/shard_map/ppermute | solution.py:14
  100.4 12.6 %copy-start.2 = (s32[256]{0:T(256)S(1)}, s32[256]{0:T(256)}, u32[]{:S(2)}) copy-start(s32[256]{0:T(256)} %eq.451) | copy-start | bytes 3076
  100.4 12.6 %copy-start.3 = (s32[256]{0:T(256)S(1)}, s32[256]{0:T(256)}, u32[]{:S(2)}) copy-start(s32[256]{0:T(256)} %eq.455) | copy-start | bytes 3076
  100.4 43.1 %collective-permute-start.10 = (bf16[136,3072]{1,0:T(8,128)(2,1)}, bf16[136,3072]{1,0:T(8,128)(2,1)}, u32[]{:S(2)}, u32[]{:S(2)}) collective-permute-start(bf16[136,3072]{1,0:T(8,128)(2,1)} %get-tuple-element.30), channel_id=1, source_target_pairs={{0,4},{4,0},{8,12},{12,8},{1,5},{5,1},{9,13},{13,9},{2,6},{6,2},{1... | collective-permute-start | bytes 2506760 | tf_op jit(solution)/shard_map/ppermute | solution.py:14
  114.8 45.0 %collective-permute-start.23 = (bf16[136,3072]{1,0:T(8,128)(2,1)}, bf16[136,3072]{1,0:T(8,128)(2,1)}, u32[]{:S(2)}, u32[]{:S(2)}) collective-permute-start(bf16[136,3072]{1,0:T(8,128)(2,1)} %get-tuple-element.38), channel_id=1, source_target_pairs={{0,4},{4,0},{8,12},{12,8},{1,5},{5,1},{9,13},{13,9},{2,6},{6,2},{1... | collective-permute-start | bytes 2506760 | tf_op jit(solution)/shard_map/ppermute | solution.py:14
  129.2 46.6 %collective-permute-start.6 = (bf16[136,3072]{1,0:T(8,128)(2,1)}, bf16[136,3072]{1,0:T(8,128)(2,1)}, u32[]{:S(2)}, u32[]{:S(2)}) collective-permute-start(bf16[136,3072]{1,0:T(8,128)(2,1)} %get-tuple-element.32), channel_id=1, source_target_pairs={{0,4},{4,0},{8,12},{12,8},{1,5},{5,1},{9,13},{13,9},{2,6},{6,2},{1... | collective-permute-start | bytes 2506760 | tf_op jit(solution)/shard_map/ppermute | solution.py:14
  143.1 44.2 %collective-permute-start.19 = (bf16[136,3072]{1,0:T(8,128)(2,1)}, bf16[136,3072]{1,0:T(8,128)(2,1)S(1)}, u32[]{:S(2)}, u32[]{:S(2)}) collective-permute-start(bf16[136,3072]{1,0:T(8,128)(2,1)} %get-tuple-element.40), channel_id=1, source_target_pairs={{0,4},{4,0},{8,12},{12,8},{1,5},{5,1},{9,13},{13,9},{2,6},{6,2},{1... | collective-permute-start | bytes 2506760 | tf_op jit(solution)/shard_map/ppermute | solution.py:14
  159.7 21.3 %collective-permute-start.11 = (bf16[136,3072]{1,0:T(8,128)(2,1)}, bf16[136,3072]{1,0:T(8,128)(2,1)}, u32[]{:S(2)}, u32[]{:S(2)}) collective-permute-start(bf16[136,3072]{1,0:T(8,128)(2,1)} %get-tuple-element.28), channel_id=1, source_target_pairs={{0,4},{4,0},{8,12},{12,8},{1,5},{5,1},{9,13},{13,9},{2,6},{6,2},{1... | collective-permute-start | bytes 2506760 | tf_op jit(solution)/shard_map/ppermute | solution.py:14
  175.5 12.9 %collective-permute-start.24 = (bf16[136,3072]{1,0:T(8,128)(2,1)S(1)}, bf16[136,3072]{1,0:T(8,128)(2,1)S(1)}, u32[]{:S(2)}, u32[]{:S(2)}) collective-permute-start(bf16[136,3072]{1,0:T(8,128)(2,1)S(1)} %get-tuple-element.36), channel_id=1, source_target_pairs={{0,4},{4,0},{8,12},{12,8},{1,5},{5,1},{9,13},{13,9},{2,6},{6,2},{1... | collective-permute-start | bytes 2506760 | tf_op jit(solution)/shard_map/ppermute | solution.py:14
  180.4 54.7 %collective-permute-start.7 = (bf16[128,3072]{1,0:T(8,128)(2,1)S(1)}, bf16[128,3072]{1,0:T(8,128)(2,1)S(1)}, u32[]{:S(2)}, u32[]{:S(2)}) collective-permute-start(bf16[128,3072]{1,0:T(8,128)(2,1)S(1)} %slice.431), channel_id=1, source_target_pairs={{0,8},{4,12},{8,0},{12,4},{1,9},{5,13},{9,1},{13,5},{2,10},{6,14},... | collective-permute-start | bytes 2359304 | tf_op jit(solution)/shard_map/ppermute | solution.py:14
  183.3 4.0 %copy-start.6 = (f32[256]{0:T(256)S(1)}, f32[256]{0:T(256)}, u32[]{:S(2)}) copy-start(f32[256]{0:T(256)} %broadcast_in_dim.165) | copy-start | bytes 3076
  185.7 32.0 %collective-permute-start.12 = (bf16[128,3072]{1,0:T(8,128)(2,1)S(1)}, bf16[128,3072]{1,0:T(8,128)(2,1)S(1)}, u32[]{:S(2)}, u32[]{:S(2)}) collective-permute-start(bf16[128,3072]{1,0:T(8,128)(2,1)S(1)} %slice.430), channel_id=1, source_target_pairs={{0,8},{4,12},{8,0},{12,4},{1,9},{5,13},{9,1},{13,5},{2,10},{6,14},... | collective-permute-start | bytes 2359304 | tf_op jit(solution)/shard_map/ppermute | solution.py:14
  190.7 43.9 %collective-permute-start.25 = (bf16[128,3072]{1,0:T(8,128)(2,1)S(1)}, bf16[128,3072]{1,0:T(8,128)(2,1)S(1)}, u32[]{:S(2)}, u32[]{:S(2)}) collective-permute-start(bf16[128,3072]{1,0:T(8,128)(2,1)S(1)} %slice.428), channel_id=1, source_target_pairs={{0,8},{4,12},{8,0},{12,4},{1,9},{5,13},{9,1},{13,5},{2,10},{6,14},... | collective-permute-start | bytes 2359304 | tf_op jit(solution)/shard_map/ppermute | solution.py:14
  217.9 18.3 %collective-permute-start.13 = (bf16[128,3072]{1,0:T(8,128)(2,1)S(1)}, bf16[128,3072]{1,0:T(8,128)(2,1)S(1)}, u32[]{:S(2)}, u32[]{:S(2)}) collective-permute-start(bf16[128,3072]{1,0:T(8,128)(2,1)S(1)} %fusion.50), channel_id=1, source_target_pairs={{0,1},{1,0},{2,3},{3,2},{4,5},{5,4},{6,7},{7,6},{8,9},{9,8},{10,11... | collective-permute-start | bytes 2359304 | tf_op jit(solution)/shard_map/ppermute | solution.py:14
  219.6 31.2 %collective-permute-start.20 = (bf16[128,3072]{1,0:T(8,128)(2,1)S(1)}, bf16[128,3072]{1,0:T(8,128)(2,1)S(1)}, u32[]{:S(2)}, u32[]{:S(2)}) collective-permute-start(bf16[128,3072]{1,0:T(8,128)(2,1)S(1)} %slice.429), channel_id=1, source_target_pairs={{0,8},{4,12},{8,0},{12,4},{1,9},{5,13},{9,1},{13,5},{2,10},{6,14},... | collective-permute-start | bytes 2359304 | tf_op jit(solution)/shard_map/ppermute | solution.py:14
  234.7 26.8 %collective-permute-start.26 = (bf16[128,3072]{1,0:T(8,128)(2,1)S(1)}, bf16[128,3072]{1,0:T(8,128)(2,1)S(1)}, u32[]{:S(2)}, u32[]{:S(2)}) collective-permute-start(bf16[128,3072]{1,0:T(8,128)(2,1)S(1)} %fusion.48), channel_id=1, source_target_pairs={{0,1},{1,0},{2,3},{3,2},{4,5},{5,4},{6,7},{7,6},{8,9},{9,8},{10,11... | collective-permute-start | bytes 2359304 | tf_op jit(solution)/shard_map/ppermute | solution.py:14
  236.6 25.7 %collective-permute-start.14 = (bf16[64,3072]{1,0:T(8,128)(2,1)S(1)}, bf16[64,3072]{1,0:T(8,128)(2,1)S(1)}, u32[]{:S(2)}, u32[]{:S(2)}) collective-permute-start(bf16[64,3072]{1,0:T(8,128)(2,1)S(1)} %slice.433), channel_id=1, source_target_pairs={{0,2},{1,3},{2,0},{3,1},{4,6},{5,7},{6,4},{7,5},{8,10},{9,11},{10,... | collective-permute-start | bytes 1179656 | tf_op jit(solution)/shard_map/ppermute | solution.py:14
  261.9 18.2 %collective-permute-start.27 = (bf16[64,3072]{1,0:T(8,128)(2,1)S(1)}, bf16[64,3072]{1,0:T(8,128)(2,1)S(1)}, u32[]{:S(2)}, u32[]{:S(2)}) collective-permute-start(bf16[64,3072]{1,0:T(8,128)(2,1)S(1)} %slice.432), channel_id=1, source_target_pairs={{0,2},{1,3},{2,0},{3,1},{4,6},{5,7},{6,4},{7,5},{8,10},{9,11},{10,... | collective-permute-start | bytes 1179656 | tf_op jit(solution)/shard_map/ppermute | solution.py:14
  262.4 19.3 %collective-permute-start.15 = (bf16[64,3072]{1,0:T(8,128)(2,1)S(1)}, bf16[64,3072]{1,0:T(8,128)(2,1)S(1)}, u32[]{:S(2)}, u32[]{:S(2)}) collective-permute-start(bf16[64,3072]{1,0:T(8,128)(2,1)S(1)} %fusion.73), channel_id=1, source_target_pairs={{16,0},{0,16},{17,1},{1,17},{18,2},{2,18},{19,3},{3,19},{20,4},{4,... | collective-permute-start | bytes 1179656 | tf_op jit(solution)/shard_map/ppermute | solution.py:10
  280.1 11.1 %collective-permute-start.28 = (bf16[64,3072]{1,0:T(8,128)(2,1)S(1)}, bf16[64,3072]{1,0:T(8,128)(2,1)S(1)}, u32[]{:S(2)}, u32[]{:S(2)}) collective-permute-start(bf16[64,3072]{1,0:T(8,128)(2,1)S(1)} %fusion.72), channel_id=1, source_target_pairs={{16,0},{0,16},{17,1},{1,17},{18,2},{2,18},{19,3},{3,19},{20,4},{4,... | collective-permute-start | bytes 1179656 | tf_op jit(solution)/shard_map/ppermute | solution.py:10
  (12 other events, 26.2 us)

commit v2 on v1

v2 whole, which is shorter than its diff:
```python
import functools

import jax
import jax.numpy as jnp
from jax import lax
from jax.experimental import pallas as pl
from jax.experimental.pallas import tpu as pltpu
from jax.sharding import PartitionSpec as P

BF16, F32 = jnp.bfloat16, jnp.float32


def passed_along(block, axis, distance):
    devices = range(lax.axis_size(axis))
    route = [((i - distance) % len(devices), i) for i in devices]
    return lax.ppermute(block, axis, route)


def swapped(block, axis, bits):
    return lax.ppermute(block, axis, [(i, i ^ bits) for i in range(lax.axis_size(axis))])


def placed_pairs(routes, expert_home):
    first, second = routes[:, 0], routes[:, 1]
    count = routes.shape[0]
    earlier = jnp.arange(count)[:, None] < jnp.arange(count)[None, :]
    rank_first = jnp.sum(jnp.where(earlier & (first[:, None] == first[None, :]), 1, 0), axis=0)
    rank_second = jnp.sum(
        jnp.where(first[:, None] == second[None, :], 1, 0)
        + jnp.where(earlier & (second[:, None] == second[None, :]), 1, 0),
        axis=0,
    )
    chosen = routes.T
    ids = jnp.arange(expert_home.shape[0], dtype=jnp.int32)
    home = jnp.sum(jnp.where(chosen[:, :, None] == ids, expert_home, 0), axis=-1)
    return home, jnp.stack([rank_first, rank_second])


def arrivals(sides, batch):
    steps = ((0,), (1, 2), (3,)) if batch == 0 else ((0,), (1, 2, 3))
    return [(j, bits) for step in steps for j in range(sides) for bits in step]


def departures(sides):
    return [(j, bits) for j in range(sides) for bits in (3, 1, 2, 0)]


def plan_kernel(sides, batches, top_count, capacity, half, place_ref, facts_ref, pick_ref, high_ref, low_ref):
    side, core = place_ref[0], place_ref[1]
    tok_rows = facts_ref.shape[-1]
    rows = 2 * half
    tokens = sides * 4 * tok_rows
    padded = -(-rows // 128) * 128
    ids = lax.broadcasted_iota(jnp.int32, (padded, tokens), 0)
    for m in range(batches):
        pick = jnp.zeros((rows, tokens), F32)
        mix = jnp.zeros((padded, tokens), F32)
        for k in range(top_count):
            slots, weights = {}, {}
            for j, bits in departures(sides):
                at = m * 2 * top_count + k
                code = facts_ref[j, bits, at : at + 1, :].astype(jnp.int32)
                at = at + top_count
                weights[j, bits] = facts_ref[j, bits, at : at + 1, :]
                home, rank = code // tok_rows, code % tok_rows
                slot = (j * 4 + bits) * capacity + rank + jnp.where(home % 2 == core, 0, half)
                slots[j, bits] = jnp.where(home // 2 == side, slot, -1)
            hit = ids[:rows] == jnp.concatenate([slots[at] for at in arrivals(sides, m)], axis=1)
            pick = jnp.where(hit, 1.0, pick)
            hit = ids == jnp.concatenate([slots[at] for at in departures(sides)], axis=1)
            mix = jnp.where(hit, jnp.concatenate([weights[at] for at in departures(sides)], axis=1), mix)
        mix = mix.T[:, :rows]
        high = mix.astype(BF16)
        pick_ref[m] = pick.astype(BF16)
        high_ref[m] = high
        low_ref[m] = (mix - high.astype(F32)).astype(BF16)


def plan(place, facts, batches, top_count, capacity, half):
    sides, tok_rows = facts.shape[0], facts.shape[-1]
    shape = jax.ShapeDtypeStruct((batches, 2 * half, sides * 4 * tok_rows), BF16)
    mixed = jax.ShapeDtypeStruct((batches, sides * 4 * tok_rows, 2 * half), BF16)
    vmem = pl.BlockSpec(memory_space=pltpu.VMEM)
    return pl.pallas_call(
        functools.partial(plan_kernel, sides, batches, top_count, capacity, half),
        out_shape=[shape, mixed, mixed],
        in_specs=[pl.BlockSpec(memory_space=pltpu.SMEM), vmem],
        out_specs=[vmem] * 3,
        cost_estimate=pl.CostEstimate(
            flops=10 * shape.size, bytes_accessed=6 * shape.size, transcendentals=0
        ),
        compiler_params=pltpu.CompilerParams(vmem_limit_bytes=32 * 2**20),
    )(place, facts)


def expert_kernel(steps, half, mine_ref, other_ref, up_ref, down_ref, *refs):
    mine_out, other_out, rows, hidden = refs[-4:]
    step = pl.program_id(0)
    chunk = up_ref.shape[0]

    @pl.when(step == 0)
    def _():
        rows[:half] = mine_ref[...]
        rows[half:] = other_ref[...]

    for s in range(steps):

        @pl.when(step == s)
        def _():
            pre_act = lax.dot_general(
                rows[...], up_ref[...], (((1,), (1,)), ((), ())), preferred_element_type=F32
            )
            hidden[:, s * chunk : (s + 1) * chunk] = jax.nn.silu(pre_act).astype(BF16)

    @pl.when(step >= steps)
    def _():
        answer = jnp.dot(hidden[...], down_ref[...], preferred_element_type=F32).astype(BF16)
        mine_out[...] = answer[:half]
        other_out[...] = answer[half:]


def expert_share(mine, other, up_rows, down_rows, *earlier):
    half, features = mine.shape
    units = up_rows.shape[0]
    steps = 4
    chunk, width = units // steps, features // steps
    shape = jax.ShapeDtypeStruct((half, features), BF16)
    whole = pl.BlockSpec((half, features), lambda i: (0, 0))
    part = pl.BlockSpec((half, width), lambda i: (0, jnp.maximum(i - steps, 0)))
    return pl.pallas_call(
        functools.partial(expert_kernel, steps, half),
        grid=(2 * steps,),
        out_shape=[shape] * 2,
        in_specs=[
            whole,
            whole,
            pl.BlockSpec((chunk, features), lambda i: (jnp.minimum(i, steps - 1), 0)),
            pl.BlockSpec((units, width), lambda i: (0, jnp.maximum(i - steps, 0))),
            *[pl.BlockSpec(memory_space=pl.ANY) for _ in earlier],
        ],
        out_specs=[part] * 2,
        scratch_shapes=[pltpu.VMEM((2 * half, features), BF16), pltpu.VMEM((2 * half, units), BF16)],
        cost_estimate=pl.CostEstimate(
            flops=8 * half * units * features,
            bytes_accessed=4 * units * features + 8 * half * features,
            transcendentals=2 * half * units,
        ),
        compiler_params=pltpu.CompilerParams(vmem_limit_bytes=40 * 2**20),
    )(mine, other, up_rows, down_rows, *earlier)


def pack_kernel(count, half, pick_ref, *refs):
    mine_ref, other_ref, group = refs[-3:]
    tok_rows, at = refs[0].shape[-2], 0
    for block in refs[:count]:
        rows = block.shape[-2]
        group[at : at + rows] = block[...].reshape(rows, block.shape[-1])
        at += rows
    chosen = jnp.dot(pick_ref[0], group[...], preferred_element_type=F32).astype(BF16)
    mine_ref[...] = chosen[:half]
    other_ref[...] = chosen[half:]


def pack(m, pick, blocks, *earlier):
    _, rows, tokens = pick.shape
    half, features = rows // 2, blocks[0].shape[-1]
    width = features // 4

    def spec(block):
        if block.ndim == 3:
            return pl.BlockSpec((1, block.shape[1], width), lambda i: (m, 0, i))
        return pl.BlockSpec((block.shape[0], width), lambda i: (0, i))

    return pl.pallas_call(
        functools.partial(pack_kernel, len(blocks), half),
        grid=(features // width,),
        out_shape=[jax.ShapeDtypeStruct((half, features), BF16)] * 2,
        in_specs=[
            pl.BlockSpec((1, rows, tokens), lambda i: (m, 0, 0)),
            *[spec(block) for block in blocks],
            *[pl.BlockSpec(memory_space=pl.ANY) for _ in earlier],
        ],
        out_specs=[pl.BlockSpec((half, width), lambda i: (0, i))] * 2,
        scratch_shapes=[pltpu.VMEM((tokens, width), BF16)],
        cost_estimate=pl.CostEstimate(
            flops=2 * rows * tokens * features,
            bytes_accessed=2 * (rows + tokens) * features + 2 * rows * tokens,
            transcendentals=0,
        ),
        compiler_params=pltpu.CompilerParams(vmem_limit_bytes=24 * 2**20),
    )(pick, *blocks, *earlier)


def unpack_kernel(stays, skipped, mine_ref, other_ref, high_ref, low_ref, *refs):
    refs, answers = refs[skipped:], refs[-1]
    half = mine_ref.shape[0]
    answers[:half] = mine_ref[...]
    answers[half:] = other_ref[...]
    total = None
    for part in (high_ref, low_ref):
        term = jnp.dot(part[0], answers[...], preferred_element_type=F32)
        total = term if total is None else total + term
    refs[0][...] = total[:stays]
    for n, out in enumerate(refs[1:-1]):
        out[...] = total[(n + 1) * stays : (n + 2) * stays].astype(BF16)


def unpack(m, sides, mine, other, high, low, *earlier):
    _, tokens, rows = high.shape
    half, features = mine.shape
    width, stays = features // 4, tokens // sides
    out_shape = [jax.ShapeDtypeStruct((stays, features), F32)]
    out_shape += [jax.ShapeDtypeStruct((stays, features), BF16)] * (sides - 1)
    part = pl.BlockSpec((half, width), lambda i: (0, i))
    whole = pl.BlockSpec((1, tokens, rows), lambda i: (m, 0, 0))
    return pl.pallas_call(
        functools.partial(unpack_kernel, stays, len(earlier)),
        grid=(features // width,),
        out_shape=out_shape,
        in_specs=[part, part, whole, whole, *[pl.BlockSpec(memory_space=pl.ANY) for _ in earlier]],
        out_specs=[pl.BlockSpec((shape.shape[0], width), lambda i: (0, i)) for shape in out_shape],
        scratch_shapes=[pltpu.VMEM((rows, width), BF16)],
        cost_estimate=pl.CostEstimate(
            flops=4 * rows * tokens * features,
            bytes_accessed=2 * (rows + 2 * tokens) * features + 4 * rows * tokens,
            transcendentals=0,
        ),
        compiler_params=pltpu.CompilerParams(vmem_limit_bytes=24 * 2**20),
    )(mine, other, high, low, *earlier)


def after(value, *earlier):
    return lax.optimization_barrier((value,) + earlier)[0] if earlier else value


def on_device(tokens, routes, combine, expert_home, up_weight, down_weight):
    up_rows = up_weight[0, 0]
    down_rows = down_weight[0, 0]
    batches, tok_rows, features = tokens.shape
    top_count = routes.shape[2]
    experts = expert_home.shape[0]
    sides = lax.axis_size("expert") // 2
    capacity = min(tok_rows, tok_rows * top_count // experts + tok_rows // 32)
    here = lax.axis_index("expert")
    place = jnp.stack([here // 2, here % 2]).astype(jnp.int32)
    half = -(-sides * 4 * capacity // 16) * 16

    facts = []
    for m in range(batches):
        home, rank = placed_pairs(routes[m], expert_home)
        facts += [(home * tok_rows + rank).astype(F32), combine[m].T]
    facts = jnp.concatenate(facts)
    facts = jnp.stack([facts] + [swapped(facts, "dp", bits) for bits in (1, 2, 3)])

    def across(block):
        return [swapped(block, "expert", 2 * j) for j in range(1, sides)]

    own_x = across(tokens)
    far, both = [None] * batches, [None] * batches
    pair, pair_x, both_x = [None], [None], [None]
    near = swapped(after(tokens, facts), "dp", 1)
    far[0] = swapped(after(tokens[0], facts), "dp", 2)
    facts_x = jnp.stack([facts] + across(facts))
    pick, high, low = plan(place, facts_x, batches, top_count, capacity, half)
    both[0] = swapped(far[0], "dp", 1)
    pair[0] = jnp.concatenate([near[0], far[0]])
    pair_x[0] = across(after(pair[0], facts_x))
    far[1] = swapped(after(tokens[1], far[0]), "dp", 2)
    both_x[0] = across(both[0])
    both[1] = swapped(far[1], "dp", 1)
    triple = jnp.concatenate([near[1], far[1], both[1]])
    triple_x = across(triple)

    def packed(m, blocks, *earlier):
        mine, other = pack(m, pick, [tokens] + own_x + blocks, *earlier)
        return mine, swapped(other, "expert", 1)

    def crossed(block):
        part = block.shape[0] // 48 * 16
        cuts = [block[at : at + part] for at in range(0, block.shape[0], part)]
        return jnp.concatenate([swapped(cut, "expert", 1) for cut in cuts])

    def unpacked(m, mine, other, *earlier):
        return unpack(m, sides, mine, crossed(other), high, low, *earlier)

    def near_sum(staying, first):
        return sum([block.astype(F32) for block in first], staying[: 2 * tok_rows]).astype(BF16)

    def far_sums(staying, second, back):
        return sum([block.astype(F32) for block in second + [back]], staying[2 * tok_rows :])

    rows_0 = packed(0, [pair[0]] + pair_x[0] + [both[0]] + both_x[0], triple)
    answers_0 = expert_share(*rows_0, up_rows, down_rows)
    rows_1 = packed(1, [triple] + triple_x, answers_0[0])
    staying_0, *leaving_0 = unpacked(0, *answers_0, *triple_x)
    sums_0 = [swapped(block, "expert", 2 * j + 2) for j, block in enumerate(leaving_0)]
    answers_1 = expert_share(*rows_1, up_rows, down_rows, leaving_0[0])
    staying_1, *leaving_1 = unpacked(1, *answers_1, *sums_0)
    count = 2 * tok_rows
    first_1, second_1 = (
        [swapped(block[at : at + count], "expert", 2 * j + 2) for j, block in enumerate(leaving_1)]
        for at in (0, count)
    )
    back_0 = swapped(near_sum(staying_0, [b[:count] for b in sums_0]), "dp", 1)
    total_0 = far_sums(staying_0, [b[count:] for b in sums_0], back_0)
    far_0 = swapped(total_0[:tok_rows].astype(BF16), "dp", 2)
    back_1 = swapped(after(near_sum(staying_1, first_1), back_0), "dp", 1)
    total_1 = far_sums(staying_1, second_1, back_1)
    far_1 = swapped(after(total_1[:tok_rows].astype(BF16), far_0), "dp", 2)
    totals = [
        passed_along((total[tok_rows:] + far_part.astype(F32)).astype(BF16), "segment", 1)
        for total, far_part in ((total_0, far_0), (total_1, far_1))
    ]
    return jnp.stack(totals, axis=0)


def solution(mesh):
    return jax.shard_map(
        on_device,
        mesh=mesh,
        in_specs=(
            P(None, ("segment", "expert", "dp"), None),
            P(None, ("segment", "expert", "dp"), None),
            P(None, ("segment", "expert", "dp"), None),
            P(),
            P("segment", "expert", "dp", None),
            P("segment", "expert", "dp", None),
        ),
        out_specs=P(None, ("segment", "expert", "dp"), None),
        check_vma=False,
    )
```

time: 293 us -> 236 us (0.81)
  matrix products: 68.5 us -> 0 us
  Pallas kernels: 0 us -> 58.7 us
  local copies, waits for them, and re-layouts: 37.1 us -> 3.86 us
  waiting for transfers between devices: 156 us -> 136 us
  starting transfers between devices: 26.2 us -> 31.5 us
    dot_general x16 -> x0, matrix products: 68.5 us -> none  [the longest x4 52.7 us: expert_share(): jnp.dot(hidden, down_rows, preferred_element_type=jnp.float32)]
    pallas_call x0 -> x7, Pallas kernels: none -> 58.7 us  [the longest x2 37.6 us: expert_share(): pl.pallas_call(functools.partial(expert_kernel, steps, half), grid=(2 * s...]
    ppermute x27 -> x30, waiting for transfers between devices: 146 us -> 127 us  [swapped(): lax.ppermute(block, axis, [(i, i ^ bits) for i in range(lax.axis_size(axi...]
    slice x19 -> x7, local copies, waits for them, and re-layouts: 16.7 us -> 0.41 us  [the longest x4 0.22 us: crossed(): cuts = [block[at:at + part] for at in range(0, block.shape[0], part)]]
    broadcast_in_dim x8 -> x0, local copies, waits for them, and re-layouts: 9.13 us -> none  [served(): jnp.where(slot[k][:, None] == ids[None, :], weight[k][:, None], 0.0)]
    eq x8 -> x0, local copies, waits for them, and re-layouts: 8.29 us -> none  [served(): slot[k][:, None] == ids[None, :]]
    ppermute x27 -> x30, starting transfers between devices: 23 us -> 28.3 us  [swapped(): lax.ppermute(block, axis, [(i, i ^ bits) for i in range(lax.axis_size(axi...]
  transfers between devices with their start and end apart: 29 -> 32, of which waited for: 14 -> 17; matrix products, arithmetic and copies ran while one was open for 36% -> 3% of each run, Pallas kernels for 0% -> 19%
where the time goes in v2:
time: 236 us
  waiting for transfers between devices  136 us (58%)
  Pallas kernels  58.7 us (25%)
  starting transfers between devices  31.5 us (13%)
  other arithmetic  5.61 us (2%)
  local copies, waits for them, and re-layouts  3.86 us (2%)
    ppermute x30, waiting for transfers between devices, swapped(): lax.ppermute(block, axis, [(i, i ^ bits) for i in range(lax.axis_size(axi...  127 us
    pallas_call x2, Pallas kernels, expert_share(): pl.pallas_call(functools.partial(expert_kernel, steps, half), grid=(2 * s...  37.6 us
    ppermute x30, starting transfers between devices, swapped(): lax.ppermute(block, axis, [(i, i ^ bits) for i in range(lax.axis_size(axi...  28.3 us
    pallas_call x2, Pallas kernels, unpack(): pl.pallas_call(functools.partial(unpack_kernel, stays, len(earlier)), gri...  12.1 us
    ppermute x2, waiting for transfers between devices, passed_along(): return lax.ppermute(block, axis, route)  9.52 us
    pallas_call x2, Pallas kernels, pack(): pl.pallas_call(functools.partial(pack_kernel, len(blocks), half), grid=(f...  7 us
  transfers between devices with their start and end apart: 32, of which 17 were waited for; matrix products, arithmetic and copies ran while one was open for 3% of the time, Pallas kernels for 19%

profile of v2, /device:TPU:0, one launch (start us, length us, event | category | flops | bytes accessed | tf_op | source)
XLA Modules:
  0.0 236.0 jit_solution(3583393633774081702)
XLA Ops:
  2.5 4.1 %collective-permute-start.1 = (f32[8,64]{1,0:T(8,128)S(1)}, f32[8,64]{1,0:T(8,128)S(1)}, u32[]{:S(2)}, u32[]{:S(2)}) collective-permute-start(f32[8,64]{1,0:T(8,128)S(1)} %get-tuple-element.68), channel_id=1, source_target_pairs={{0,2},{1,3},{2,0},{3,1},{4,6},{5,7},{6,4},{7,5},{8,10},{9,11},{10,... | collective-permute-start | bytes 6152 | tf_op jit(solution)/shard_map/ppermute | solution.py:20
  8.2 2.0 collective-permute-done
  10.2 3.4 %collective-permute-done.2 = f32[8,64]{1,0:T(8,128)S(1)} collective-permute-done((f32[8,64]{1,0:T(8,128)S(1)}, f32[8,64]{1,0:T(8,128)S(1)}, u32[]{:S(2)}, u32[]{:S(2)}) %collective-permute-start.2) | collective-permute-done | bytes 2080 | tf_op jit(solution)/shard_map/ppermute | solution.py:20
  15.4 1.7 collective-permute-start.3
  17.4 1.9 collective-permute-done.3
  19.4 18.2 %collective-permute-done.6 = bf16[64,3072]{1,0:T(8,128)(2,1)} collective-permute-done((bf16[64,3072]{1,0:T(8,128)(2,1)S(1)}, bf16[64,3072]{1,0:T(8,128)(2,1)}, u32[]{:S(2)}, u32[]{:S(2)}) %collective-permute-start.6) | collective-permute-done | bytes 393248 | tf_op jit(solution)/shard_map/ppermute | solution.py:20
  37.6 3.6 %collective-permute-start.10 = (bf16[64,3072]{1,0:T(8,128)(2,1)S(1)}, bf16[64,3072]{1,0:T(8,128)(2,1)}, u32[]{:S(2)}, u32[]{:S(2)}) collective-permute-start(bf16[64,3072]{1,0:T(8,128)(2,1)S(1)} %get-tuple-element.30), channel_id=1, source_target_pairs={{0,2},{1,3},{2,0},{3,1},{4,6},{5,7},{6,4},{7,5},{8,10},{9,11},{10,... | collective-permute-start | bytes 1179656 | tf_op jit(solution)/shard_map/ppermute | solution.py:20
  44.6 11.9 %collective-permute-done.10 = bf16[64,3072]{1,0:T(8,128)(2,1)} collective-permute-done((bf16[64,3072]{1,0:T(8,128)(2,1)S(1)}, bf16[64,3072]{1,0:T(8,128)(2,1)}, u32[]{:S(2)}, u32[]{:S(2)}) %collective-permute-start.10) | collective-permute-done | bytes 393248 | tf_op jit(solution)/shard_map/ppermute | solution.py:20
  57.5 1.7 collective-permute-start.9
  59.3 2.0 shard_map.64
  61.2 6.0 %collective-permute-done.11 = bf16[64,3072]{1,0:T(8,128)(2,1)} collective-permute-done((bf16[64,3072]{1,0:T(8,128)(2,1)}, bf16[64,3072]{1,0:T(8,128)(2,1)}, u32[]{:S(2)}, u32[]{:S(2)}) %collective-permute-start.11) | collective-permute-done | bytes 393248 | tf_op jit(solution)/shard_map/ppermute | solution.py:20
  68.6 4.1 %shard_map.65 = (bf16[272,3072]{1,0:T(8,128)(2,1)S(1)}, bf16[272,3072]{1,0:T(8,128)(2,1)S(1)}) custom-call(bf16[2,544,512]{2,1,0:T(8,128)(2,1)S(1)} %get-tuple-element.26.pick_ref, bf16[2,64,3072]{2,1,0:T(8,128)(2,1)S(1)} %copy-done, bf16[2,64,3072]{2,1,0:T(8,128)(2,1)S(1)} %collective-permute-done.4.refs_1_, ...), custom_call_target="tpu_custom_call" | custom-call | flops 1711276032 | bytes 7045120 | tf_op jit(solution)/shard_map/pallas_call | solution.py:174
  72.8 1.8 collective-permute-start.17
  74.6 1.7 collective-permute-done.12.other_ref
  76.4 18.8 %shard_map.66 = (bf16[272,3072]{1,0:T(8,128)(2,1)S(1)}, bf16[272,3072]{1,0:T(8,128)(2,1)S(1)}) custom-call(bf16[272,3072]{1,0:T(8,128)(2,1)S(1)} %get-tuple-element.31.mine_ref, bf16[272,3072]{1,0:T(8,128)(2,1)S(1)} %collective-permute-done.12.other_ref, bf16[2048,3072]{1,0:T(8,128)(2,1)} %bitcast.62, bf16[2048,3072]{1,0:T(8,128)(2,1)} %bitcast.64), custom_call_target="tpu_custom_call" | custom-call | flops 13690208256 | bytes 31850496 | tf_op jit(solution)/shard_map/pallas_call | solution.py:130
  95.2 6.1 %collective-permute-done.17.refs_0_.refs_3_ = bf16[192,3072]{1,0:T(8,128)(2,1)S(1)} collective-permute-done((bf16[192,3072]{1,0:T(8,128)(2,1)S(1)}, bf16[192,3072]{1,0:T(8,128)(2,1)S(1)}, u32[]{:S(2)}, u32[]{:S(2)}) %collective-permute-start.17) | collective-permute-done | bytes 1179680 | tf_op jit(solution)/shard_map/ppermute | solution.py:20
  101.2 2.9 %shard_map.68 = (bf16[272,3072]{1,0:T(8,128)(2,1)S(1)}, bf16[272,3072]{1,0:T(8,128)(2,1)S(1)}) custom-call(bf16[2,544,512]{2,1,0:T(8,128)(2,1)S(1)} %get-tuple-element.26.pick_ref, bf16[2,64,3072]{2,1,0:T(8,128)(2,1)S(1)} %copy-done, bf16[2,64,3072]{2,1,0:T(8,128)(2,1)S(1)} %collective-permute-done.4.refs_1_, ...), custom_call_target="tpu_custom_call" | custom-call | flops 1711276032 | bytes 7045120 | tf_op jit(solution)/shard_map/pallas_call | solution.py:174
  105.5 4.6 %collective-permute-done.16 = bf16[32,3072]{1,0:T(8,128)(2,1)S(1)} collective-permute-done((bf16[32,3072]{1,0:T(8,128)(2,1)S(1)}, bf16[32,3072]{1,0:T(8,128)(2,1)S(1)}, u32[]{:S(2)}, u32[]{:S(2)}) %collective-permute-start.16) | collective-permute-done | bytes 196640 | tf_op jit(solution)/shard_map/ppermute | solution.py:20
  110.2 6.1 %shard_map.67 = (f32[256,3072]{1,0:T(8,128)S(1)}, bf16[256,3072]{1,0:T(8,128)(2,1)S(1)}) custom-call(bf16[272,3072]{1,0:T(8,128)(2,1)S(1)} %get-tuple-element.33.mine_ref.refs_4_, bf16[272,3072]{1,0:T(8,128)(2,1)S(1)} %pad_maximum_fusion.other_ref, bf16[2,512,544]{2,1,0:T(8,128)(2,1)S(1)} %get-tuple-element.35.high_ref, ...), custom_call_target="tpu_custom_call" | custom-call | flops 3422552064 | bytes 10747904 | tf_op jit(solution)/shard_map/pallas_call | solution.py:216
  116.3 1.8 collective-permute-start.18
  118.1 18.8 %shard_map.69 = (bf16[272,3072]{1,0:T(8,128)(2,1)S(1)}, bf16[272,3072]{1,0:T(8,128)(2,1)S(1)}) custom-call(bf16[272,3072]{1,0:T(8,128)(2,1)S(1)} %get-tuple-element.39.mine_ref, bf16[272,3072]{1,0:T(8,128)(2,1)S(1)} %collective-permute-done.22.other_ref, bf16[2048,3072]{1,0:T(8,128)(2,1)} %bitcast.63, bf16[2048,3072]{1,0:T(8,128)(2,1)} %bitcast.65, ...), custom_call_target="tpu_custom_call" | custom-call | flops 13690208256 | bytes 31850496 | tf_op jit(solution)/shard_map/pallas_call | solution.py:130
  138.2 2.4 %collective-permute-done.26 = bf16[32,3072]{1,0:T(8,128)(2,1)S(1)} collective-permute-done((bf16[32,3072]{1,0:T(8,128)(2,1)S(1)}, bf16[32,3072]{1,0:T(8,128)(2,1)S(1)}, u32[]{:S(2)}, u32[]{:S(2)}) %collective-permute-start.26) | collective-permute-done | bytes 196640 | tf_op jit(solution)/shard_map/ppermute | solution.py:20
  140.8 12.0 %collective-permute-done.18.refs_0_ = bf16[256,3072]{1,0:T(8,128)(2,1)S(1)} collective-permute-done((bf16[256,3072]{1,0:T(8,128)(2,1)S(1)}, bf16[256,3072]{1,0:T(8,128)(2,1)S(1)}, u32[]{:S(2)}, u32[]{:S(2)}) %collective-permute-start.18) | collective-permute-done | bytes 1572896 | tf_op jit(solution)/shard_map/ppermute | solution.py:20
  152.8 6.1 %shard_map.70 = (f32[256,3072]{1,0:T(8,128)S(1)}, bf16[256,3072]{1,0:T(8,128)(2,1)S(1)}) custom-call(bf16[272,3072]{1,0:T(8,128)(2,1)S(1)} %get-tuple-element.41.mine_ref, bf16[272,3072]{1,0:T(8,128)(2,1)S(1)} %pad_maximum_fusion.1.other_ref, bf16[2,512,544]{2,1,0:T(8,128)(2,1)S(1)} %get-tuple-element.35.high_ref, ...), custom_call_target="tpu_custom_call" | custom-call | flops 3422552064 | bytes 10747904 | tf_op jit(solution)/shard_map/pallas_call | solution.py:216
  159.0 1.8 collective-permute-start.28
  162.3 17.2 %collective-permute-done.28 = bf16[128,3072]{1,0:T(8,128)(2,1)S(1)} collective-permute-done((bf16[128,3072]{1,0:T(8,128)(2,1)S(1)}, bf16[128,3072]{1,0:T(8,128)(2,1)S(1)}, u32[]{:S(2)}, u32[]{:S(2)}) %collective-permute-start.28) | collective-permute-done | bytes 786464 | tf_op jit(solution)/shard_map/ppermute | solution.py:20
  182.6 12.0 %collective-permute-done.27 = bf16[128,3072]{1,0:T(8,128)(2,1)S(1)} collective-permute-done((bf16[128,3072]{1,0:T(8,128)(2,1)S(1)}, bf16[128,3072]{1,0:T(8,128)(2,1)S(1)}, u32[]{:S(2)}, u32[]{:S(2)}) %collective-permute-start.27) | collective-permute-done | bytes 786464 | tf_op jit(solution)/shard_map/ppermute | solution.py:20
  194.7 10.8 %collective-permute-done.29 = bf16[128,3072]{1,0:T(8,128)(2,1)S(1)} collective-permute-done((bf16[128,3072]{1,0:T(8,128)(2,1)S(1)}, bf16[128,3072]{1,0:T(8,128)(2,1)S(1)}, u32[]{:S(2)}, u32[]{:S(2)}) %collective-permute-start.29) | collective-permute-done | bytes 786464 | tf_op jit(solution)/shard_map/ppermute | solution.py:20
  207.2 1.6 collective-permute-start.21
  208.8 15.1 %collective-permute-done.30 = bf16[64,3072]{1,0:T(8,128)(2,1)S(1)} collective-permute-done((bf16[64,3072]{1,0:T(8,128)(2,1)S(1)}, bf16[64,3072]{1,0:T(8,128)(2,1)S(1)}, u32[]{:S(2)}, u32[]{:S(2)}) %collective-permute-start.30) | collective-permute-done | bytes 393248 | tf_op jit(solution)/shard_map/ppermute | solution.py:20
  223.9 1.6 collective-permute-start.31
  225.5 9.5 %collective-permute-done.31 = bf16[64,3072]{1,0:T(8,128)(2,1)S(1)} collective-permute-done((bf16[64,3072]{1,0:T(8,128)(2,1)S(1)}, bf16[64,3072]{1,0:T(8,128)(2,1)S(1)}, u32[]{:S(2)}, u32[]{:S(2)}) %collective-permute-start.31) | collective-permute-done | bytes 393248 | tf_op jit(solution)/shard_map/ppermute | solution.py:16
  (73 shorter events, 22.4 us)
Async XLA Ops:
  2.5 5.7 %collective-permute-start.1 = (f32[8,64]{1,0:T(8,128)S(1)}, f32[8,64]{1,0:T(8,128)S(1)}, u32[]{:S(2)}, u32[]{:S(2)}) collective-permute-start(f32[8,64]{1,0:T(8,128)S(1)} %get-tuple-element.68), channel_id=1, source_target_pairs={{0,2},{1,3},{2,0},{3,1},{4,6},{5,7},{6,4},{7,5},{8,10},{9,11},{10,... | collective-permute-start | bytes 6152 | tf_op jit(solution)/shard_map/ppermute | solution.py:20
  6.6 3.6 %collective-permute-start = (f32[8,64]{1,0:T(8,128)S(1)}, f32[8,64]{1,0:T(8,128)S(1)}, u32[]{:S(2)}, u32[]{:S(2)}) collective-permute-start(f32[8,64]{1,0:T(8,128)S(1)} %get-tuple-element.68), channel_id=1, source_target_pairs={{0,1},{1,0},{2,3},{3,2},{4,5},{5,4},{6,7},{7,6},{8,9},{9,8},{10,11... | collective-permute-start | bytes 6152 | tf_op jit(solution)/shard_map/ppermute | solution.py:20
  8.2 5.4 %collective-permute-start.2 = (f32[8,64]{1,0:T(8,128)S(1)}, f32[8,64]{1,0:T(8,128)S(1)}, u32[]{:S(2)}, u32[]{:S(2)}) collective-permute-start(f32[8,64]{1,0:T(8,128)S(1)} %get-tuple-element.68), channel_id=1, source_target_pairs={{0,3},{1,2},{2,1},{3,0},{4,7},{5,6},{6,5},{7,4},{8,11},{9,10},{10,... | collective-permute-start | bytes 6152 | tf_op jit(solution)/shard_map/ppermute | solution.py:20
  13.6 27.6 %collective-permute-start.5 = (bf16[2,64,3072]{2,1,0:T(8,128)(2,1)}, bf16[2,64,3072]{2,1,0:T(8,128)(2,1)S(1)}, u32[]{:S(2)}, u32[]{:S(2)}) collective-permute-start(bf16[2,64,3072]{2,1,0:T(8,128)(2,1)} %refs_0_.3), channel_id=1, source_target_pairs={{0,1},{1,0},{2,3},{3,2},{4,5},{5,4},{6,7},{7,6},{8,9},{9,8},{10,11... | collective-permute-start | bytes 2359304 | tf_op jit(solution)/shard_map/ppermute | solution.py:20
  14.8 22.8 %collective-permute-start.6 = (bf16[64,3072]{1,0:T(8,128)(2,1)S(1)}, bf16[64,3072]{1,0:T(8,128)(2,1)}, u32[]{:S(2)}, u32[]{:S(2)}) collective-permute-start(bf16[64,3072]{1,0:T(8,128)(2,1)S(1)} %get-tuple-element.28), channel_id=1, source_target_pairs={{0,2},{1,3},{2,0},{3,1},{4,6},{5,7},{6,4},{7,5},{8,10},{9,11},{10,... | collective-permute-start | bytes 1179656 | tf_op jit(solution)/shard_map/ppermute | solution.py:20
  15.4 4.0 %collective-permute-start.3 = (f32[4,8,64]{2,1,0:T(8,128)S(1)}, f32[4,8,64]{2,1,0:T(8,128)S(1)}, u32[]{:S(2)}, u32[]{:S(2)}) collective-permute-start(f32[4,8,64]{2,1,0:T(8,128)S(1)} %get-tuple-element.66), channel_id=1, source_target_pairs={{0,8},{4,12},{8,0},{12,4},{1,9},{5,13},{9,1},{13,5},{2,10},{6,14},... | collective-permute-start | bytes 24584 | tf_op jit(solution)/shard_map/ppermute | solution.py:20
  17.1 51.5 %collective-permute-start.4 = (bf16[2,64,3072]{2,1,0:T(8,128)(2,1)S(1)}, bf16[2,64,3072]{2,1,0:T(8,128)(2,1)S(1)}, u32[]{:S(2)}, u32[]{:S(2)}) collective-permute-start(bf16[2,64,3072]{2,1,0:T(8,128)(2,1)S(1)} %copy-done), channel_id=1, source_target_pairs={{0,8},{4,12},{8,0},{12,4},{1,9},{5,13},{9,1},{13,5},{2,10},{6,14},... | collective-permute-start | bytes 2359304 | tf_op jit(solution)/shard_map/ppermute | solution.py:20
  37.6 18.9 %collective-permute-start.10 = (bf16[64,3072]{1,0:T(8,128)(2,1)S(1)}, bf16[64,3072]{1,0:T(8,128)(2,1)}, u32[]{:S(2)}, u32[]{:S(2)}) collective-permute-start(bf16[64,3072]{1,0:T(8,128)(2,1)S(1)} %get-tuple-element.30), channel_id=1, source_target_pairs={{0,2},{1,3},{2,0},{3,1},{4,6},{5,7},{6,4},{7,5},{8,10},{9,11},{10,... | collective-permute-start | bytes 1179656 | tf_op jit(solution)/shard_map/ppermute | solution.py:20
  41.2 16.3 %collective-permute-start.8 = (bf16[64,3072]{1,0:T(8,128)(2,1)}, bf16[64,3072]{1,0:T(8,128)(2,1)}, u32[]{:S(2)}, u32[]{:S(2)}) collective-permute-start(bf16[64,3072]{1,0:T(8,128)(2,1)} %collective-permute-done.6), channel_id=1, source_target_pairs={{0,1},{1,0},{2,3},{3,2},{4,5},{5,4},{6,7},{7,6},{8,9},{9,8},{10,11... | collective-permute-start | bytes 1179656 | tf_op jit(solution)/shard_map/ppermute | solution.py:20
  43.0 25.6 %collective-permute-start.7 = (bf16[128,3072]{1,0:T(8,128)(2,1)S(1)}, bf16[128,3072]{1,0:T(8,128)(2,1)S(1)}, u32[]{:S(2)}, u32[]{:S(2)}) collective-permute-start(bf16[128,3072]{1,0:T(8,128)(2,1)S(1)} %pad_maximum_fusion.3.refs_2_), channel_id=1, source_target_pairs={{0,8},{4,12},{8,0},{12,4},{1,9},{5,13},{9,1},{13,5},{2,10},{6,14},... | collective-permute-start | bytes 2359304 | tf_op jit(solution)/shard_map/ppermute | solution.py:20
  56.5 10.8 %collective-permute-start.11 = (bf16[64,3072]{1,0:T(8,128)(2,1)}, bf16[64,3072]{1,0:T(8,128)(2,1)}, u32[]{:S(2)}, u32[]{:S(2)}) collective-permute-start(bf16[64,3072]{1,0:T(8,128)(2,1)} %collective-permute-done.10), channel_id=1, source_target_pairs={{0,1},{1,0},{2,3},{3,2},{4,5},{5,4},{6,7},{7,6},{8,9},{9,8},{10,11... | collective-permute-start | bytes 1179656 | tf_op jit(solution)/shard_map/ppermute | solution.py:20
  57.5 11.1 %collective-permute-start.9 = (bf16[64,3072]{1,0:T(8,128)(2,1)}, bf16[64,3072]{1,0:T(8,128)(2,1)S(1)}, u32[]{:S(2)}, u32[]{:S(2)}) collective-permute-start(bf16[64,3072]{1,0:T(8,128)(2,1)} %collective-permute-done.8.refs_4_), channel_id=1, source_target_pairs={{0,8},{4,12},{8,0},{12,4},{1,9},{5,13},{9,1},{13,5},{2,10},{6,14},... | collective-permute-start | bytes 1179656 | tf_op jit(solution)/shard_map/ppermute | solution.py:20
  72.7 3.6 %collective-permute-start.12 = (bf16[272,3072]{1,0:T(8,128)(2,1)S(1)}, bf16[272,3072]{1,0:T(8,128)(2,1)S(1)}, u32[]{:S(2)}, u32[]{:S(2)}) collective-permute-start(bf16[272,3072]{1,0:T(8,128)(2,1)S(1)} %get-tuple-element.32), channel_id=1, source_target_pairs={{0,4},{4,0},{8,12},{12,8},{1,5},{5,1},{9,13},{13,9},{2,6},{6,2},{1... | collective-permute-start | bytes 5013512 | tf_op jit(solution)/shard_map/ppermute | solution.py:20
  72.8 28.4 %collective-permute-start.17 = (bf16[192,3072]{1,0:T(8,128)(2,1)S(1)}, bf16[192,3072]{1,0:T(8,128)(2,1)S(1)}, u32[]{:S(2)}, u32[]{:S(2)}) collective-permute-start(bf16[192,3072]{1,0:T(8,128)(2,1)S(1)} %pad_maximum_fusion.2.refs_6_.refs_2_), channel_id=1, source_target_pairs={{0,8},{4,12},{8,0},{12,4},{1,9},{5,13},{9,1},{13,5},{2,10},{6,14},... | collective-permute-start | bytes 3538952 | tf_op jit(solution)/shard_map/ppermute | solution.py:20
  104.1 14.0 %collective-permute-start.22 = (bf16[272,3072]{1,0:T(8,128)(2,1)S(1)}, bf16[272,3072]{1,0:T(8,128)(2,1)S(1)}, u32[]{:S(2)}, u32[]{:S(2)}) collective-permute-start(bf16[272,3072]{1,0:T(8,128)(2,1)S(1)} %get-tuple-element.40), channel_id=1, source_target_pairs={{0,4},{4,0},{8,12},{12,8},{1,5},{5,1},{9,13},{13,9},{2,6},{6,2},{1... | collective-permute-start | bytes 5013512 | tf_op jit(solution)/shard_map/ppermute | solution.py:20
  104.3 5.8 %collective-permute-start.13 = (bf16[80,3072]{1,0:T(8,128)(2,1)S(1)}, bf16[80,3072]{1,0:T(8,128)(2,1)S(1)}, u32[]{:S(2)}, u32[]{:S(2)}) collective-permute-start(bf16[80,3072]{1,0:T(8,128)(2,1)S(1)} %get-tuple-element.56), channel_id=1, source_target_pairs={{0,4},{4,0},{8,12},{12,8},{1,5},{5,1},{9,13},{13,9},{2,6},{6,2},{1... | collective-permute-start | bytes 1474568 | tf_op jit(solution)/shard_map/ppermute | solution.py:20
  104.8 5.3 %collective-permute-start.15 = (bf16[80,3072]{1,0:T(8,128)(2,1)S(1)}, bf16[80,3072]{1,0:T(8,128)(2,1)S(1)}, u32[]{:S(2)}, u32[]{:S(2)}) collective-permute-start(bf16[80,3072]{1,0:T(8,128)(2,1)S(1)} %get-tuple-element.57), channel_id=1, source_target_pairs={{0,4},{4,0},{8,12},{12,8},{1,5},{5,1},{9,13},{13,9},{2,6},{6,2},{1... | collective-permute-start | bytes 1474568 | tf_op jit(solution)/shard_map/ppermute | solution.py:20
  104.9 5.2 %collective-permute-start.14 = (bf16[80,3072]{1,0:T(8,128)(2,1)S(1)}, bf16[80,3072]{1,0:T(8,128)(2,1)S(1)}, u32[]{:S(2)}, u32[]{:S(2)}) collective-permute-start(bf16[80,3072]{1,0:T(8,128)(2,1)S(1)} %get-tuple-element.58), channel_id=1, source_target_pairs={{0,4},{4,0},{8,12},{12,8},{1,5},{5,1},{9,13},{13,9},{2,6},{6,2},{1... | collective-permute-start | bytes 1474568 | tf_op jit(solution)/shard_map/ppermute | solution.py:20
  105.4 4.7 %collective-permute-start.16 = (bf16[32,3072]{1,0:T(8,128)(2,1)S(1)}, bf16[32,3072]{1,0:T(8,128)(2,1)S(1)}, u32[]{:S(2)}, u32[]{:S(2)}) collective-permute-start(bf16[32,3072]{1,0:T(8,128)(2,1)S(1)} %slice.113), channel_id=1, source_target_pairs={{0,4},{4,0},{8,12},{12,8},{1,5},{5,1},{9,13},{13,9},{2,6},{6,2},{1... | collective-permute-start | bytes 589832 | tf_op jit(solution)/shard_map/ppermute | solution.py:20
  116.3 36.5 %collective-permute-start.18 = (bf16[256,3072]{1,0:T(8,128)(2,1)S(1)}, bf16[256,3072]{1,0:T(8,128)(2,1)S(1)}, u32[]{:S(2)}, u32[]{:S(2)}) collective-permute-start(bf16[256,3072]{1,0:T(8,128)(2,1)S(1)} %get-tuple-element.38.refs_0_), channel_id=1, source_target_pairs={{0,8},{4,12},{8,0},{12,4},{1,9},{5,13},{9,1},{13,5},{2,10},{6,14},... | collective-permute-start | bytes 4718600 | tf_op jit(solution)/shard_map/ppermute | solution.py:20
  137.0 3.6 %collective-permute-start.23 = (bf16[80,3072]{1,0:T(8,128)(2,1)S(1)}, bf16[80,3072]{1,0:T(8,128)(2,1)S(1)}, u32[]{:S(2)}, u32[]{:S(2)}) collective-permute-start(bf16[80,3072]{1,0:T(8,128)(2,1)S(1)} %get-tuple-element.53), channel_id=1, source_target_pairs={{0,4},{4,0},{8,12},{12,8},{1,5},{5,1},{9,13},{13,9},{2,6},{6,2},{1... | collective-permute-start | bytes 1474568 | tf_op jit(solution)/shard_map/ppermute | solution.py:20
  137.1 3.5 %collective-permute-start.25 = (bf16[80,3072]{1,0:T(8,128)(2,1)S(1)}, bf16[80,3072]{1,0:T(8,128)(2,1)S(1)}, u32[]{:S(2)}, u32[]{:S(2)}) collective-permute-start(bf16[80,3072]{1,0:T(8,128)(2,1)S(1)} %get-tuple-element.54), channel_id=1, source_target_pairs={{0,4},{4,0},{8,12},{12,8},{1,5},{5,1},{9,13},{13,9},{2,6},{6,2},{1... | collective-permute-start | bytes 1474568 | tf_op jit(solution)/shard_map/ppermute | solution.py:20
  137.6 3.0 %collective-permute-start.24 = (bf16[80,3072]{1,0:T(8,128)(2,1)S(1)}, bf16[80,3072]{1,0:T(8,128)(2,1)S(1)}, u32[]{:S(2)}, u32[]{:S(2)}) collective-permute-start(bf16[80,3072]{1,0:T(8,128)(2,1)S(1)} %get-tuple-element.55), channel_id=1, source_target_pairs={{0,4},{4,0},{8,12},{12,8},{1,5},{5,1},{9,13},{13,9},{2,6},{6,2},{1... | collective-permute-start | bytes 1474568 | tf_op jit(solution)/shard_map/ppermute | solution.py:20
  137.7 2.9 %collective-permute-start.26 = (bf16[32,3072]{1,0:T(8,128)(2,1)S(1)}, bf16[32,3072]{1,0:T(8,128)(2,1)S(1)}, u32[]{:S(2)}, u32[]{:S(2)}) collective-permute-start(bf16[32,3072]{1,0:T(8,128)(2,1)S(1)} %slice.123), channel_id=1, source_target_pairs={{0,4},{4,0},{8,12},{12,8},{1,5},{5,1},{9,13},{13,9},{2,6},{6,2},{1... | collective-permute-start | bytes 589832 | tf_op jit(solution)/shard_map/ppermute | solution.py:20
  159.0 20.5 %collective-permute-start.28 = (bf16[128,3072]{1,0:T(8,128)(2,1)S(1)}, bf16[128,3072]{1,0:T(8,128)(2,1)S(1)}, u32[]{:S(2)}, u32[]{:S(2)}) collective-permute-start(bf16[128,3072]{1,0:T(8,128)(2,1)S(1)} %get-tuple-element.60), channel_id=1, source_target_pairs={{0,8},{4,12},{8,0},{12,4},{1,9},{5,13},{9,1},{13,5},{2,10},{6,14},... | collective-permute-start | bytes 2359304 | tf_op jit(solution)/shard_map/ppermute | solution.py:20
  160.9 18.8 %collective-permute-start.19 = (bf16[128,3072]{1,0:T(8,128)(2,1)S(1)}, bf16[128,3072]{1,0:T(8,128)(2,1)S(1)}, u32[]{:S(2)}, u32[]{:S(2)}) collective-permute-start(bf16[128,3072]{1,0:T(8,128)(2,1)S(1)} %add_convert_fusion.1), channel_id=1, source_target_pairs={{0,1},{1,0},{2,3},{3,2},{4,5},{5,4},{6,7},{7,6},{8,9},{9,8},{10,11... | collective-permute-start | bytes 2359304 | tf_op jit(solution)/shard_map/ppermute | solution.py:20
  161.8 32.9 %collective-permute-start.27 = (bf16[128,3072]{1,0:T(8,128)(2,1)S(1)}, bf16[128,3072]{1,0:T(8,128)(2,1)S(1)}, u32[]{:S(2)}, u32[]{:S(2)}) collective-permute-start(bf16[128,3072]{1,0:T(8,128)(2,1)S(1)} %get-tuple-element.59), channel_id=1, source_target_pairs={{0,8},{4,12},{8,0},{12,4},{1,9},{5,13},{9,1},{13,5},{2,10},{6,14},... | collective-permute-start | bytes 2359304 | tf_op jit(solution)/shard_map/ppermute | solution.py:20
  179.7 25.7 %collective-permute-start.29 = (bf16[128,3072]{1,0:T(8,128)(2,1)S(1)}, bf16[128,3072]{1,0:T(8,128)(2,1)S(1)}, u32[]{:S(2)}, u32[]{:S(2)}) collective-permute-start(bf16[128,3072]{1,0:T(8,128)(2,1)S(1)} %add_convert_fusion), channel_id=1, source_target_pairs={{0,1},{1,0},{2,3},{3,2},{4,5},{5,4},{6,7},{7,6},{8,9},{9,8},{10,11... | collective-permute-start | bytes 2359304 | tf_op jit(solution)/shard_map/ppermute | solution.py:20
  181.1 24.7 %collective-permute-start.20 = (bf16[64,3072]{1,0:T(8,128)(2,1)S(1)}, bf16[64,3072]{1,0:T(8,128)(2,1)S(1)}, u32[]{:S(2)}, u32[]{:S(2)}) collective-permute-start(bf16[64,3072]{1,0:T(8,128)(2,1)S(1)} %slice.167), channel_id=1, source_target_pairs={{0,2},{1,3},{2,0},{3,1},{4,6},{5,7},{6,4},{7,5},{8,10},{9,11},{10,... | collective-permute-start | bytes 1179656 | tf_op jit(solution)/shard_map/ppermute | solution.py:20
  205.8 18.0 %collective-permute-start.30 = (bf16[64,3072]{1,0:T(8,128)(2,1)S(1)}, bf16[64,3072]{1,0:T(8,128)(2,1)S(1)}, u32[]{:S(2)}, u32[]{:S(2)}) collective-permute-start(bf16[64,3072]{1,0:T(8,128)(2,1)S(1)} %slice.166), channel_id=1, source_target_pairs={{0,2},{1,3},{2,0},{3,1},{4,6},{5,7},{6,4},{7,5},{8,10},{9,11},{10,... | collective-permute-start | bytes 1179656 | tf_op jit(solution)/shard_map/ppermute | solution.py:20
  207.2 18.3 %collective-permute-start.21 = (bf16[64,3072]{1,0:T(8,128)(2,1)S(1)}, bf16[64,3072]{1,0:T(8,128)(2,1)S(1)}, u32[]{:S(2)}, u32[]{:S(2)}) collective-permute-start(bf16[64,3072]{1,0:T(8,128)(2,1)S(1)} %fusion.1), channel_id=1, source_target_pairs={{16,0},{0,16},{17,1},{1,17},{18,2},{2,18},{19,3},{3,19},{20,4},{4,... | collective-permute-start | bytes 1179656 | tf_op jit(solution)/shard_map/ppermute | solution.py:16
  223.9 11.1 %collective-permute-start.31 = (bf16[64,3072]{1,0:T(8,128)(2,1)S(1)}, bf16[64,3072]{1,0:T(8,128)(2,1)S(1)}, u32[]{:S(2)}, u32[]{:S(2)}) collective-permute-start(bf16[64,3072]{1,0:T(8,128)(2,1)S(1)} %fusion), channel_id=1, source_target_pairs={{16,0},{0,16},{17,1},{1,17},{18,2},{2,18},{19,3},{3,19},{20,4},{4,... | collective-permute-start | bytes 1179656 | tf_op jit(solution)/shard_map/ppermute | solution.py:16
  (1 other events, 17.1 us)

commit v3 on v2

--- a/solution.py
+++ b/solution.py
@@ -41,8 +41,9 @@
     return [(j, bits) for step in steps for j in range(sides) for bits in step]
 
 
-def departures(sides):
-    return [(j, bits) for j in range(sides) for bits in (3, 1, 2, 0)]
+def departures(sides, batch):
+    order = (3, 1, 2, 0) if batch == 0 else (3, 2, 1, 0)
+    return [(j, bits) for j in range(sides) for bits in order]
 
 
 def plan_kernel(sides, batches, top_count, capacity, half, place_ref, facts_ref, pick_ref, high_ref, low_ref):
@@ -57,7 +58,7 @@
         mix = jnp.zeros((padded, tokens), F32)
         for k in range(top_count):
             slots, weights = {}, {}
-            for j, bits in departures(sides):
+            for j, bits in departures(sides, m):
                 at = m * 2 * top_count + k
                 code = facts_ref[j, bits, at : at + 1, :].astype(jnp.int32)
                 at = at + top_count
@@ -67,8 +68,8 @@
                 slots[j, bits] = jnp.where(home // 2 == side, slot, -1)
             hit = ids[:rows] == jnp.concatenate([slots[at] for at in arrivals(sides, m)], axis=1)
             pick = jnp.where(hit, 1.0, pick)
-            hit = ids == jnp.concatenate([slots[at] for at in departures(sides)], axis=1)
-            mix = jnp.where(hit, jnp.concatenate([weights[at] for at in departures(sides)], axis=1), mix)
+            hit = ids == jnp.concatenate([slots[at] for at in departures(sides, m)], axis=1)
+            mix = jnp.where(hit, jnp.concatenate([weights[at] for at in departures(sides, m)], axis=1), mix)
         mix = mix.T[:, :rows]
         high = mix.astype(BF16)
         pick_ref[m] = pick.astype(BF16)
@@ -281,7 +282,7 @@
         return jnp.concatenate([swapped(cut, "expert", 1) for cut in cuts])
 
     def unpacked(m, mine, other, *earlier):
-        return unpack(m, sides, mine, crossed(other), high, low, *earlier)
+        return unpack(m, sides, mine, other, high, low, *earlier)
 
     def near_sum(staying, first):
         return sum([block.astype(F32) for block in first], staying[: 2 * tok_rows]).astype(BF16)
@@ -292,25 +293,33 @@
     rows_0 = packed(0, [pair[0]] + pair_x[0] + [both[0]] + both_x[0], triple)
     answers_0 = expert_share(*rows_0, up_rows, down_rows)
     rows_1 = packed(1, [triple] + triple_x, answers_0[0])
-    staying_0, *leaving_0 = unpacked(0, *answers_0, *triple_x)
+    other = swapped(after(answers_0[1], *triple_x), "expert", 1)
+    staying_0, *leaving_0 = unpacked(0, answers_0[0], other)
     sums_0 = [swapped(block, "expert", 2 * j + 2) for j, block in enumerate(leaving_0)]
     answers_1 = expert_share(*rows_1, up_rows, down_rows, leaving_0[0])
-    staying_1, *leaving_1 = unpacked(1, *answers_1, *sums_0)
+    staying_1, *leaving_1 = unpacked(1, answers_1[0], crossed(answers_1[1]))
     count = 2 * tok_rows
-    first_1, second_1 = (
-        [swapped(block[at : at + count], "expert", 2 * j + 2) for j, block in enumerate(leaving_1)]
-        for at in (0, count)
+    leaving_1 = [after(block, *sums_0) for block in leaving_1]
+    far_1, pair_1 = (
+        [swapped(block[at : at + tok_rows], "expert", 2 * j + 2) for j, block in enumerate(leaving_1)]
+        for at in (0, tok_rows)
     )
     back_0 = swapped(near_sum(staying_0, [b[:count] for b in sums_0]), "dp", 1)
     total_0 = far_sums(staying_0, [b[count:] for b in sums_0], back_0)
     far_0 = swapped(total_0[:tok_rows].astype(BF16), "dp", 2)
-    back_1 = swapped(after(near_sum(staying_1, first_1), back_0), "dp", 1)
-    total_1 = far_sums(staying_1, second_1, back_1)
-    far_1 = swapped(after(total_1[:tok_rows].astype(BF16), far_0), "dp", 2)
-    totals = [
-        passed_along((total[tok_rows:] + far_part.astype(F32)).astype(BF16), "segment", 1)
-        for total, far_part in ((total_0, far_0), (total_1, far_1))
+    def summed(at, blocks):
+        return sum([block.astype(F32) for block in blocks], staying_1[at * tok_rows : (at + 1) * tok_rows])
+
+    back_1 = swapped(summed(0, far_1).astype(BF16), "dp", 1)
+    rest_1 = [
+        swapped(after(block[count:], back_1, *pair_1), "expert", 2 * j + 2) for j, block in enumerate(leaving_1)
     ]
+    total_1 = summed(1, pair_1 + [back_1])
+    far_1 = swapped(total_1.astype(BF16), "dp", 2)
+    back = swapped(summed(2, [block[:tok_rows] for block in rest_1]).astype(BF16), "dp", 1)
+    total_1 = summed(3, [block[tok_rows:] for block in rest_1] + [back, far_1])
+    total_0 = total_0[tok_rows:] + far_0.astype(F32)
+    totals = [passed_along(total.astype(BF16), "segment", 1) for total in (total_0, total_1)]
     return jnp.stack(totals, axis=0)
 
 

time: 236 us -> 224 us (0.949)
  waiting for transfers between devices: 136 us -> 123 us
    ppermute x30 -> x29, waiting for transfers between devices: 127 us -> 116 us  [swapped(): lax.ppermute(block, axis, [(i, i ^ bits) for i in range(lax.axis_size(axi...]
    ppermute x2, waiting for transfers between devices: 9.52 us -> 7.15 us  [passed_along(): return lax.ppermute(block, axis, route)]
    ppermute x30 -> x29, starting transfers between devices: 28.3 us -> 29.3 us  [swapped(): lax.ppermute(block, axis, [(i, i ^ bits) for i in range(lax.axis_size(axi...]
  transfers between devices with their start and end apart: 32 -> 31, of which waited for: 17 -> 19; matrix products, arithmetic and copies ran while one was open for 3% -> 3% of each run, Pallas kernels for 19% -> 24%
where the time goes in v3:
time: 224 us; the launch traced here: 223 us
  waiting for transfers between devices  123 us (55%)
  Pallas kernels  58.7 us (26%)
  starting transfers between devices  32.5 us (15%)
  other arithmetic  5.49 us (2%)
  local copies, waits for them, and re-layouts  3.71 us (2%)
    ppermute x29, waiting for transfers between devices, swapped(): lax.ppermute(block, axis, [(i, i ^ bits) for i in range(lax.axis_size(axi...  116 us
    pallas_call x2, Pallas kernels, expert_share(): pl.pallas_call(functools.partial(expert_kernel, steps, half), grid=(2 * s...  37.6 us
    ppermute x29, starting transfers between devices, swapped(): lax.ppermute(block, axis, [(i, i ^ bits) for i in range(lax.axis_size(axi...  29.3 us
    pallas_call x2, Pallas kernels, unpack(): pl.pallas_call(functools.partial(unpack_kernel, stays, len(earlier)), gri...  12.1 us
    ppermute x2, waiting for transfers between devices, passed_along(): return lax.ppermute(block, axis, route)  7.15 us
    pallas_call x2, Pallas kernels, pack(): pl.pallas_call(functools.partial(pack_kernel, len(blocks), half), grid=(f...  7.01 us
  transfers between devices with their start and end apart: 31, of which 19 were waited for; matrix products, arithmetic and copies ran while one was open for 3% of the time, Pallas kernels for 24%

profile of v3, /device:TPU:0, one launch (start us, length us, event | category | flops | bytes accessed | tf_op | source)
XLA Modules:
  0.0 223.3 jit_solution(1471156778600520308)
XLA Ops:
  2.5 4.1 %collective-permute-start.1 = (f32[8,64]{1,0:T(8,128)S(1)}, f32[8,64]{1,0:T(8,128)S(1)}, u32[]{:S(2)}, u32[]{:S(2)}) collective-permute-start(f32[8,64]{1,0:T(8,128)S(1)} %get-tuple-element.69), channel_id=1, source_target_pairs={{0,2},{1,3},{2,0},{3,1},{4,6},{5,7},{6,4},{7,5},{8,10},{9,11},{10,... | collective-permute-start | bytes 6152 | tf_op jit(solution)/shard_map/ppermute | solution.py:20
  8.2 2.0 collective-permute-done
  10.2 3.4 %collective-permute-done.2 = f32[8,64]{1,0:T(8,128)S(1)} collective-permute-done((f32[8,64]{1,0:T(8,128)S(1)}, f32[8,64]{1,0:T(8,128)S(1)}, u32[]{:S(2)}, u32[]{:S(2)}) %collective-permute-start.2) | collective-permute-done | bytes 2080 | tf_op jit(solution)/shard_map/ppermute | solution.py:20
  15.4 1.7 collective-permute-start.3
  17.4 1.9 collective-permute-done.3
  19.4 18.2 %collective-permute-done.6 = bf16[64,3072]{1,0:T(8,128)(2,1)} collective-permute-done((bf16[64,3072]{1,0:T(8,128)(2,1)S(1)}, bf16[64,3072]{1,0:T(8,128)(2,1)}, u32[]{:S(2)}, u32[]{:S(2)}) %collective-permute-start.6) | collective-permute-done | bytes 393248 | tf_op jit(solution)/shard_map/ppermute | solution.py:20
  37.6 3.6 %collective-permute-start.10 = (bf16[64,3072]{1,0:T(8,128)(2,1)S(1)}, bf16[64,3072]{1,0:T(8,128)(2,1)}, u32[]{:S(2)}, u32[]{:S(2)}) collective-permute-start(bf16[64,3072]{1,0:T(8,128)(2,1)S(1)} %get-tuple-element.31), channel_id=1, source_target_pairs={{0,2},{1,3},{2,0},{3,1},{4,6},{5,7},{6,4},{7,5},{8,10},{9,11},{10,... | collective-permute-start | bytes 1179656 | tf_op jit(solution)/shard_map/ppermute | solution.py:20
  44.6 11.9 %collective-permute-done.10 = bf16[64,3072]{1,0:T(8,128)(2,1)} collective-permute-done((bf16[64,3072]{1,0:T(8,128)(2,1)S(1)}, bf16[64,3072]{1,0:T(8,128)(2,1)}, u32[]{:S(2)}, u32[]{:S(2)}) %collective-permute-start.10) | collective-permute-done | bytes 393248 | tf_op jit(solution)/shard_map/ppermute | solution.py:20
  57.5 1.7 collective-permute-start.9
  59.3 2.0 shard_map.64
  61.3 6.0 %collective-permute-done.11 = bf16[64,3072]{1,0:T(8,128)(2,1)} collective-permute-done((bf16[64,3072]{1,0:T(8,128)(2,1)}, bf16[64,3072]{1,0:T(8,128)(2,1)}, u32[]{:S(2)}, u32[]{:S(2)}) %collective-permute-start.11) | collective-permute-done | bytes 393248 | tf_op jit(solution)/shard_map/ppermute | solution.py:20
  68.6 4.1 %shard_map.65 = (bf16[272,3072]{1,0:T(8,128)(2,1)S(1)}, bf16[272,3072]{1,0:T(8,128)(2,1)S(1)}) custom-call(bf16[2,544,512]{2,1,0:T(8,128)(2,1)S(1)} %get-tuple-element.27.pick_ref, bf16[2,64,3072]{2,1,0:T(8,128)(2,1)S(1)} %copy-done, bf16[2,64,3072]{2,1,0:T(8,128)(2,1)S(1)} %collective-permute-done.4.refs_1_, ...), custom_call_target="tpu_custom_call" | custom-call | flops 1711276032 | bytes 7045120 | tf_op jit(solution)/shard_map/pallas_call | solution.py:175
  72.8 1.8 collective-permute-start.13
  74.6 1.7 collective-permute-done.12.other_ref
  76.4 18.8 %shard_map.66 = (bf16[272,3072]{1,0:T(8,128)(2,1)S(1)}, bf16[272,3072]{1,0:T(8,128)(2,1)S(1)}) custom-call(bf16[272,3072]{1,0:T(8,128)(2,1)S(1)} %get-tuple-element.32.mine_ref, bf16[272,3072]{1,0:T(8,128)(2,1)S(1)} %collective-permute-done.12.other_ref, bf16[2048,3072]{1,0:T(8,128)(2,1)} %bitcast.62, bf16[2048,3072]{1,0:T(8,128)(2,1)} %bitcast.64), custom_call_target="tpu_custom_call" | custom-call | flops 13690208256 | bytes 31850496 | tf_op jit(solution)/shard_map/pallas_call | solution.py:131
  95.2 6.1 %collective-permute-done.13.refs_3_ = bf16[192,3072]{1,0:T(8,128)(2,1)S(1)} collective-permute-done((bf16[192,3072]{1,0:T(8,128)(2,1)S(1)}, bf16[192,3072]{1,0:T(8,128)(2,1)S(1)}, u32[]{:S(2)}, u32[]{:S(2)}) %collective-permute-start.13) | collective-permute-done | bytes 1179680 | tf_op jit(solution)/shard_map/ppermute | solution.py:20
  101.2 2.9 %shard_map.68 = (bf16[272,3072]{1,0:T(8,128)(2,1)S(1)}, bf16[272,3072]{1,0:T(8,128)(2,1)S(1)}) custom-call(bf16[2,544,512]{2,1,0:T(8,128)(2,1)S(1)} %get-tuple-element.27.pick_ref, bf16[2,64,3072]{2,1,0:T(8,128)(2,1)S(1)} %copy-done, bf16[2,64,3072]{2,1,0:T(8,128)(2,1)S(1)} %collective-permute-done.4.refs_1_, ...), custom_call_target="tpu_custom_call" | custom-call | flops 1711276032 | bytes 7045120 | tf_op jit(solution)/shard_map/pallas_call | solution.py:175
  104.8 6.1 %shard_map.67 = (f32[256,3072]{1,0:T(8,128)S(1)}, bf16[256,3072]{1,0:T(8,128)(2,1)S(1)}) custom-call(bf16[272,3072]{1,0:T(8,128)(2,1)S(1)} %get-tuple-element.34.mine_ref.refs_4_, bf16[272,3072]{1,0:T(8,128)(2,1)S(1)} %collective-permute-done.14.other_ref, bf16[2,512,544]{2,1,0:T(8,128)(2,1)S(1)} %get-tuple-element.37.high_ref, ...), custom_call_target="tpu_custom_call" | custom-call | flops 3422552064 | bytes 10747904 | tf_op jit(solution)/shard_map/pallas_call | solution.py:217
  110.8 1.8 collective-permute-start.15
  112.6 18.8 %shard_map.69 = (bf16[272,3072]{1,0:T(8,128)(2,1)S(1)}, bf16[272,3072]{1,0:T(8,128)(2,1)S(1)}) custom-call(bf16[272,3072]{1,0:T(8,128)(2,1)S(1)} %get-tuple-element.41.mine_ref, bf16[272,3072]{1,0:T(8,128)(2,1)S(1)} %collective-permute-done.19.other_ref, bf16[2048,3072]{1,0:T(8,128)(2,1)} %bitcast.63, bf16[2048,3072]{1,0:T(8,128)(2,1)} %bitcast.65, ...), custom_call_target="tpu_custom_call" | custom-call | flops 13690208256 | bytes 31850496 | tf_op jit(solution)/shard_map/pallas_call | solution.py:131
  132.7 2.4 %collective-permute-done.23 = bf16[32,3072]{1,0:T(8,128)(2,1)S(1)} collective-permute-done((bf16[32,3072]{1,0:T(8,128)(2,1)S(1)}, bf16[32,3072]{1,0:T(8,128)(2,1)S(1)}, u32[]{:S(2)}, u32[]{:S(2)}) %collective-permute-start.23) | collective-permute-done | bytes 196640 | tf_op jit(solution)/shard_map/ppermute | solution.py:20
  135.3 6.1 %shard_map.70 = (f32[256,3072]{1,0:T(8,128)S(1)}, bf16[256,3072]{1,0:T(8,128)(2,1)S(1)}) custom-call(bf16[272,3072]{1,0:T(8,128)(2,1)S(1)} %get-tuple-element.43.mine_ref, bf16[272,3072]{1,0:T(8,128)(2,1)S(1)} %pad_maximum_fusion.other_ref, bf16[2,512,544]{2,1,0:T(8,128)(2,1)S(1)} %get-tuple-element.37.high_ref, ...), custom_call_target="tpu_custom_call" | custom-call | flops 3422552064 | bytes 10747904 | tf_op jit(solution)/shard_map/pallas_call | solution.py:217
  141.4 6.0 %collective-permute-done.15 = bf16[256,3072]{1,0:T(8,128)(2,1)S(1)} collective-permute-done((bf16[256,3072]{1,0:T(8,128)(2,1)S(1)}, bf16[256,3072]{1,0:T(8,128)(2,1)S(1)}, u32[]{:S(2)}, u32[]{:S(2)}) %collective-permute-start.15) | collective-permute-done | bytes 1572896 | tf_op jit(solution)/shard_map/ppermute | solution.py:20
  147.4 1.8 collective-permute-start.26
  150.7 15.5 %collective-permute-done.24 = bf16[64,3072]{1,0:T(8,128)(2,1)S(1)} collective-permute-done((bf16[64,3072]{1,0:T(8,128)(2,1)S(1)}, bf16[64,3072]{1,0:T(8,128)(2,1)S(1)}, u32[]{:S(2)}, u32[]{:S(2)}) %collective-permute-start.24) | collective-permute-done | bytes 393248 | tf_op jit(solution)/shard_map/ppermute | solution.py:20
  167.4 9.0 %collective-permute-done.25 = bf16[64,3072]{1,0:T(8,128)(2,1)S(1)} collective-permute-done((bf16[64,3072]{1,0:T(8,128)(2,1)S(1)}, bf16[64,3072]{1,0:T(8,128)(2,1)S(1)}, u32[]{:S(2)}, u32[]{:S(2)}) %collective-permute-start.25) | collective-permute-done | bytes 393248 | tf_op jit(solution)/shard_map/ppermute | solution.py:20
  176.4 1.7 collective-permute-start.27
  178.9 15.0 %collective-permute-done.27 = bf16[128,3072]{1,0:T(8,128)(2,1)S(1)} collective-permute-done((bf16[128,3072]{1,0:T(8,128)(2,1)S(1)}, bf16[128,3072]{1,0:T(8,128)(2,1)S(1)}, u32[]{:S(2)}, u32[]{:S(2)}) %collective-permute-start.27) | collective-permute-done | bytes 786464 | tf_op jit(solution)/shard_map/ppermute | solution.py:20
  198.6 12.3 %collective-permute-done.28 = bf16[64,3072]{1,0:T(8,128)(2,1)S(1)} collective-permute-done((bf16[64,3072]{1,0:T(8,128)(2,1)S(1)}, bf16[64,3072]{1,0:T(8,128)(2,1)S(1)}, u32[]{:S(2)}, u32[]{:S(2)}) %collective-permute-start.28) | collective-permute-done | bytes 393248 | tf_op jit(solution)/shard_map/ppermute | solution.py:20
  210.8 2.6 %collective-permute-done.29 = bf16[64,3072]{1,0:T(8,128)(2,1)S(1)} collective-permute-done((bf16[64,3072]{1,0:T(8,128)(2,1)S(1)}, bf16[64,3072]{1,0:T(8,128)(2,1)S(1)}, u32[]{:S(2)}, u32[]{:S(2)}) %collective-permute-start.29) | collective-permute-done | bytes 393248 | tf_op jit(solution)/shard_map/ppermute | solution.py:20
  213.6 1.6 collective-permute-start.30
  215.2 7.1 %collective-permute-done.30 = bf16[64,3072]{1,0:T(8,128)(2,1)S(1)} collective-permute-done((bf16[64,3072]{1,0:T(8,128)(2,1)S(1)}, bf16[64,3072]{1,0:T(8,128)(2,1)S(1)}, u32[]{:S(2)}, u32[]{:S(2)}) %collective-permute-start.30) | collective-permute-done | bytes 393248 | tf_op jit(solution)/shard_map/ppermute | solution.py:16
  (68 shorter events, 23.6 us)
Async XLA Ops:
  0.0 17.1 %copy-start = (bf16[2,64,3072]{2,1,0:T(8,128)(2,1)S(1)}, bf16[2,64,3072]{2,1,0:T(8,128)(2,1)}, u32[]{:S(2)}) copy-start(bf16[2,64,3072]{2,1,0:T(8,128)(2,1)} %refs_0_.3) | copy-start | bytes 2359300
  2.5 5.7 %collective-permute-start.1 = (f32[8,64]{1,0:T(8,128)S(1)}, f32[8,64]{1,0:T(8,128)S(1)}, u32[]{:S(2)}, u32[]{:S(2)}) collective-permute-start(f32[8,64]{1,0:T(8,128)S(1)} %get-tuple-element.69), channel_id=1, source_target_pairs={{0,2},{1,3},{2,0},{3,1},{4,6},{5,7},{6,4},{7,5},{8,10},{9,11},{10,... | collective-permute-start | bytes 6152 | tf_op jit(solution)/shard_map/ppermute | solution.py:20
  6.6 3.6 %collective-permute-start = (f32[8,64]{1,0:T(8,128)S(1)}, f32[8,64]{1,0:T(8,128)S(1)}, u32[]{:S(2)}, u32[]{:S(2)}) collective-permute-start(f32[8,64]{1,0:T(8,128)S(1)} %get-tuple-element.69), channel_id=1, source_target_pairs={{0,1},{1,0},{2,3},{3,2},{4,5},{5,4},{6,7},{7,6},{8,9},{9,8},{10,11... | collective-permute-start | bytes 6152 | tf_op jit(solution)/shard_map/ppermute | solution.py:20
  8.2 5.4 %collective-permute-start.2 = (f32[8,64]{1,0:T(8,128)S(1)}, f32[8,64]{1,0:T(8,128)S(1)}, u32[]{:S(2)}, u32[]{:S(2)}) collective-permute-start(f32[8,64]{1,0:T(8,128)S(1)} %get-tuple-element.69), channel_id=1, source_target_pairs={{0,3},{1,2},{2,1},{3,0},{4,7},{5,6},{6,5},{7,4},{8,11},{9,10},{10,... | collective-permute-start | bytes 6152 | tf_op jit(solution)/shard_map/ppermute | solution.py:20
  13.6 27.6 %collective-permute-start.5 = (bf16[2,64,3072]{2,1,0:T(8,128)(2,1)}, bf16[2,64,3072]{2,1,0:T(8,128)(2,1)S(1)}, u32[]{:S(2)}, u32[]{:S(2)}) collective-permute-start(bf16[2,64,3072]{2,1,0:T(8,128)(2,1)} %refs_0_.3), channel_id=1, source_target_pairs={{0,1},{1,0},{2,3},{3,2},{4,5},{5,4},{6,7},{7,6},{8,9},{9,8},{10,11... | collective-permute-start | bytes 2359304 | tf_op jit(solution)/shard_map/ppermute | solution.py:20
  14.8 22.8 %collective-permute-start.6 = (bf16[64,3072]{1,0:T(8,128)(2,1)S(1)}, bf16[64,3072]{1,0:T(8,128)(2,1)}, u32[]{:S(2)}, u32[]{:S(2)}) collective-permute-start(bf16[64,3072]{1,0:T(8,128)(2,1)S(1)} %get-tuple-element.29), channel_id=1, source_target_pairs={{0,2},{1,3},{2,0},{3,1},{4,6},{5,7},{6,4},{7,5},{8,10},{9,11},{10,... | collective-permute-start | bytes 1179656 | tf_op jit(solution)/shard_map/ppermute | solution.py:20
  15.4 4.0 %collective-permute-start.3 = (f32[4,8,64]{2,1,0:T(8,128)S(1)}, f32[4,8,64]{2,1,0:T(8,128)S(1)}, u32[]{:S(2)}, u32[]{:S(2)}) collective-permute-start(f32[4,8,64]{2,1,0:T(8,128)S(1)} %get-tuple-element.67), channel_id=1, source_target_pairs={{0,8},{4,12},{8,0},{12,4},{1,9},{5,13},{9,1},{13,5},{2,10},{6,14},... | collective-permute-start | bytes 24584 | tf_op jit(solution)/shard_map/ppermute | solution.py:20
  17.1 51.5 %collective-permute-start.4 = (bf16[2,64,3072]{2,1,0:T(8,128)(2,1)S(1)}, bf16[2,64,3072]{2,1,0:T(8,128)(2,1)S(1)}, u32[]{:S(2)}, u32[]{:S(2)}) collective-permute-start(bf16[2,64,3072]{2,1,0:T(8,128)(2,1)S(1)} %copy-done), channel_id=1, source_target_pairs={{0,8},{4,12},{8,0},{12,4},{1,9},{5,13},{9,1},{13,5},{2,10},{6,14},... | collective-permute-start | bytes 2359304 | tf_op jit(solution)/shard_map/ppermute | solution.py:20
  37.6 18.9 %collective-permute-start.10 = (bf16[64,3072]{1,0:T(8,128)(2,1)S(1)}, bf16[64,3072]{1,0:T(8,128)(2,1)}, u32[]{:S(2)}, u32[]{:S(2)}) collective-permute-start(bf16[64,3072]{1,0:T(8,128)(2,1)S(1)} %get-tuple-element.31), channel_id=1, source_target_pairs={{0,2},{1,3},{2,0},{3,1},{4,6},{5,7},{6,4},{7,5},{8,10},{9,11},{10,... | collective-permute-start | bytes 1179656 | tf_op jit(solution)/shard_map/ppermute | solution.py:20
  41.2 16.3 %collective-permute-start.8 = (bf16[64,3072]{1,0:T(8,128)(2,1)}, bf16[64,3072]{1,0:T(8,128)(2,1)}, u32[]{:S(2)}, u32[]{:S(2)}) collective-permute-start(bf16[64,3072]{1,0:T(8,128)(2,1)} %collective-permute-done.6), channel_id=1, source_target_pairs={{0,1},{1,0},{2,3},{3,2},{4,5},{5,4},{6,7},{7,6},{8,9},{9,8},{10,11... | collective-permute-start | bytes 1179656 | tf_op jit(solution)/shard_map/ppermute | solution.py:20
  43.0 25.6 %collective-permute-start.7 = (bf16[128,3072]{1,0:T(8,128)(2,1)S(1)}, bf16[128,3072]{1,0:T(8,128)(2,1)S(1)}, u32[]{:S(2)}, u32[]{:S(2)}) collective-permute-start(bf16[128,3072]{1,0:T(8,128)(2,1)S(1)} %pad_maximum_fusion.2.refs_2_), channel_id=1, source_target_pairs={{0,8},{4,12},{8,0},{12,4},{1,9},{5,13},{9,1},{13,5},{2,10},{6,14},... | collective-permute-start | bytes 2359304 | tf_op jit(solution)/shard_map/ppermute | solution.py:20
  56.5 10.8 %collective-permute-start.11 = (bf16[64,3072]{1,0:T(8,128)(2,1)}, bf16[64,3072]{1,0:T(8,128)(2,1)}, u32[]{:S(2)}, u32[]{:S(2)}) collective-permute-start(bf16[64,3072]{1,0:T(8,128)(2,1)} %collective-permute-done.10), channel_id=1, source_target_pairs={{0,1},{1,0},{2,3},{3,2},{4,5},{5,4},{6,7},{7,6},{8,9},{9,8},{10,11... | collective-permute-start | bytes 1179656 | tf_op jit(solution)/shard_map/ppermute | solution.py:20
  57.5 11.1 %collective-permute-start.9 = (bf16[64,3072]{1,0:T(8,128)(2,1)}, bf16[64,3072]{1,0:T(8,128)(2,1)S(1)}, u32[]{:S(2)}, u32[]{:S(2)}) collective-permute-start(bf16[64,3072]{1,0:T(8,128)(2,1)} %collective-permute-done.8.refs_4_), channel_id=1, source_target_pairs={{0,8},{4,12},{8,0},{12,4},{1,9},{5,13},{9,1},{13,5},{2,10},{6,14},... | collective-permute-start | bytes 1179656 | tf_op jit(solution)/shard_map/ppermute | solution.py:20
  72.7 3.6 %collective-permute-start.12 = (bf16[272,3072]{1,0:T(8,128)(2,1)S(1)}, bf16[272,3072]{1,0:T(8,128)(2,1)S(1)}, u32[]{:S(2)}, u32[]{:S(2)}) collective-permute-start(bf16[272,3072]{1,0:T(8,128)(2,1)S(1)} %get-tuple-element.33), channel_id=1, source_target_pairs={{0,4},{4,0},{8,12},{12,8},{1,5},{5,1},{9,13},{13,9},{2,6},{6,2},{1... | collective-permute-start | bytes 5013512 | tf_op jit(solution)/shard_map/ppermute | solution.py:20
  72.8 28.4 %collective-permute-start.13 = (bf16[192,3072]{1,0:T(8,128)(2,1)S(1)}, bf16[192,3072]{1,0:T(8,128)(2,1)S(1)}, u32[]{:S(2)}, u32[]{:S(2)}) collective-permute-start(bf16[192,3072]{1,0:T(8,128)(2,1)S(1)} %pad_maximum_fusion.1.refs_6_.refs_2_), channel_id=1, source_target_pairs={{0,8},{4,12},{8,0},{12,4},{1,9},{5,13},{9,1},{13,5},{2,10},{6,14},... | collective-permute-start | bytes 3538952 | tf_op jit(solution)/shard_map/ppermute | solution.py:20
  101.2 3.6 %collective-permute-start.14 = (bf16[272,3072]{1,0:T(8,128)(2,1)S(1)}, bf16[272,3072]{1,0:T(8,128)(2,1)S(1)}, u32[]{:S(2)}, u32[]{:S(2)}) collective-permute-start(bf16[272,3072]{1,0:T(8,128)(2,1)S(1)} %get-tuple-element.36), channel_id=1, source_target_pairs={{0,4},{4,0},{8,12},{12,8},{1,5},{5,1},{9,13},{13,9},{2,6},{6,2},{1... | collective-permute-start | bytes 5013512 | tf_op jit(solution)/shard_map/ppermute | solution.py:20
  104.1 8.5 %collective-permute-start.19 = (bf16[272,3072]{1,0:T(8,128)(2,1)S(1)}, bf16[272,3072]{1,0:T(8,128)(2,1)S(1)}, u32[]{:S(2)}, u32[]{:S(2)}) collective-permute-start(bf16[272,3072]{1,0:T(8,128)(2,1)S(1)} %get-tuple-element.42), channel_id=1, source_target_pairs={{0,4},{4,0},{8,12},{12,8},{1,5},{5,1},{9,13},{13,9},{2,6},{6,2},{1... | collective-permute-start | bytes 5013512 | tf_op jit(solution)/shard_map/ppermute | solution.py:20
  110.8 36.5 %collective-permute-start.15 = (bf16[256,3072]{1,0:T(8,128)(2,1)S(1)}, bf16[256,3072]{1,0:T(8,128)(2,1)S(1)}, u32[]{:S(2)}, u32[]{:S(2)}) collective-permute-start(bf16[256,3072]{1,0:T(8,128)(2,1)S(1)} %get-tuple-element.40.refs_0_), channel_id=1, source_target_pairs={{0,8},{4,12},{8,0},{12,4},{1,9},{5,13},{9,1},{13,5},{2,10},{6,14},... | collective-permute-start | bytes 4718600 | tf_op jit(solution)/shard_map/ppermute | solution.py:20
  131.5 3.6 %collective-permute-start.20 = (bf16[80,3072]{1,0:T(8,128)(2,1)S(1)}, bf16[80,3072]{1,0:T(8,128)(2,1)S(1)}, u32[]{:S(2)}, u32[]{:S(2)}) collective-permute-start(bf16[80,3072]{1,0:T(8,128)(2,1)S(1)} %get-tuple-element.57), channel_id=1, source_target_pairs={{0,4},{4,0},{8,12},{12,8},{1,5},{5,1},{9,13},{13,9},{2,6},{6,2},{1... | collective-permute-start | bytes 1474568 | tf_op jit(solution)/shard_map/ppermute | solution.py:20
  131.6 3.5 %collective-permute-start.22 = (bf16[80,3072]{1,0:T(8,128)(2,1)S(1)}, bf16[80,3072]{1,0:T(8,128)(2,1)S(1)}, u32[]{:S(2)}, u32[]{:S(2)}) collective-permute-start(bf16[80,3072]{1,0:T(8,128)(2,1)S(1)} %get-tuple-element.58), channel_id=1, source_target_pairs={{0,4},{4,0},{8,12},{12,8},{1,5},{5,1},{9,13},{13,9},{2,6},{6,2},{1... | collective-permute-start | bytes 1474568 | tf_op jit(solution)/shard_map/ppermute | solution.py:20
  132.1 3.0 %collective-permute-start.21 = (bf16[80,3072]{1,0:T(8,128)(2,1)S(1)}, bf16[80,3072]{1,0:T(8,128)(2,1)S(1)}, u32[]{:S(2)}, u32[]{:S(2)}) collective-permute-start(bf16[80,3072]{1,0:T(8,128)(2,1)S(1)} %get-tuple-element.59), channel_id=1, source_target_pairs={{0,4},{4,0},{8,12},{12,8},{1,5},{5,1},{9,13},{13,9},{2,6},{6,2},{1... | collective-permute-start | bytes 1474568 | tf_op jit(solution)/shard_map/ppermute | solution.py:20
  132.2 2.9 %collective-permute-start.23 = (bf16[32,3072]{1,0:T(8,128)(2,1)S(1)}, bf16[32,3072]{1,0:T(8,128)(2,1)S(1)}, u32[]{:S(2)}, u32[]{:S(2)}) collective-permute-start(bf16[32,3072]{1,0:T(8,128)(2,1)S(1)} %slice.115), channel_id=1, source_target_pairs={{0,4},{4,0},{8,12},{12,8},{1,5},{5,1},{9,13},{13,9},{2,6},{6,2},{1... | collective-permute-start | bytes 589832 | tf_op jit(solution)/shard_map/ppermute | solution.py:20
  147.4 20.0 %collective-permute-start.26 = (bf16[64,3072]{1,0:T(8,128)(2,1)S(1)}, bf16[64,3072]{1,0:T(8,128)(2,1)S(1)}, u32[]{:S(2)}, u32[]{:S(2)}) collective-permute-start(bf16[64,3072]{1,0:T(8,128)(2,1)S(1)} %get-tuple-element.60), channel_id=1, source_target_pairs={{0,8},{4,12},{8,0},{12,4},{1,9},{5,13},{9,1},{13,5},{2,10},{6,14},... | collective-permute-start | bytes 1179656 | tf_op jit(solution)/shard_map/ppermute | solution.py:20
  149.2 17.0 %collective-permute-start.24 = (bf16[64,3072]{1,0:T(8,128)(2,1)S(1)}, bf16[64,3072]{1,0:T(8,128)(2,1)S(1)}, u32[]{:S(2)}, u32[]{:S(2)}) collective-permute-start(bf16[64,3072]{1,0:T(8,128)(2,1)S(1)} %get-tuple-element.61), channel_id=1, source_target_pairs={{0,8},{4,12},{8,0},{12,4},{1,9},{5,13},{9,1},{13,5},{2,10},{6,14},... | collective-permute-start | bytes 1179656 | tf_op jit(solution)/shard_map/ppermute | solution.py:20
  149.6 28.4 %collective-permute-start.16 = (bf16[128,3072]{1,0:T(8,128)(2,1)S(1)}, bf16[128,3072]{1,0:T(8,128)(2,1)S(1)}, u32[]{:S(2)}, u32[]{:S(2)}) collective-permute-start(bf16[128,3072]{1,0:T(8,128)(2,1)S(1)} %add_convert_fusion), channel_id=1, source_target_pairs={{0,1},{1,0},{2,3},{3,2},{4,5},{5,4},{6,7},{7,6},{8,9},{9,8},{10,11... | collective-permute-start | bytes 2359304 | tf_op jit(solution)/shard_map/ppermute | solution.py:20
  166.3 10.1 %collective-permute-start.25 = (bf16[64,3072]{1,0:T(8,128)(2,1)S(1)}, bf16[64,3072]{1,0:T(8,128)(2,1)S(1)}, u32[]{:S(2)}, u32[]{:S(2)}) collective-permute-start(bf16[64,3072]{1,0:T(8,128)(2,1)S(1)} %add_convert_fusion.4), channel_id=1, source_target_pairs={{0,1},{1,0},{2,3},{3,2},{4,5},{5,4},{6,7},{7,6},{8,9},{9,8},{10,11... | collective-permute-start | bytes 1179656 | tf_op jit(solution)/shard_map/ppermute | solution.py:20
  176.4 17.5 %collective-permute-start.27 = (bf16[128,3072]{1,0:T(8,128)(2,1)S(1)}, bf16[128,3072]{1,0:T(8,128)(2,1)S(1)}, u32[]{:S(2)}, u32[]{:S(2)}) collective-permute-start(bf16[128,3072]{1,0:T(8,128)(2,1)S(1)} %slice.117), channel_id=1, source_target_pairs={{0,8},{4,12},{8,0},{12,4},{1,9},{5,13},{9,1},{13,5},{2,10},{6,14},... | collective-permute-start | bytes 2359304 | tf_op jit(solution)/shard_map/ppermute | solution.py:20
  178.4 18.5 %collective-permute-start.17 = (bf16[64,3072]{1,0:T(8,128)(2,1)S(1)}, bf16[64,3072]{1,0:T(8,128)(2,1)S(1)}, u32[]{:S(2)}, u32[]{:S(2)}) collective-permute-start(bf16[64,3072]{1,0:T(8,128)(2,1)S(1)} %slice.161), channel_id=1, source_target_pairs={{0,2},{1,3},{2,0},{3,1},{4,6},{5,7},{6,4},{7,5},{8,10},{9,11},{10,... | collective-permute-start | bytes 1179656 | tf_op jit(solution)/shard_map/ppermute | solution.py:20
  194.1 16.7 %collective-permute-start.28 = (bf16[64,3072]{1,0:T(8,128)(2,1)S(1)}, bf16[64,3072]{1,0:T(8,128)(2,1)S(1)}, u32[]{:S(2)}, u32[]{:S(2)}) collective-permute-start(bf16[64,3072]{1,0:T(8,128)(2,1)S(1)} %get-tuple-element.55), channel_id=1, source_target_pairs={{0,1},{1,0},{2,3},{3,2},{4,5},{5,4},{6,7},{7,6},{8,9},{9,8},{10,11... | collective-permute-start | bytes 1179656 | tf_op jit(solution)/shard_map/ppermute | solution.py:20
  195.1 18.3 %collective-permute-start.29 = (bf16[64,3072]{1,0:T(8,128)(2,1)S(1)}, bf16[64,3072]{1,0:T(8,128)(2,1)S(1)}, u32[]{:S(2)}, u32[]{:S(2)}) collective-permute-start(bf16[64,3072]{1,0:T(8,128)(2,1)S(1)} %get-tuple-element.56), channel_id=1, source_target_pairs={{0,2},{1,3},{2,0},{3,1},{4,6},{5,7},{6,4},{7,5},{8,10},{9,11},{10,... | collective-permute-start | bytes 1179656 | tf_op jit(solution)/shard_map/ppermute | solution.py:20
  197.0 18.2 %collective-permute-start.18 = (bf16[64,3072]{1,0:T(8,128)(2,1)S(1)}, bf16[64,3072]{1,0:T(8,128)(2,1)S(1)}, u32[]{:S(2)}, u32[]{:S(2)}) collective-permute-start(bf16[64,3072]{1,0:T(8,128)(2,1)S(1)} %fusion), channel_id=1, source_target_pairs={{16,0},{0,16},{17,1},{1,17},{18,2},{2,18},{19,3},{3,19},{20,4},{4,... | collective-permute-start | bytes 1179656 | tf_op jit(solution)/shard_map/ppermute | solution.py:16
  213.6 8.7 %collective-permute-start.30 = (bf16[64,3072]{1,0:T(8,128)(2,1)S(1)}, bf16[64,3072]{1,0:T(8,128)(2,1)S(1)}, u32[]{:S(2)}, u32[]{:S(2)}) collective-permute-start(bf16[64,3072]{1,0:T(8,128)(2,1)S(1)} %add_convert_fusion.1), channel_id=1, source_target_pairs={{16,0},{0,16},{17,1},{1,17},{18,2},{2,18},{19,3},{3,19},{20,4},{4,... | collective-permute-start | bytes 1179656 | tf_op jit(solution)/shard_map/ppermute | solution.py:16

commit v4 on v3

--- a/solution.py
+++ b/solution.py
@@ -123,7 +123,7 @@
 def expert_share(mine, other, up_rows, down_rows, *earlier):
     half, features = mine.shape
     units = up_rows.shape[0]
-    steps = 4
+    steps = 2
     chunk, width = units // steps, features // steps
     shape = jax.ShapeDtypeStruct((half, features), BF16)
     whole = pl.BlockSpec((half, features), lambda i: (0, 0))
@@ -146,7 +146,7 @@
             bytes_accessed=4 * units * features + 8 * half * features,
             transcendentals=2 * half * units,
         ),
-        compiler_params=pltpu.CompilerParams(vmem_limit_bytes=40 * 2**20),
+        compiler_params=pltpu.CompilerParams(vmem_limit_bytes=52 * 2**20),
     )(mine, other, up_rows, down_rows, *earlier)
 
 

time: 224 us -> 225 us (level)
  waiting for transfers between devices: 123 us -> 113 us
  local copies, waits for them, and re-layouts: 3.71 us -> 9.56 us
  Pallas kernels: 58.7 us -> 63.8 us
    ppermute x29, waiting for transfers between devices: 116 us -> 106 us  [swapped(): lax.ppermute(block, axis, [(i, i ^ bits) for i in range(lax.axis_size(axi...]
    pallas_call x2, Pallas kernels: 37.6 us -> 42.7 us  [expert_share(): pl.pallas_call(functools.partial(expert_kernel, steps, half), grid=(2 * s...]
    unnamed x2 -> x22, local copies, waits for them, and re-layouts: 0.01 us -> 3.62 us
  transfers between devices with their start and end apart: 31 -> 31, of which waited for: 19 -> 19; matrix products, arithmetic and copies ran while one was open for 3% -> 4% of each run, Pallas kernels for 24% -> 27%
where the time goes in v4:
time: 225 us
  waiting for transfers between devices  113 us (50%)
  Pallas kernels  63.8 us (28%)
  starting transfers between devices  32.4 us (14%)
  local copies, waits for them, and re-layouts  9.56 us (4%)
  other arithmetic  5.49 us (2%)
    ppermute x29, waiting for transfers between devices, swapped(): lax.ppermute(block, axis, [(i, i ^ bits) for i in range(lax.axis_size(axi...  106 us
    pallas_call x2, Pallas kernels, expert_share(): pl.pallas_call(functools.partial(expert_kernel, steps, half), grid=(2 * s...  42.7 us
    ppermute x29, starting transfers between devices, swapped(): lax.ppermute(block, axis, [(i, i ^ bits) for i in range(lax.axis_size(axi...  29.2 us
    pallas_call x2, Pallas kernels, unpack(): pl.pallas_call(functools.partial(unpack_kernel, stays, len(earlier)), gri...  12.1 us
    ppermute x2, waiting for transfers between devices, passed_along(): return lax.ppermute(block, axis, route)  7.13 us
    pallas_call x2, Pallas kernels, pack(): pl.pallas_call(functools.partial(pack_kernel, len(blocks), half), grid=(f...  7.02 us
  transfers between devices with their start and end apart: 31, of which 19 were waited for; matrix products, arithmetic and copies ran while one was open for 4% of the time, Pallas kernels for 27%

profile of v4, /device:TPU:0, one launch (start us, length us, event | category | flops | bytes accessed | tf_op | source)
XLA Modules:
  0.0 224.7 jit_solution(3094696810949251946)
XLA Ops:
  2.5 4.1 %collective-permute-start.1 = (f32[8,64]{1,0:T(8,128)S(1)}, f32[8,64]{1,0:T(8,128)S(1)}, u32[]{:S(2)}, u32[]{:S(2)}) collective-permute-start(f32[8,64]{1,0:T(8,128)S(1)} %get-tuple-element.69), channel_id=1, source_target_pairs={{0,2},{1,3},{2,0},{3,1},{4,6},{5,7},{6,4},{7,5},{8,10},{9,11},{10,... | collective-permute-start | bytes 6152 | tf_op jit(solution)/shard_map/ppermute | solution.py:20
  6.6 1.6 collective-permute-start
  8.2 2.0 collective-permute-done
  10.2 3.4 %collective-permute-done.2 = f32[8,64]{1,0:T(8,128)S(1)} collective-permute-done((f32[8,64]{1,0:T(8,128)S(1)}, f32[8,64]{1,0:T(8,128)S(1)}, u32[]{:S(2)}, u32[]{:S(2)}) %collective-permute-start.2) | collective-permute-done | bytes 2080 | tf_op jit(solution)/shard_map/ppermute | solution.py:20
  15.4 1.7 collective-permute-start.3
  17.4 1.9 collective-permute-done.3
  19.4 18.2 %collective-permute-done.6 = bf16[64,3072]{1,0:T(8,128)(2,1)} collective-permute-done((bf16[64,3072]{1,0:T(8,128)(2,1)S(1)}, bf16[64,3072]{1,0:T(8,128)(2,1)}, u32[]{:S(2)}, u32[]{:S(2)}) %collective-permute-start.6) | collective-permute-done | bytes 393248 | tf_op jit(solution)/shard_map/ppermute | solution.py:20
  37.6 3.6 %collective-permute-start.10 = (bf16[64,3072]{1,0:T(8,128)(2,1)S(1)}, bf16[64,3072]{1,0:T(8,128)(2,1)}, u32[]{:S(2)}, u32[]{:S(2)}) collective-permute-start(bf16[64,3072]{1,0:T(8,128)(2,1)S(1)} %get-tuple-element.31), channel_id=1, source_target_pairs={{0,2},{1,3},{2,0},{3,1},{4,6},{5,7},{6,4},{7,5},{8,10},{9,11},{10,... | collective-permute-start | bytes 1179656 | tf_op jit(solution)/shard_map/ppermute | solution.py:20
  44.6 11.9 %collective-permute-done.10 = bf16[64,3072]{1,0:T(8,128)(2,1)} collective-permute-done((bf16[64,3072]{1,0:T(8,128)(2,1)S(1)}, bf16[64,3072]{1,0:T(8,128)(2,1)}, u32[]{:S(2)}, u32[]{:S(2)}) %collective-permute-start.10) | collective-permute-done | bytes 393248 | tf_op jit(solution)/shard_map/ppermute | solution.py:20
  57.5 1.7 collective-permute-start.9
  59.3 2.0 shard_map.64
  61.3 6.0 %collective-permute-done.11 = bf16[64,3072]{1,0:T(8,128)(2,1)} collective-permute-done((bf16[64,3072]{1,0:T(8,128)(2,1)}, bf16[64,3072]{1,0:T(8,128)(2,1)}, u32[]{:S(2)}, u32[]{:S(2)}) %collective-permute-start.11) | collective-permute-done | bytes 393248 | tf_op jit(solution)/shard_map/ppermute | solution.py:20
  68.6 4.1 %shard_map.65 = (bf16[272,3072]{1,0:T(8,128)(2,1)S(1)}, bf16[272,3072]{1,0:T(8,128)(2,1)S(1)}) custom-call(bf16[2,544,512]{2,1,0:T(8,128)(2,1)S(1)} %get-tuple-element.27.pick_ref, bf16[2,64,3072]{2,1,0:T(8,128)(2,1)S(1)} %copy-done, bf16[2,64,3072]{2,1,0:T(8,128)(2,1)S(1)} %collective-permute-done.4.refs_1_, ...), custom_call_target="tpu_custom_call" | custom-call | flops 1711276032 | bytes 7045120 | tf_op jit(solution)/shard_map/pallas_call | solution.py:175
  74.0 1.7 collective-permute-start.13
  75.7 1.8 collective-permute-done.12.other_ref
  78.7 21.3 %shard_map.66 = (bf16[272,3072]{1,0:T(8,128)(2,1)S(1)}, bf16[272,3072]{1,0:T(8,128)(2,1)}) custom-call(bf16[272,3072]{1,0:T(8,128)(2,1)} %copy-done.7, bf16[272,3072]{1,0:T(8,128)(2,1)} %copy-done.10, bf16[2048,3072]{1,0:T(8,128)(2,1)} %bitcast.62, bf16[2048,3072]{1,0:T(8,128)(2,1)} %bitcast.64), custom_call_target="tpu_custom_call" | custom-call | flops 13690208256 | bytes 31850496 | tf_op jit(solution)/shard_map/pallas_call | solution.py:131
  100.0 2.4 %collective-permute-done.13.refs_3_ = bf16[192,3072]{1,0:T(8,128)(2,1)S(1)} collective-permute-done((bf16[192,3072]{1,0:T(8,128)(2,1)S(1)}, bf16[192,3072]{1,0:T(8,128)(2,1)S(1)}, u32[]{:S(2)}, u32[]{:S(2)}) %collective-permute-start.13) | collective-permute-done | bytes 1179680 | tf_op jit(solution)/shard_map/ppermute | solution.py:20
  102.4 2.9 %shard_map.68 = (bf16[272,3072]{1,0:T(8,128)(2,1)S(1)}, bf16[272,3072]{1,0:T(8,128)(2,1)S(1)}) custom-call(bf16[2,544,512]{2,1,0:T(8,128)(2,1)S(1)} %get-tuple-element.27.pick_ref, bf16[2,64,3072]{2,1,0:T(8,128)(2,1)S(1)} %copy-done, bf16[2,64,3072]{2,1,0:T(8,128)(2,1)S(1)} %collective-permute-done.4.refs_1_, ...), custom_call_target="tpu_custom_call" | custom-call | flops 1711276032 | bytes 7045120 | tf_op jit(solution)/shard_map/pallas_call | solution.py:175
  106.1 6.1 %shard_map.67 = (f32[256,3072]{1,0:T(8,128)S(1)}, bf16[256,3072]{1,0:T(8,128)(2,1)S(1)}) custom-call(bf16[272,3072]{1,0:T(8,128)(2,1)S(1)} %get-tuple-element.34.mine_ref.refs_4_, bf16[272,3072]{1,0:T(8,128)(2,1)S(1)} %collective-permute-done.14.other_ref, bf16[2,512,544]{2,1,0:T(8,128)(2,1)S(1)} %copy-done.3, bf16[2,512,544]{2,1,0:T(8,128)(2,1)S(1)} %copy-done.5), custom_call_target="tpu_custom_call" | custom-call | flops 3422552064 | bytes 10747904 | tf_op jit(solution)/shard_map/pallas_call | solution.py:217
  112.2 1.8 collective-permute-start.15
  115.2 21.4 %shard_map.69 = (bf16[272,3072]{1,0:T(8,128)(2,1)}, bf16[272,3072]{1,0:T(8,128)(2,1)}) custom-call(bf16[272,3072]{1,0:T(8,128)(2,1)} %copy-done.1, bf16[272,3072]{1,0:T(8,128)(2,1)} %copy-done.9, bf16[2048,3072]{1,0:T(8,128)(2,1)} %bitcast.63, bf16[2048,3072]{1,0:T(8,128)(2,1)} %bitcast.65, bf16[256,3072]{1,0:T(8,128)(2,1)S(1)} %get-tuple-element.40.refs_0_), custom_call_target="tpu_custom_call" | custom-call | flops 13690208256 | bytes 31850496 | tf_op jit(solution)/shard_map/pallas_call | solution.py:131
  141.8 6.1 %shard_map.70 = (f32[256,3072]{1,0:T(8,128)S(1)}, bf16[256,3072]{1,0:T(8,128)(2,1)S(1)}) custom-call(bf16[272,3072]{1,0:T(8,128)(2,1)S(1)} %copy-done.8, bf16[272,3072]{1,0:T(8,128)(2,1)S(1)} %pad_maximum_fusion.other_ref, bf16[2,512,544]{2,1,0:T(8,128)(2,1)S(1)} %copy-done.3, bf16[2,512,544]{2,1,0:T(8,128)(2,1)S(1)} %copy-done.6), custom_call_target="tpu_custom_call" | custom-call | flops 3422552064 | bytes 10747904 | tf_op jit(solution)/shard_map/pallas_call | solution.py:217
  148.8 1.8 collective-permute-start.26
  152.1 15.5 %collective-permute-done.24 = bf16[64,3072]{1,0:T(8,128)(2,1)S(1)} collective-permute-done((bf16[64,3072]{1,0:T(8,128)(2,1)S(1)}, bf16[64,3072]{1,0:T(8,128)(2,1)S(1)}, u32[]{:S(2)}, u32[]{:S(2)}) %collective-permute-start.24) | collective-permute-done | bytes 393248 | tf_op jit(solution)/shard_map/ppermute | solution.py:20
  168.8 8.9 %collective-permute-done.25 = bf16[64,3072]{1,0:T(8,128)(2,1)S(1)} collective-permute-done((bf16[64,3072]{1,0:T(8,128)(2,1)S(1)}, bf16[64,3072]{1,0:T(8,128)(2,1)S(1)}, u32[]{:S(2)}, u32[]{:S(2)}) %collective-permute-start.25) | collective-permute-done | bytes 393248 | tf_op jit(solution)/shard_map/ppermute | solution.py:20
  177.8 1.7 collective-permute-start.27
  180.3 15.0 %collective-permute-done.27 = bf16[128,3072]{1,0:T(8,128)(2,1)S(1)} collective-permute-done((bf16[128,3072]{1,0:T(8,128)(2,1)S(1)}, bf16[128,3072]{1,0:T(8,128)(2,1)S(1)}, u32[]{:S(2)}, u32[]{:S(2)}) %collective-permute-start.27) | collective-permute-done | bytes 786464 | tf_op jit(solution)/shard_map/ppermute | solution.py:20
  198.4 1.6 collective-permute-start.18
  199.9 12.2 %collective-permute-done.28 = bf16[64,3072]{1,0:T(8,128)(2,1)S(1)} collective-permute-done((bf16[64,3072]{1,0:T(8,128)(2,1)S(1)}, bf16[64,3072]{1,0:T(8,128)(2,1)S(1)}, u32[]{:S(2)}, u32[]{:S(2)}) %collective-permute-start.28) | collective-permute-done | bytes 393248 | tf_op jit(solution)/shard_map/ppermute | solution.py:20
  212.2 2.6 %collective-permute-done.29 = bf16[64,3072]{1,0:T(8,128)(2,1)S(1)} collective-permute-done((bf16[64,3072]{1,0:T(8,128)(2,1)S(1)}, bf16[64,3072]{1,0:T(8,128)(2,1)S(1)}, u32[]{:S(2)}, u32[]{:S(2)}) %collective-permute-start.29) | collective-permute-done | bytes 393248 | tf_op jit(solution)/shard_map/ppermute | solution.py:20
  215.0 1.6 collective-permute-start.30
  216.6 7.1 %collective-permute-done.30 = bf16[64,3072]{1,0:T(8,128)(2,1)S(1)} collective-permute-done((bf16[64,3072]{1,0:T(8,128)(2,1)S(1)}, bf16[64,3072]{1,0:T(8,128)(2,1)S(1)}, u32[]{:S(2)}, u32[]{:S(2)}) %collective-permute-start.30) | collective-permute-done | bytes 393248 | tf_op jit(solution)/shard_map/ppermute | solution.py:16
  (88 shorter events, 28.8 us)
Async XLA Ops:
  0.0 17.1 %copy-start = (bf16[2,64,3072]{2,1,0:T(8,128)(2,1)S(1)}, bf16[2,64,3072]{2,1,0:T(8,128)(2,1)}, u32[]{:S(2)}) copy-start(bf16[2,64,3072]{2,1,0:T(8,128)(2,1)} %refs_0_.3) | copy-start | bytes 2359300
  2.5 5.7 %collective-permute-start.1 = (f32[8,64]{1,0:T(8,128)S(1)}, f32[8,64]{1,0:T(8,128)S(1)}, u32[]{:S(2)}, u32[]{:S(2)}) collective-permute-start(f32[8,64]{1,0:T(8,128)S(1)} %get-tuple-element.69), channel_id=1, source_target_pairs={{0,2},{1,3},{2,0},{3,1},{4,6},{5,7},{6,4},{7,5},{8,10},{9,11},{10,... | collective-permute-start | bytes 6152 | tf_op jit(solution)/shard_map/ppermute | solution.py:20
  6.6 3.6 %collective-permute-start = (f32[8,64]{1,0:T(8,128)S(1)}, f32[8,64]{1,0:T(8,128)S(1)}, u32[]{:S(2)}, u32[]{:S(2)}) collective-permute-start(f32[8,64]{1,0:T(8,128)S(1)} %get-tuple-element.69), channel_id=1, source_target_pairs={{0,1},{1,0},{2,3},{3,2},{4,5},{5,4},{6,7},{7,6},{8,9},{9,8},{10,11... | collective-permute-start | bytes 6152 | tf_op jit(solution)/shard_map/ppermute | solution.py:20
  8.2 5.4 %collective-permute-start.2 = (f32[8,64]{1,0:T(8,128)S(1)}, f32[8,64]{1,0:T(8,128)S(1)}, u32[]{:S(2)}, u32[]{:S(2)}) collective-permute-start(f32[8,64]{1,0:T(8,128)S(1)} %get-tuple-element.69), channel_id=1, source_target_pairs={{0,3},{1,2},{2,1},{3,0},{4,7},{5,6},{6,5},{7,4},{8,11},{9,10},{10,... | collective-permute-start | bytes 6152 | tf_op jit(solution)/shard_map/ppermute | solution.py:20
  13.6 27.6 %collective-permute-start.5 = (bf16[2,64,3072]{2,1,0:T(8,128)(2,1)}, bf16[2,64,3072]{2,1,0:T(8,128)(2,1)S(1)}, u32[]{:S(2)}, u32[]{:S(2)}) collective-permute-start(bf16[2,64,3072]{2,1,0:T(8,128)(2,1)} %refs_0_.3), channel_id=1, source_target_pairs={{0,1},{1,0},{2,3},{3,2},{4,5},{5,4},{6,7},{7,6},{8,9},{9,8},{10,11... | collective-permute-start | bytes 2359304 | tf_op jit(solution)/shard_map/ppermute | solution.py:20
  14.8 22.8 %collective-permute-start.6 = (bf16[64,3072]{1,0:T(8,128)(2,1)S(1)}, bf16[64,3072]{1,0:T(8,128)(2,1)}, u32[]{:S(2)}, u32[]{:S(2)}) collective-permute-start(bf16[64,3072]{1,0:T(8,128)(2,1)S(1)} %get-tuple-element.29), channel_id=1, source_target_pairs={{0,2},{1,3},{2,0},{3,1},{4,6},{5,7},{6,4},{7,5},{8,10},{9,11},{10,... | collective-permute-start | bytes 1179656 | tf_op jit(solution)/shard_map/ppermute | solution.py:20
  15.4 4.0 %collective-permute-start.3 = (f32[4,8,64]{2,1,0:T(8,128)S(1)}, f32[4,8,64]{2,1,0:T(8,128)S(1)}, u32[]{:S(2)}, u32[]{:S(2)}) collective-permute-start(f32[4,8,64]{2,1,0:T(8,128)S(1)} %get-tuple-element.67), channel_id=1, source_target_pairs={{0,8},{4,12},{8,0},{12,4},{1,9},{5,13},{9,1},{13,5},{2,10},{6,14},... | collective-permute-start | bytes 24584 | tf_op jit(solution)/shard_map/ppermute | solution.py:20
  17.1 51.5 %collective-permute-start.4 = (bf16[2,64,3072]{2,1,0:T(8,128)(2,1)S(1)}, bf16[2,64,3072]{2,1,0:T(8,128)(2,1)S(1)}, u32[]{:S(2)}, u32[]{:S(2)}) collective-permute-start(bf16[2,64,3072]{2,1,0:T(8,128)(2,1)S(1)} %copy-done), channel_id=1, source_target_pairs={{0,8},{4,12},{8,0},{12,4},{1,9},{5,13},{9,1},{13,5},{2,10},{6,14},... | collective-permute-start | bytes 2359304 | tf_op jit(solution)/shard_map/ppermute | solution.py:20
  37.6 18.9 %collective-permute-start.10 = (bf16[64,3072]{1,0:T(8,128)(2,1)S(1)}, bf16[64,3072]{1,0:T(8,128)(2,1)}, u32[]{:S(2)}, u32[]{:S(2)}) collective-permute-start(bf16[64,3072]{1,0:T(8,128)(2,1)S(1)} %get-tuple-element.31), channel_id=1, source_target_pairs={{0,2},{1,3},{2,0},{3,1},{4,6},{5,7},{6,4},{7,5},{8,10},{9,11},{10,... | collective-permute-start | bytes 1179656 | tf_op jit(solution)/shard_map/ppermute | solution.py:20
  41.2 16.3 %collective-permute-start.8 = (bf16[64,3072]{1,0:T(8,128)(2,1)}, bf16[64,3072]{1,0:T(8,128)(2,1)}, u32[]{:S(2)}, u32[]{:S(2)}) collective-permute-start(bf16[64,3072]{1,0:T(8,128)(2,1)} %collective-permute-done.6), channel_id=1, source_target_pairs={{0,1},{1,0},{2,3},{3,2},{4,5},{5,4},{6,7},{7,6},{8,9},{9,8},{10,11... | collective-permute-start | bytes 1179656 | tf_op jit(solution)/shard_map/ppermute | solution.py:20
  43.0 25.6 %collective-permute-start.7 = (bf16[128,3072]{1,0:T(8,128)(2,1)S(1)}, bf16[128,3072]{1,0:T(8,128)(2,1)S(1)}, u32[]{:S(2)}, u32[]{:S(2)}) collective-permute-start(bf16[128,3072]{1,0:T(8,128)(2,1)S(1)} %pad_maximum_fusion.2.refs_2_), channel_id=1, source_target_pairs={{0,8},{4,12},{8,0},{12,4},{1,9},{5,13},{9,1},{13,5},{2,10},{6,14},... | collective-permute-start | bytes 2359304 | tf_op jit(solution)/shard_map/ppermute | solution.py:20
  56.5 10.8 %collective-permute-start.11 = (bf16[64,3072]{1,0:T(8,128)(2,1)}, bf16[64,3072]{1,0:T(8,128)(2,1)}, u32[]{:S(2)}, u32[]{:S(2)}) collective-permute-start(bf16[64,3072]{1,0:T(8,128)(2,1)} %collective-permute-done.10), channel_id=1, source_target_pairs={{0,1},{1,0},{2,3},{3,2},{4,5},{5,4},{6,7},{7,6},{8,9},{9,8},{10,11... | collective-permute-start | bytes 1179656 | tf_op jit(solution)/shard_map/ppermute | solution.py:20
  57.5 11.1 %collective-permute-start.9 = (bf16[64,3072]{1,0:T(8,128)(2,1)}, bf16[64,3072]{1,0:T(8,128)(2,1)S(1)}, u32[]{:S(2)}, u32[]{:S(2)}) collective-permute-start(bf16[64,3072]{1,0:T(8,128)(2,1)} %collective-permute-done.8.refs_4_), channel_id=1, source_target_pairs={{0,8},{4,12},{8,0},{12,4},{1,9},{5,13},{9,1},{13,5},{2,10},{6,14},... | collective-permute-start | bytes 1179656 | tf_op jit(solution)/shard_map/ppermute | solution.py:20
  74.0 3.6 %collective-permute-start.12 = (bf16[272,3072]{1,0:T(8,128)(2,1)S(1)}, bf16[272,3072]{1,0:T(8,128)(2,1)S(1)}, u32[]{:S(2)}, u32[]{:S(2)}) collective-permute-start(bf16[272,3072]{1,0:T(8,128)(2,1)S(1)} %get-tuple-element.33), channel_id=1, source_target_pairs={{0,4},{4,0},{8,12},{12,8},{1,5},{5,1},{9,13},{13,9},{2,6},{6,2},{1... | collective-permute-start | bytes 5013512 | tf_op jit(solution)/shard_map/ppermute | solution.py:20
  74.0 28.4 %collective-permute-start.13 = (bf16[192,3072]{1,0:T(8,128)(2,1)S(1)}, bf16[192,3072]{1,0:T(8,128)(2,1)S(1)}, u32[]{:S(2)}, u32[]{:S(2)}) collective-permute-start(bf16[192,3072]{1,0:T(8,128)(2,1)S(1)} %pad_maximum_fusion.1.refs_6_.refs_2_), channel_id=1, source_target_pairs={{0,8},{4,12},{8,0},{12,4},{1,9},{5,13},{9,1},{13,5},{2,10},{6,14},... | collective-permute-start | bytes 3538952 | tf_op jit(solution)/shard_map/ppermute | solution.py:20
  102.4 3.8 %collective-permute-start.14 = (bf16[272,3072]{1,0:T(8,128)(2,1)}, bf16[272,3072]{1,0:T(8,128)(2,1)S(1)}, u32[]{:S(2)}, u32[]{:S(2)}) collective-permute-start(bf16[272,3072]{1,0:T(8,128)(2,1)} %get-tuple-element.36), channel_id=1, source_target_pairs={{0,4},{4,0},{8,12},{12,8},{1,5},{5,1},{9,13},{13,9},{2,6},{6,2},{1... | collective-permute-start | bytes 5013512 | tf_op jit(solution)/shard_map/ppermute | solution.py:20
  105.3 8.7 %collective-permute-start.19 = (bf16[272,3072]{1,0:T(8,128)(2,1)S(1)}, bf16[272,3072]{1,0:T(8,128)(2,1)S(1)}, u32[]{:S(2)}, u32[]{:S(2)}) collective-permute-start(bf16[272,3072]{1,0:T(8,128)(2,1)S(1)} %get-tuple-element.42), channel_id=1, source_target_pairs={{0,4},{4,0},{8,12},{12,8},{1,5},{5,1},{9,13},{13,9},{2,6},{6,2},{1... | collective-permute-start | bytes 5013512 | tf_op jit(solution)/shard_map/ppermute | solution.py:20
  112.2 36.5 %collective-permute-start.15 = (bf16[256,3072]{1,0:T(8,128)(2,1)S(1)}, bf16[256,3072]{1,0:T(8,128)(2,1)S(1)}, u32[]{:S(2)}, u32[]{:S(2)}) collective-permute-start(bf16[256,3072]{1,0:T(8,128)(2,1)S(1)} %get-tuple-element.40.refs_0_), channel_id=1, source_target_pairs={{0,8},{4,12},{8,0},{12,4},{1,9},{5,13},{9,1},{13,5},{2,10},{6,14},... | collective-permute-start | bytes 4718600 | tf_op jit(solution)/shard_map/ppermute | solution.py:20
  138.0 3.6 %collective-permute-start.20 = (bf16[80,3072]{1,0:T(8,128)(2,1)S(1)}, bf16[80,3072]{1,0:T(8,128)(2,1)S(1)}, u32[]{:S(2)}, u32[]{:S(2)}) collective-permute-start(bf16[80,3072]{1,0:T(8,128)(2,1)S(1)} %get-tuple-element.57), channel_id=1, source_target_pairs={{0,4},{4,0},{8,12},{12,8},{1,5},{5,1},{9,13},{13,9},{2,6},{6,2},{1... | collective-permute-start | bytes 1474568 | tf_op jit(solution)/shard_map/ppermute | solution.py:20
  138.1 3.5 %collective-permute-start.22 = (bf16[80,3072]{1,0:T(8,128)(2,1)S(1)}, bf16[80,3072]{1,0:T(8,128)(2,1)S(1)}, u32[]{:S(2)}, u32[]{:S(2)}) collective-permute-start(bf16[80,3072]{1,0:T(8,128)(2,1)S(1)} %get-tuple-element.58), channel_id=1, source_target_pairs={{0,4},{4,0},{8,12},{12,8},{1,5},{5,1},{9,13},{13,9},{2,6},{6,2},{1... | collective-permute-start | bytes 1474568 | tf_op jit(solution)/shard_map/ppermute | solution.py:20
  138.6 3.0 %collective-permute-start.21 = (bf16[80,3072]{1,0:T(8,128)(2,1)S(1)}, bf16[80,3072]{1,0:T(8,128)(2,1)S(1)}, u32[]{:S(2)}, u32[]{:S(2)}) collective-permute-start(bf16[80,3072]{1,0:T(8,128)(2,1)S(1)} %get-tuple-element.59), channel_id=1, source_target_pairs={{0,4},{4,0},{8,12},{12,8},{1,5},{5,1},{9,13},{13,9},{2,6},{6,2},{1... | collective-permute-start | bytes 1474568 | tf_op jit(solution)/shard_map/ppermute | solution.py:20
  139.7 2.0 collective-permute-start.23
  148.8 20.0 %collective-permute-start.26 = (bf16[64,3072]{1,0:T(8,128)(2,1)S(1)}, bf16[64,3072]{1,0:T(8,128)(2,1)S(1)}, u32[]{:S(2)}, u32[]{:S(2)}) collective-permute-start(bf16[64,3072]{1,0:T(8,128)(2,1)S(1)} %get-tuple-element.60), channel_id=1, source_target_pairs={{0,8},{4,12},{8,0},{12,4},{1,9},{5,13},{9,1},{13,5},{2,10},{6,14},... | collective-permute-start | bytes 1179656 | tf_op jit(solution)/shard_map/ppermute | solution.py:20
  150.6 17.0 %collective-permute-start.24 = (bf16[64,3072]{1,0:T(8,128)(2,1)S(1)}, bf16[64,3072]{1,0:T(8,128)(2,1)S(1)}, u32[]{:S(2)}, u32[]{:S(2)}) collective-permute-start(bf16[64,3072]{1,0:T(8,128)(2,1)S(1)} %get-tuple-element.61), channel_id=1, source_target_pairs={{0,8},{4,12},{8,0},{12,4},{1,9},{5,13},{9,1},{13,5},{2,10},{6,14},... | collective-permute-start | bytes 1179656 | tf_op jit(solution)/shard_map/ppermute | solution.py:20
  151.0 28.4 %collective-permute-start.16 = (bf16[128,3072]{1,0:T(8,128)(2,1)S(1)}, bf16[128,3072]{1,0:T(8,128)(2,1)S(1)}, u32[]{:S(2)}, u32[]{:S(2)}) collective-permute-start(bf16[128,3072]{1,0:T(8,128)(2,1)S(1)} %add_convert_fusion), channel_id=1, source_target_pairs={{0,1},{1,0},{2,3},{3,2},{4,5},{5,4},{6,7},{7,6},{8,9},{9,8},{10,11... | collective-permute-start | bytes 2359304 | tf_op jit(solution)/shard_map/ppermute | solution.py:20
  167.7 10.1 %collective-permute-start.25 = (bf16[64,3072]{1,0:T(8,128)(2,1)S(1)}, bf16[64,3072]{1,0:T(8,128)(2,1)S(1)}, u32[]{:S(2)}, u32[]{:S(2)}) collective-permute-start(bf16[64,3072]{1,0:T(8,128)(2,1)S(1)} %add_convert_fusion.4), channel_id=1, source_target_pairs={{0,1},{1,0},{2,3},{3,2},{4,5},{5,4},{6,7},{7,6},{8,9},{9,8},{10,11... | collective-permute-start | bytes 1179656 | tf_op jit(solution)/shard_map/ppermute | solution.py:20
  177.8 17.5 %collective-permute-start.27 = (bf16[128,3072]{1,0:T(8,128)(2,1)S(1)}, bf16[128,3072]{1,0:T(8,128)(2,1)S(1)}, u32[]{:S(2)}, u32[]{:S(2)}) collective-permute-start(bf16[128,3072]{1,0:T(8,128)(2,1)S(1)} %slice.117), channel_id=1, source_target_pairs={{0,8},{4,12},{8,0},{12,4},{1,9},{5,13},{9,1},{13,5},{2,10},{6,14},... | collective-permute-start | bytes 2359304 | tf_op jit(solution)/shard_map/ppermute | solution.py:20
  179.8 18.5 %collective-permute-start.17 = (bf16[64,3072]{1,0:T(8,128)(2,1)S(1)}, bf16[64,3072]{1,0:T(8,128)(2,1)S(1)}, u32[]{:S(2)}, u32[]{:S(2)}) collective-permute-start(bf16[64,3072]{1,0:T(8,128)(2,1)S(1)} %slice.161), channel_id=1, source_target_pairs={{0,2},{1,3},{2,0},{3,1},{4,6},{5,7},{6,4},{7,5},{8,10},{9,11},{10,... | collective-permute-start | bytes 1179656 | tf_op jit(solution)/shard_map/ppermute | solution.py:20
  195.5 16.7 %collective-permute-start.28 = (bf16[64,3072]{1,0:T(8,128)(2,1)S(1)}, bf16[64,3072]{1,0:T(8,128)(2,1)S(1)}, u32[]{:S(2)}, u32[]{:S(2)}) collective-permute-start(bf16[64,3072]{1,0:T(8,128)(2,1)S(1)} %get-tuple-element.55), channel_id=1, source_target_pairs={{0,1},{1,0},{2,3},{3,2},{4,5},{5,4},{6,7},{7,6},{8,9},{9,8},{10,11... | collective-permute-start | bytes 1179656 | tf_op jit(solution)/shard_map/ppermute | solution.py:20
  196.5 18.3 %collective-permute-start.29 = (bf16[64,3072]{1,0:T(8,128)(2,1)S(1)}, bf16[64,3072]{1,0:T(8,128)(2,1)S(1)}, u32[]{:S(2)}, u32[]{:S(2)}) collective-permute-start(bf16[64,3072]{1,0:T(8,128)(2,1)S(1)} %get-tuple-element.56), channel_id=1, source_target_pairs={{0,2},{1,3},{2,0},{3,1},{4,6},{5,7},{6,4},{7,5},{8,10},{9,11},{10,... | collective-permute-start | bytes 1179656 | tf_op jit(solution)/shard_map/ppermute | solution.py:20
  198.4 18.2 %collective-permute-start.18 = (bf16[64,3072]{1,0:T(8,128)(2,1)S(1)}, bf16[64,3072]{1,0:T(8,128)(2,1)S(1)}, u32[]{:S(2)}, u32[]{:S(2)}) collective-permute-start(bf16[64,3072]{1,0:T(8,128)(2,1)S(1)} %fusion), channel_id=1, source_target_pairs={{16,0},{0,16},{17,1},{1,17},{18,2},{2,18},{19,3},{3,19},{20,4},{4,... | collective-permute-start | bytes 1179656 | tf_op jit(solution)/shard_map/ppermute | solution.py:16
  215.0 8.7 %collective-permute-start.30 = (bf16[64,3072]{1,0:T(8,128)(2,1)S(1)}, bf16[64,3072]{1,0:T(8,128)(2,1)S(1)}, u32[]{:S(2)}, u32[]{:S(2)}) collective-permute-start(bf16[64,3072]{1,0:T(8,128)(2,1)S(1)} %add_convert_fusion.1), channel_id=1, source_target_pairs={{16,0},{0,16},{17,1},{1,17},{18,2},{2,18},{19,3},{3,19},{20,4},{4,... | collective-permute-start | bytes 1179656 | tf_op jit(solution)/shard_map/ppermute | solution.py:16
  (10 other events, 45.3 us)

commit v5 on v3

--- a/solution.py
+++ b/solution.py
@@ -165,7 +165,7 @@
 def pack(m, pick, blocks, *earlier):
     _, rows, tokens = pick.shape
     half, features = rows // 2, blocks[0].shape[-1]
-    width = features // 4
+    width = features // 2
 
     def spec(block):
         if block.ndim == 3:
@@ -188,7 +188,7 @@
             bytes_accessed=2 * (rows + tokens) * features + 2 * rows * tokens,
             transcendentals=0,
         ),
-        compiler_params=pltpu.CompilerParams(vmem_limit_bytes=24 * 2**20),
+        compiler_params=pltpu.CompilerParams(vmem_limit_bytes=32 * 2**20),
     )(pick, *blocks, *earlier)
 
 
@@ -209,7 +209,7 @@
 def unpack(m, sides, mine, other, high, low, *earlier):
     _, tokens, rows = high.shape
     half, features = mine.shape
-    width, stays = features // 4, tokens // sides
+    width, stays = features // 2, tokens // sides
     out_shape = [jax.ShapeDtypeStruct((stays, features), F32)]
     out_shape += [jax.ShapeDtypeStruct((stays, features), BF16)] * (sides - 1)
     part = pl.BlockSpec((half, width), lambda i: (0, i))
@@ -226,7 +226,7 @@
             bytes_accessed=2 * (rows + 2 * tokens) * features + 4 * rows * tokens,
             transcendentals=0,
         ),
-        compiler_params=pltpu.CompilerParams(vmem_limit_bytes=24 * 2**20),
+        compiler_params=pltpu.CompilerParams(vmem_limit_bytes=32 * 2**20),
     )(mine, other, high, low, *earlier)
 
 

time: 224 us -> 223 us (level)
  no operation moved by 1% of the time
where the time goes in v5:
time: 223 us; the launch traced here: 222 us
  waiting for transfers between devices  123 us (55%)
  Pallas kernels  57.1 us (26%)
  starting transfers between devices  32.5 us (15%)
  other arithmetic  5.39 us (2%)
  local copies, waits for them, and re-layouts  3.71 us (2%)
    ppermute x29, waiting for transfers between devices, swapped(): lax.ppermute(block, axis, [(i, i ^ bits) for i in range(lax.axis_size(axi...  116 us
    pallas_call x2, Pallas kernels, expert_share(): pl.pallas_call(functools.partial(expert_kernel, steps, half), grid=(2 * s...  37.6 us
    ppermute x29, starting transfers between devices, swapped(): lax.ppermute(block, axis, [(i, i ^ bits) for i in range(lax.axis_size(axi...  29.3 us
    pallas_call x2, Pallas kernels, unpack(): pl.pallas_call(functools.partial(unpack_kernel, stays, len(earlier)), gri...  11.5 us
    ppermute x2, waiting for transfers between devices, passed_along(): return lax.ppermute(block, axis, route)  7.11 us
    pallas_call x2, Pallas kernels, pack(): pl.pallas_call(functools.partial(pack_kernel, len(blocks), half), grid=(f...  6.03 us
  transfers between devices with their start and end apart: 31, of which 19 were waited for; matrix products, arithmetic and copies ran while one was open for 3% of the time, Pallas kernels for 24%

profile of v5, /device:TPU:0, one launch (start us, length us, event | category | flops | bytes accessed | tf_op | source)
XLA Modules:
  0.0 222.3 jit_solution(5603889213529907487)
XLA Ops:
  2.5 4.1 %collective-permute-start.1 = (f32[8,64]{1,0:T(8,128)S(1)}, f32[8,64]{1,0:T(8,128)S(1)}, u32[]{:S(2)}, u32[]{:S(2)}) collective-permute-start(f32[8,64]{1,0:T(8,128)S(1)} %get-tuple-element.69), channel_id=1, source_target_pairs={{0,2},{1,3},{2,0},{3,1},{4,6},{5,7},{6,4},{7,5},{8,10},{9,11},{10,... | collective-permute-start | bytes 6152 | tf_op jit(solution)/shard_map/ppermute | solution.py:20
  8.2 2.0 collective-permute-done
  10.2 3.4 %collective-permute-done.2 = f32[8,64]{1,0:T(8,128)S(1)} collective-permute-done((f32[8,64]{1,0:T(8,128)S(1)}, f32[8,64]{1,0:T(8,128)S(1)}, u32[]{:S(2)}, u32[]{:S(2)}) %collective-permute-start.2) | collective-permute-done | bytes 2080 | tf_op jit(solution)/shard_map/ppermute | solution.py:20
  15.4 1.7 collective-permute-start.3
  17.4 1.9 collective-permute-done.3
  19.4 18.2 %collective-permute-done.6 = bf16[64,3072]{1,0:T(8,128)(2,1)} collective-permute-done((bf16[64,3072]{1,0:T(8,128)(2,1)S(1)}, bf16[64,3072]{1,0:T(8,128)(2,1)}, u32[]{:S(2)}, u32[]{:S(2)}) %collective-permute-start.6) | collective-permute-done | bytes 393248 | tf_op jit(solution)/shard_map/ppermute | solution.py:20
  37.6 3.6 %collective-permute-start.10 = (bf16[64,3072]{1,0:T(8,128)(2,1)S(1)}, bf16[64,3072]{1,0:T(8,128)(2,1)}, u32[]{:S(2)}, u32[]{:S(2)}) collective-permute-start(bf16[64,3072]{1,0:T(8,128)(2,1)S(1)} %get-tuple-element.31), channel_id=1, source_target_pairs={{0,2},{1,3},{2,0},{3,1},{4,6},{5,7},{6,4},{7,5},{8,10},{9,11},{10,... | collective-permute-start | bytes 1179656 | tf_op jit(solution)/shard_map/ppermute | solution.py:20
  44.6 11.9 %collective-permute-done.10 = bf16[64,3072]{1,0:T(8,128)(2,1)} collective-permute-done((bf16[64,3072]{1,0:T(8,128)(2,1)S(1)}, bf16[64,3072]{1,0:T(8,128)(2,1)}, u32[]{:S(2)}, u32[]{:S(2)}) %collective-permute-start.10) | collective-permute-done | bytes 393248 | tf_op jit(solution)/shard_map/ppermute | solution.py:20
  57.5 1.7 collective-permute-start.9
  59.3 2.0 shard_map.64
  61.3 6.0 %collective-permute-done.11 = bf16[64,3072]{1,0:T(8,128)(2,1)} collective-permute-done((bf16[64,3072]{1,0:T(8,128)(2,1)}, bf16[64,3072]{1,0:T(8,128)(2,1)}, u32[]{:S(2)}, u32[]{:S(2)}) %collective-permute-start.11) | collective-permute-done | bytes 393248 | tf_op jit(solution)/shard_map/ppermute | solution.py:20
  68.6 3.5 %shard_map.65 = (bf16[272,3072]{1,0:T(8,128)(2,1)S(1)}, bf16[272,3072]{1,0:T(8,128)(2,1)S(1)}) custom-call(bf16[2,544,512]{2,1,0:T(8,128)(2,1)S(1)} %get-tuple-element.27.pick_ref, bf16[2,64,3072]{2,1,0:T(8,128)(2,1)S(1)} %copy-done, bf16[2,64,3072]{2,1,0:T(8,128)(2,1)S(1)} %collective-permute-done.4.refs_1_, ...), custom_call_target="tpu_custom_call" | custom-call | flops 1711276032 | bytes 7045120 | tf_op jit(solution)/shard_map/pallas_call | solution.py:175
  72.2 1.8 collective-permute-start.13
  74.0 1.7 collective-permute-done.12.other_ref
  75.7 18.8 %shard_map.66 = (bf16[272,3072]{1,0:T(8,128)(2,1)S(1)}, bf16[272,3072]{1,0:T(8,128)(2,1)S(1)}) custom-call(bf16[272,3072]{1,0:T(8,128)(2,1)S(1)} %get-tuple-element.32.mine_ref, bf16[272,3072]{1,0:T(8,128)(2,1)S(1)} %collective-permute-done.12.other_ref, bf16[2048,3072]{1,0:T(8,128)(2,1)} %bitcast.62, bf16[2048,3072]{1,0:T(8,128)(2,1)} %bitcast.64), custom_call_target="tpu_custom_call" | custom-call | flops 13690208256 | bytes 31850496 | tf_op jit(solution)/shard_map/pallas_call | solution.py:131
  94.5 6.0 %collective-permute-done.13.refs_3_ = bf16[192,3072]{1,0:T(8,128)(2,1)S(1)} collective-permute-done((bf16[192,3072]{1,0:T(8,128)(2,1)S(1)}, bf16[192,3072]{1,0:T(8,128)(2,1)S(1)}, u32[]{:S(2)}, u32[]{:S(2)}) %collective-permute-start.13) | collective-permute-done | bytes 1179680 | tf_op jit(solution)/shard_map/ppermute | solution.py:20
  100.6 2.5 %shard_map.68 = (bf16[272,3072]{1,0:T(8,128)(2,1)S(1)}, bf16[272,3072]{1,0:T(8,128)(2,1)S(1)}) custom-call(bf16[2,544,512]{2,1,0:T(8,128)(2,1)S(1)} %get-tuple-element.27.pick_ref, bf16[2,64,3072]{2,1,0:T(8,128)(2,1)S(1)} %copy-done, bf16[2,64,3072]{2,1,0:T(8,128)(2,1)S(1)} %collective-permute-done.4.refs_1_, ...), custom_call_target="tpu_custom_call" | custom-call | flops 1711276032 | bytes 7045120 | tf_op jit(solution)/shard_map/pallas_call | solution.py:175
  104.1 5.8 %shard_map.67 = (f32[256,3072]{1,0:T(8,128)S(1)}, bf16[256,3072]{1,0:T(8,128)(2,1)S(1)}) custom-call(bf16[272,3072]{1,0:T(8,128)(2,1)S(1)} %get-tuple-element.34.mine_ref.refs_4_, bf16[272,3072]{1,0:T(8,128)(2,1)S(1)} %collective-permute-done.14.other_ref, bf16[2,512,544]{2,1,0:T(8,128)(2,1)S(1)} %get-tuple-element.37.high_ref, ...), custom_call_target="tpu_custom_call" | custom-call | flops 3422552064 | bytes 10747904 | tf_op jit(solution)/shard_map/pallas_call | solution.py:217
  109.9 1.8 collective-permute-start.15
  111.7 18.8 %shard_map.69 = (bf16[272,3072]{1,0:T(8,128)(2,1)S(1)}, bf16[272,3072]{1,0:T(8,128)(2,1)S(1)}) custom-call(bf16[272,3072]{1,0:T(8,128)(2,1)S(1)} %get-tuple-element.41.mine_ref, bf16[272,3072]{1,0:T(8,128)(2,1)S(1)} %collective-permute-done.19.other_ref, bf16[2048,3072]{1,0:T(8,128)(2,1)} %bitcast.63, bf16[2048,3072]{1,0:T(8,128)(2,1)} %bitcast.65, ...), custom_call_target="tpu_custom_call" | custom-call | flops 13690208256 | bytes 31850496 | tf_op jit(solution)/shard_map/pallas_call | solution.py:131
  131.8 2.4 %collective-permute-done.23 = bf16[32,3072]{1,0:T(8,128)(2,1)S(1)} collective-permute-done((bf16[32,3072]{1,0:T(8,128)(2,1)S(1)}, bf16[32,3072]{1,0:T(8,128)(2,1)S(1)}, u32[]{:S(2)}, u32[]{:S(2)}) %collective-permute-start.23) | collective-permute-done | bytes 196640 | tf_op jit(solution)/shard_map/ppermute | solution.py:20
  134.4 5.8 %shard_map.70 = (f32[256,3072]{1,0:T(8,128)S(1)}, bf16[256,3072]{1,0:T(8,128)(2,1)S(1)}) custom-call(bf16[272,3072]{1,0:T(8,128)(2,1)S(1)} %get-tuple-element.43.mine_ref, bf16[272,3072]{1,0:T(8,128)(2,1)S(1)} %pad_maximum_fusion.other_ref, bf16[2,512,544]{2,1,0:T(8,128)(2,1)S(1)} %get-tuple-element.37.high_ref, ...), custom_call_target="tpu_custom_call" | custom-call | flops 3422552064 | bytes 10747904 | tf_op jit(solution)/shard_map/pallas_call | solution.py:217
  140.1 6.3 %collective-permute-done.15 = bf16[256,3072]{1,0:T(8,128)(2,1)S(1)} collective-permute-done((bf16[256,3072]{1,0:T(8,128)(2,1)S(1)}, bf16[256,3072]{1,0:T(8,128)(2,1)S(1)}, u32[]{:S(2)}, u32[]{:S(2)}) %collective-permute-start.15) | collective-permute-done | bytes 1572896 | tf_op jit(solution)/shard_map/ppermute | solution.py:20
  146.5 1.8 collective-permute-start.26
  149.8 15.5 %collective-permute-done.24 = bf16[64,3072]{1,0:T(8,128)(2,1)S(1)} collective-permute-done((bf16[64,3072]{1,0:T(8,128)(2,1)S(1)}, bf16[64,3072]{1,0:T(8,128)(2,1)S(1)}, u32[]{:S(2)}, u32[]{:S(2)}) %collective-permute-start.24) | collective-permute-done | bytes 393248 | tf_op jit(solution)/shard_map/ppermute | solution.py:20
  166.5 9.0 %collective-permute-done.25 = bf16[64,3072]{1,0:T(8,128)(2,1)S(1)} collective-permute-done((bf16[64,3072]{1,0:T(8,128)(2,1)S(1)}, bf16[64,3072]{1,0:T(8,128)(2,1)S(1)}, u32[]{:S(2)}, u32[]{:S(2)}) %collective-permute-start.25) | collective-permute-done | bytes 393248 | tf_op jit(solution)/shard_map/ppermute | solution.py:20
  175.5 1.7 collective-permute-start.27
  178.0 15.0 %collective-permute-done.27 = bf16[128,3072]{1,0:T(8,128)(2,1)S(1)} collective-permute-done((bf16[128,3072]{1,0:T(8,128)(2,1)S(1)}, bf16[128,3072]{1,0:T(8,128)(2,1)S(1)}, u32[]{:S(2)}, u32[]{:S(2)}) %collective-permute-start.27) | collective-permute-done | bytes 786464 | tf_op jit(solution)/shard_map/ppermute | solution.py:20
  197.6 12.3 %collective-permute-done.28 = bf16[64,3072]{1,0:T(8,128)(2,1)S(1)} collective-permute-done((bf16[64,3072]{1,0:T(8,128)(2,1)S(1)}, bf16[64,3072]{1,0:T(8,128)(2,1)S(1)}, u32[]{:S(2)}, u32[]{:S(2)}) %collective-permute-start.28) | collective-permute-done | bytes 393248 | tf_op jit(solution)/shard_map/ppermute | solution.py:20
  209.9 2.6 %collective-permute-done.29 = bf16[64,3072]{1,0:T(8,128)(2,1)S(1)} collective-permute-done((bf16[64,3072]{1,0:T(8,128)(2,1)S(1)}, bf16[64,3072]{1,0:T(8,128)(2,1)S(1)}, u32[]{:S(2)}, u32[]{:S(2)}) %collective-permute-start.29) | collective-permute-done | bytes 393248 | tf_op jit(solution)/shard_map/ppermute | solution.py:20
  212.7 1.6 collective-permute-start.30
  214.3 7.1 %collective-permute-done.30 = bf16[64,3072]{1,0:T(8,128)(2,1)S(1)} collective-permute-done((bf16[64,3072]{1,0:T(8,128)(2,1)S(1)}, bf16[64,3072]{1,0:T(8,128)(2,1)S(1)}, u32[]{:S(2)}, u32[]{:S(2)}) %collective-permute-start.30) | collective-permute-done | bytes 393248 | tf_op jit(solution)/shard_map/ppermute | solution.py:16
  (68 shorter events, 23.9 us)
Async XLA Ops:
  0.0 17.1 %copy-start = (bf16[2,64,3072]{2,1,0:T(8,128)(2,1)S(1)}, bf16[2,64,3072]{2,1,0:T(8,128)(2,1)}, u32[]{:S(2)}) copy-start(bf16[2,64,3072]{2,1,0:T(8,128)(2,1)} %refs_0_.3) | copy-start | bytes 2359300
  2.5 5.7 %collective-permute-start.1 = (f32[8,64]{1,0:T(8,128)S(1)}, f32[8,64]{1,0:T(8,128)S(1)}, u32[]{:S(2)}, u32[]{:S(2)}) collective-permute-start(f32[8,64]{1,0:T(8,128)S(1)} %get-tuple-element.69), channel_id=1, source_target_pairs={{0,2},{1,3},{2,0},{3,1},{4,6},{5,7},{6,4},{7,5},{8,10},{9,11},{10,... | collective-permute-start | bytes 6152 | tf_op jit(solution)/shard_map/ppermute | solution.py:20
  6.6 3.6 %collective-permute-start = (f32[8,64]{1,0:T(8,128)S(1)}, f32[8,64]{1,0:T(8,128)S(1)}, u32[]{:S(2)}, u32[]{:S(2)}) collective-permute-start(f32[8,64]{1,0:T(8,128)S(1)} %get-tuple-element.69), channel_id=1, source_target_pairs={{0,1},{1,0},{2,3},{3,2},{4,5},{5,4},{6,7},{7,6},{8,9},{9,8},{10,11... | collective-permute-start | bytes 6152 | tf_op jit(solution)/shard_map/ppermute | solution.py:20
  8.2 5.4 %collective-permute-start.2 = (f32[8,64]{1,0:T(8,128)S(1)}, f32[8,64]{1,0:T(8,128)S(1)}, u32[]{:S(2)}, u32[]{:S(2)}) collective-permute-start(f32[8,64]{1,0:T(8,128)S(1)} %get-tuple-element.69), channel_id=1, source_target_pairs={{0,3},{1,2},{2,1},{3,0},{4,7},{5,6},{6,5},{7,4},{8,11},{9,10},{10,... | collective-permute-start | bytes 6152 | tf_op jit(solution)/shard_map/ppermute | solution.py:20
  13.6 27.6 %collective-permute-start.5 = (bf16[2,64,3072]{2,1,0:T(8,128)(2,1)}, bf16[2,64,3072]{2,1,0:T(8,128)(2,1)S(1)}, u32[]{:S(2)}, u32[]{:S(2)}) collective-permute-start(bf16[2,64,3072]{2,1,0:T(8,128)(2,1)} %refs_0_.3), channel_id=1, source_target_pairs={{0,1},{1,0},{2,3},{3,2},{4,5},{5,4},{6,7},{7,6},{8,9},{9,8},{10,11... | collective-permute-start | bytes 2359304 | tf_op jit(solution)/shard_map/ppermute | solution.py:20
  14.8 22.8 %collective-permute-start.6 = (bf16[64,3072]{1,0:T(8,128)(2,1)S(1)}, bf16[64,3072]{1,0:T(8,128)(2,1)}, u32[]{:S(2)}, u32[]{:S(2)}) collective-permute-start(bf16[64,3072]{1,0:T(8,128)(2,1)S(1)} %get-tuple-element.29), channel_id=1, source_target_pairs={{0,2},{1,3},{2,0},{3,1},{4,6},{5,7},{6,4},{7,5},{8,10},{9,11},{10,... | collective-permute-start | bytes 1179656 | tf_op jit(solution)/shard_map/ppermute | solution.py:20
  15.4 4.0 %collective-permute-start.3 = (f32[4,8,64]{2,1,0:T(8,128)S(1)}, f32[4,8,64]{2,1,0:T(8,128)S(1)}, u32[]{:S(2)}, u32[]{:S(2)}) collective-permute-start(f32[4,8,64]{2,1,0:T(8,128)S(1)} %get-tuple-element.67), channel_id=1, source_target_pairs={{0,8},{4,12},{8,0},{12,4},{1,9},{5,13},{9,1},{13,5},{2,10},{6,14},... | collective-permute-start | bytes 24584 | tf_op jit(solution)/shard_map/ppermute | solution.py:20
  17.1 51.5 %collective-permute-start.4 = (bf16[2,64,3072]{2,1,0:T(8,128)(2,1)S(1)}, bf16[2,64,3072]{2,1,0:T(8,128)(2,1)S(1)}, u32[]{:S(2)}, u32[]{:S(2)}) collective-permute-start(bf16[2,64,3072]{2,1,0:T(8,128)(2,1)S(1)} %copy-done), channel_id=1, source_target_pairs={{0,8},{4,12},{8,0},{12,4},{1,9},{5,13},{9,1},{13,5},{2,10},{6,14},... | collective-permute-start | bytes 2359304 | tf_op jit(solution)/shard_map/ppermute | solution.py:20
  37.6 18.9 %collective-permute-start.10 = (bf16[64,3072]{1,0:T(8,128)(2,1)S(1)}, bf16[64,3072]{1,0:T(8,128)(2,1)}, u32[]{:S(2)}, u32[]{:S(2)}) collective-permute-start(bf16[64,3072]{1,0:T(8,128)(2,1)S(1)} %get-tuple-element.31), channel_id=1, source_target_pairs={{0,2},{1,3},{2,0},{3,1},{4,6},{5,7},{6,4},{7,5},{8,10},{9,11},{10,... | collective-permute-start | bytes 1179656 | tf_op jit(solution)/shard_map/ppermute | solution.py:20
  41.2 16.3 %collective-permute-start.8 = (bf16[64,3072]{1,0:T(8,128)(2,1)}, bf16[64,3072]{1,0:T(8,128)(2,1)}, u32[]{:S(2)}, u32[]{:S(2)}) collective-permute-start(bf16[64,3072]{1,0:T(8,128)(2,1)} %collective-permute-done.6), channel_id=1, source_target_pairs={{0,1},{1,0},{2,3},{3,2},{4,5},{5,4},{6,7},{7,6},{8,9},{9,8},{10,11... | collective-permute-start | bytes 1179656 | tf_op jit(solution)/shard_map/ppermute | solution.py:20
  43.0 25.6 %collective-permute-start.7 = (bf16[128,3072]{1,0:T(8,128)(2,1)S(1)}, bf16[128,3072]{1,0:T(8,128)(2,1)S(1)}, u32[]{:S(2)}, u32[]{:S(2)}) collective-permute-start(bf16[128,3072]{1,0:T(8,128)(2,1)S(1)} %pad_maximum_fusion.2.refs_2_), channel_id=1, source_target_pairs={{0,8},{4,12},{8,0},{12,4},{1,9},{5,13},{9,1},{13,5},{2,10},{6,14},... | collective-permute-start | bytes 2359304 | tf_op jit(solution)/shard_map/ppermute | solution.py:20
  56.5 10.8 %collective-permute-start.11 = (bf16[64,3072]{1,0:T(8,128)(2,1)}, bf16[64,3072]{1,0:T(8,128)(2,1)}, u32[]{:S(2)}, u32[]{:S(2)}) collective-permute-start(bf16[64,3072]{1,0:T(8,128)(2,1)} %collective-permute-done.10), channel_id=1, source_target_pairs={{0,1},{1,0},{2,3},{3,2},{4,5},{5,4},{6,7},{7,6},{8,9},{9,8},{10,11... | collective-permute-start | bytes 1179656 | tf_op jit(solution)/shard_map/ppermute | solution.py:20
  57.5 11.1 %collective-permute-start.9 = (bf16[64,3072]{1,0:T(8,128)(2,1)}, bf16[64,3072]{1,0:T(8,128)(2,1)S(1)}, u32[]{:S(2)}, u32[]{:S(2)}) collective-permute-start(bf16[64,3072]{1,0:T(8,128)(2,1)} %collective-permute-done.8.refs_4_), channel_id=1, source_target_pairs={{0,8},{4,12},{8,0},{12,4},{1,9},{5,13},{9,1},{13,5},{2,10},{6,14},... | collective-permute-start | bytes 1179656 | tf_op jit(solution)/shard_map/ppermute | solution.py:20
  72.1 3.6 %collective-permute-start.12 = (bf16[272,3072]{1,0:T(8,128)(2,1)S(1)}, bf16[272,3072]{1,0:T(8,128)(2,1)S(1)}, u32[]{:S(2)}, u32[]{:S(2)}) collective-permute-start(bf16[272,3072]{1,0:T(8,128)(2,1)S(1)} %get-tuple-element.33), channel_id=1, source_target_pairs={{0,4},{4,0},{8,12},{12,8},{1,5},{5,1},{9,13},{13,9},{2,6},{6,2},{1... | collective-permute-start | bytes 5013512 | tf_op jit(solution)/shard_map/ppermute | solution.py:20
  72.2 28.4 %collective-permute-start.13 = (bf16[192,3072]{1,0:T(8,128)(2,1)S(1)}, bf16[192,3072]{1,0:T(8,128)(2,1)S(1)}, u32[]{:S(2)}, u32[]{:S(2)}) collective-permute-start(bf16[192,3072]{1,0:T(8,128)(2,1)S(1)} %pad_maximum_fusion.1.refs_6_.refs_2_), channel_id=1, source_target_pairs={{0,8},{4,12},{8,0},{12,4},{1,9},{5,13},{9,1},{13,5},{2,10},{6,14},... | collective-permute-start | bytes 3538952 | tf_op jit(solution)/shard_map/ppermute | solution.py:20
  100.6 3.6 %collective-permute-start.14 = (bf16[272,3072]{1,0:T(8,128)(2,1)S(1)}, bf16[272,3072]{1,0:T(8,128)(2,1)S(1)}, u32[]{:S(2)}, u32[]{:S(2)}) collective-permute-start(bf16[272,3072]{1,0:T(8,128)(2,1)S(1)} %get-tuple-element.36), channel_id=1, source_target_pairs={{0,4},{4,0},{8,12},{12,8},{1,5},{5,1},{9,13},{13,9},{2,6},{6,2},{1... | collective-permute-start | bytes 5013512 | tf_op jit(solution)/shard_map/ppermute | solution.py:20
  103.1 8.6 %collective-permute-start.19 = (bf16[272,3072]{1,0:T(8,128)(2,1)S(1)}, bf16[272,3072]{1,0:T(8,128)(2,1)S(1)}, u32[]{:S(2)}, u32[]{:S(2)}) collective-permute-start(bf16[272,3072]{1,0:T(8,128)(2,1)S(1)} %get-tuple-element.42), channel_id=1, source_target_pairs={{0,4},{4,0},{8,12},{12,8},{1,5},{5,1},{9,13},{13,9},{2,6},{6,2},{1... | collective-permute-start | bytes 5013512 | tf_op jit(solution)/shard_map/ppermute | solution.py:20
  109.9 36.5 %collective-permute-start.15 = (bf16[256,3072]{1,0:T(8,128)(2,1)S(1)}, bf16[256,3072]{1,0:T(8,128)(2,1)S(1)}, u32[]{:S(2)}, u32[]{:S(2)}) collective-permute-start(bf16[256,3072]{1,0:T(8,128)(2,1)S(1)} %get-tuple-element.40.refs_0_), channel_id=1, source_target_pairs={{0,8},{4,12},{8,0},{12,4},{1,9},{5,13},{9,1},{13,5},{2,10},{6,14},... | collective-permute-start | bytes 4718600 | tf_op jit(solution)/shard_map/ppermute | solution.py:20
  130.6 3.6 %collective-permute-start.20 = (bf16[80,3072]{1,0:T(8,128)(2,1)S(1)}, bf16[80,3072]{1,0:T(8,128)(2,1)S(1)}, u32[]{:S(2)}, u32[]{:S(2)}) collective-permute-start(bf16[80,3072]{1,0:T(8,128)(2,1)S(1)} %get-tuple-element.57), channel_id=1, source_target_pairs={{0,4},{4,0},{8,12},{12,8},{1,5},{5,1},{9,13},{13,9},{2,6},{6,2},{1... | collective-permute-start | bytes 1474568 | tf_op jit(solution)/shard_map/ppermute | solution.py:20
  130.7 3.5 %collective-permute-start.22 = (bf16[80,3072]{1,0:T(8,128)(2,1)S(1)}, bf16[80,3072]{1,0:T(8,128)(2,1)S(1)}, u32[]{:S(2)}, u32[]{:S(2)}) collective-permute-start(bf16[80,3072]{1,0:T(8,128)(2,1)S(1)} %get-tuple-element.58), channel_id=1, source_target_pairs={{0,4},{4,0},{8,12},{12,8},{1,5},{5,1},{9,13},{13,9},{2,6},{6,2},{1... | collective-permute-start | bytes 1474568 | tf_op jit(solution)/shard_map/ppermute | solution.py:20
  131.2 3.0 %collective-permute-start.21 = (bf16[80,3072]{1,0:T(8,128)(2,1)S(1)}, bf16[80,3072]{1,0:T(8,128)(2,1)S(1)}, u32[]{:S(2)}, u32[]{:S(2)}) collective-permute-start(bf16[80,3072]{1,0:T(8,128)(2,1)S(1)} %get-tuple-element.59), channel_id=1, source_target_pairs={{0,4},{4,0},{8,12},{12,8},{1,5},{5,1},{9,13},{13,9},{2,6},{6,2},{1... | collective-permute-start | bytes 1474568 | tf_op jit(solution)/shard_map/ppermute | solution.py:20
  131.3 2.9 %collective-permute-start.23 = (bf16[32,3072]{1,0:T(8,128)(2,1)S(1)}, bf16[32,3072]{1,0:T(8,128)(2,1)S(1)}, u32[]{:S(2)}, u32[]{:S(2)}) collective-permute-start(bf16[32,3072]{1,0:T(8,128)(2,1)S(1)} %slice.115), channel_id=1, source_target_pairs={{0,4},{4,0},{8,12},{12,8},{1,5},{5,1},{9,13},{13,9},{2,6},{6,2},{1... | collective-permute-start | bytes 589832 | tf_op jit(solution)/shard_map/ppermute | solution.py:20
  146.5 20.0 %collective-permute-start.26 = (bf16[64,3072]{1,0:T(8,128)(2,1)S(1)}, bf16[64,3072]{1,0:T(8,128)(2,1)S(1)}, u32[]{:S(2)}, u32[]{:S(2)}) collective-permute-start(bf16[64,3072]{1,0:T(8,128)(2,1)S(1)} %get-tuple-element.60), channel_id=1, source_target_pairs={{0,8},{4,12},{8,0},{12,4},{1,9},{5,13},{9,1},{13,5},{2,10},{6,14},... | collective-permute-start | bytes 1179656 | tf_op jit(solution)/shard_map/ppermute | solution.py:20
  148.3 17.0 %collective-permute-start.24 = (bf16[64,3072]{1,0:T(8,128)(2,1)S(1)}, bf16[64,3072]{1,0:T(8,128)(2,1)S(1)}, u32[]{:S(2)}, u32[]{:S(2)}) collective-permute-start(bf16[64,3072]{1,0:T(8,128)(2,1)S(1)} %get-tuple-element.61), channel_id=1, source_target_pairs={{0,8},{4,12},{8,0},{12,4},{1,9},{5,13},{9,1},{13,5},{2,10},{6,14},... | collective-permute-start | bytes 1179656 | tf_op jit(solution)/shard_map/ppermute | solution.py:20
  148.7 28.4 %collective-permute-start.16 = (bf16[128,3072]{1,0:T(8,128)(2,1)S(1)}, bf16[128,3072]{1,0:T(8,128)(2,1)S(1)}, u32[]{:S(2)}, u32[]{:S(2)}) collective-permute-start(bf16[128,3072]{1,0:T(8,128)(2,1)S(1)} %add_convert_fusion), channel_id=1, source_target_pairs={{0,1},{1,0},{2,3},{3,2},{4,5},{5,4},{6,7},{7,6},{8,9},{9,8},{10,11... | collective-permute-start | bytes 2359304 | tf_op jit(solution)/shard_map/ppermute | solution.py:20
  165.3 10.1 %collective-permute-start.25 = (bf16[64,3072]{1,0:T(8,128)(2,1)S(1)}, bf16[64,3072]{1,0:T(8,128)(2,1)S(1)}, u32[]{:S(2)}, u32[]{:S(2)}) collective-permute-start(bf16[64,3072]{1,0:T(8,128)(2,1)S(1)} %add_convert_fusion.4), channel_id=1, source_target_pairs={{0,1},{1,0},{2,3},{3,2},{4,5},{5,4},{6,7},{7,6},{8,9},{9,8},{10,11... | collective-permute-start | bytes 1179656 | tf_op jit(solution)/shard_map/ppermute | solution.py:20
  175.5 17.5 %collective-permute-start.27 = (bf16[128,3072]{1,0:T(8,128)(2,1)S(1)}, bf16[128,3072]{1,0:T(8,128)(2,1)S(1)}, u32[]{:S(2)}, u32[]{:S(2)}) collective-permute-start(bf16[128,3072]{1,0:T(8,128)(2,1)S(1)} %slice.117), channel_id=1, source_target_pairs={{0,8},{4,12},{8,0},{12,4},{1,9},{5,13},{9,1},{13,5},{2,10},{6,14},... | collective-permute-start | bytes 2359304 | tf_op jit(solution)/shard_map/ppermute | solution.py:20
  177.4 18.6 %collective-permute-start.17 = (bf16[64,3072]{1,0:T(8,128)(2,1)S(1)}, bf16[64,3072]{1,0:T(8,128)(2,1)S(1)}, u32[]{:S(2)}, u32[]{:S(2)}) collective-permute-start(bf16[64,3072]{1,0:T(8,128)(2,1)S(1)} %slice.161), channel_id=1, source_target_pairs={{0,2},{1,3},{2,0},{3,1},{4,6},{5,7},{6,4},{7,5},{8,10},{9,11},{10,... | collective-permute-start | bytes 1179656 | tf_op jit(solution)/shard_map/ppermute | solution.py:20
  193.2 16.7 %collective-permute-start.28 = (bf16[64,3072]{1,0:T(8,128)(2,1)S(1)}, bf16[64,3072]{1,0:T(8,128)(2,1)S(1)}, u32[]{:S(2)}, u32[]{:S(2)}) collective-permute-start(bf16[64,3072]{1,0:T(8,128)(2,1)S(1)} %get-tuple-element.55), channel_id=1, source_target_pairs={{0,1},{1,0},{2,3},{3,2},{4,5},{5,4},{6,7},{7,6},{8,9},{9,8},{10,11... | collective-permute-start | bytes 1179656 | tf_op jit(solution)/shard_map/ppermute | solution.py:20
  194.1 18.3 %collective-permute-start.29 = (bf16[64,3072]{1,0:T(8,128)(2,1)S(1)}, bf16[64,3072]{1,0:T(8,128)(2,1)S(1)}, u32[]{:S(2)}, u32[]{:S(2)}) collective-permute-start(bf16[64,3072]{1,0:T(8,128)(2,1)S(1)} %get-tuple-element.56), channel_id=1, source_target_pairs={{0,2},{1,3},{2,0},{3,1},{4,6},{5,7},{6,4},{7,5},{8,10},{9,11},{10,... | collective-permute-start | bytes 1179656 | tf_op jit(solution)/shard_map/ppermute | solution.py:20
  196.1 18.2 %collective-permute-start.18 = (bf16[64,3072]{1,0:T(8,128)(2,1)S(1)}, bf16[64,3072]{1,0:T(8,128)(2,1)S(1)}, u32[]{:S(2)}, u32[]{:S(2)}) collective-permute-start(bf16[64,3072]{1,0:T(8,128)(2,1)S(1)} %fusion), channel_id=1, source_target_pairs={{16,0},{0,16},{17,1},{1,17},{18,2},{2,18},{19,3},{3,19},{20,4},{4,... | collective-permute-start | bytes 1179656 | tf_op jit(solution)/shard_map/ppermute | solution.py:16
  212.7 8.7 %collective-permute-start.30 = (bf16[64,3072]{1,0:T(8,128)(2,1)S(1)}, bf16[64,3072]{1,0:T(8,128)(2,1)S(1)}, u32[]{:S(2)}, u32[]{:S(2)}) collective-permute-start(bf16[64,3072]{1,0:T(8,128)(2,1)S(1)} %add_convert_fusion.1), channel_id=1, source_target_pairs={{16,0},{0,16},{17,1},{1,17},{18,2},{2,18},{19,3},{3,19},{20,4},{4,... | collective-permute-start | bytes 1179656 | tf_op jit(solution)/shard_map/ppermute | solution.py:16
